TPU v7x, 512 devices: a whole 4x8x8 slice. The times are simulated.
512 devices in a mesh: head: 16 (over x_hi, z), seq: 32 (over x_lo, y, core).
Axes of the slice: x: 4 (x_hi: 2, x_lo: 2; x = x_hi * 2 + x_lo), y: 8, z: 8, core: 2. Of those that a mesh axis runs over, the one named last changes fastest.
Arguments:
- context: bfloat16 [1536, 14336], P('head', 'seq'), may hold values from -6 to 6
- stream: bfloat16 [1536, 14336], P('head', 'seq'), may hold values from -16 to 16
- out_weight: bfloat16 [1536, 1536], P('head'), may hold values from -0.21875 to 0.21875
- ln_gain: float32 [1536], replicated, may hold values from 0.1 to 1.9
- ln_bias: float32 [1536], replicated, may hold values from -3 to 3
- glu_weight: bfloat16 [2, 1536, 1536], P(None, 'head'), may hold values from -0.15625 to 0.15625
- depth_kernel: float32 [1536, 31], P('head'), may hold values from -1 to 1
- bn_gain: float32 [1536], P('head'), may hold values from 0.1 to 1.9
- bn_bias: float32 [1536], P('head'), may hold values from -3 to 3
- proj_weight: bfloat16 [1536, 1536], P('head'), may hold values from -0.21875 to 0.21875
- out_grad: bfloat16 [1536, 14336], P('head', 'seq'), may hold values from -6 to 6
Outputs:
- output: bfloat16 [1536, 14336], P('head', 'seq')
- stream_grad: bfloat16 [1536, 14336], P('head', 'seq')
- context_grad: bfloat16 [1536, 14336], P('head', 'seq')
- out_weight_grad: float32 [1536, 1536], P('head')
- glu_weight_grad: float32 [2, 1536, 1536], P(None, 'head')
- kernel_grad: float32 [1536, 31], P('head')
- bn_gain_grad: float32 [1536], P('head')
- bn_bias_grad: float32 [1536], P('head')
- proj_weight_grad: float32 [1536, 1536], P('head')
All inputs are finite; a program needn't handle non-finite values.
Results may differ from a plain program's by a relative error of at most 0.03.
Values may be sent and summed in bfloat16 or wider, within the bound.
No kernel may reach another device: no remote copies, remote signals or barrier semaphores. Data moves between devices by JAX's collectives and lax.ppermute only.
A program may use at most 64 MiB of HBM per device.

v0:
```python
import jax
import jax.numpy as jnp
from jax import lax
from jax.sharding import PartitionSpec as P

epsilon = 1e-05


def padded(array, sides, width):
    for axis, dim in sides:
        count, length = (lax.axis_size(axis), array.shape[dim])
        up = [(i, (i + 1) % count) for i in range(count - 1)]
        down = [(j, i) for i, j in up]
        last = lax.slice_in_dim(array, length - width, length, axis=dim)
        first = lax.slice_in_dim(array, 0, width, axis=dim)
        before = lax.ppermute(last, axis, up)
        after = lax.ppermute(first, axis, down)
        array = jnp.concatenate([before, array, after], axis=dim)
    return array


def contract_lead(first_op, second_op):
    return lax.dot_general(
        first_op, second_op, (((0,), (0,)), ((), ())), preferred_element_type=jnp.float32
    )


def contract_last(first_op, second_op):
    return lax.dot_general(
        first_op, second_op, (((1,), (1,)), ((), ())), preferred_element_type=jnp.float32
    )


def head_rows(row_term, row_count):
    return lax.psum_scatter(
        row_term(jnp.int32(0), lax.axis_size("head") * row_count).astype(jnp.bfloat16),
        "head",
        scatter_dimension=0,
        tiled=True,
    ).astype(jnp.float32)


def gather_heads(operand):
    return lax.all_gather(operand, "head", axis=0, tiled=True)


def frame_total(operand):
    return lax.psum(operand, "head")


def seq_total(operand):
    return lax.psum(operand, "seq")


def extend_time(operand, half_width):
    return padded(operand, (("seq", 1),), half_width)


def on_device(
    context,
    stream,
    out_weight,
    ln_gain,
    ln_bias,
    glu_weight,
    depth_kernel,
    bn_gain,
    bn_bias,
    proj_weight,
    out_grad,
):
    local_rows = stream.shape[0]
    model_width = ln_gain.shape[0]
    local_frames = stream.shape[1]
    frames_all = local_frames * lax.axis_size("seq")
    kernel_width = depth_kernel.shape[1]
    half_width = kernel_width // 2
    row_offset = lax.axis_index("head") * local_rows

    def attention_term(first_row, row_total):
        return contract_lead(out_weight, context)

    attention = head_rows(attention_term, local_rows)
    hidden = (stream.astype(jnp.float32) + attention).astype(jnp.bfloat16)
    residual = hidden.astype(jnp.float32)
    gain_rows = lax.dynamic_slice_in_dim(ln_gain, row_offset, local_rows)
    bias_rows = lax.dynamic_slice_in_dim(ln_bias, row_offset, local_rows)
    frame_mean = frame_total(jnp.sum(residual, axis=0, keepdims=True)) / model_width
    centered = residual - frame_mean
    frame_rstd = lax.rsqrt(
        frame_total(jnp.sum(centered * centered, axis=0, keepdims=True)) / model_width + epsilon
    )
    standard = centered * frame_rstd
    normed_rows = (standard * gain_rows[:, None] + bias_rows[:, None]).astype(jnp.bfloat16)
    normed = gather_heads(normed_rows)
    pair_out = jnp.einsum("jcd,dt->jct", glu_weight, normed, preferred_element_type=jnp.float32)
    glu_value = pair_out[0]
    glu_gate = pair_out[1]
    gate_sig = jax.nn.sigmoid(glu_gate)
    gated_out = (glu_value * gate_sig).astype(jnp.bfloat16)
    widened = extend_time(gated_out, half_width).astype(jnp.float32)
    conv_out = depth_kernel[:, 0:1] * widened[:, 0:local_frames]
    for tap_index in range(1, kernel_width):
        conv_out = (
            conv_out
            + depth_kernel[:, tap_index : tap_index + 1]
            * widened[:, tap_index : tap_index + local_frames]
        )
    chan_mean = seq_total(jnp.sum(conv_out, axis=1, keepdims=True)) / frames_all
    chan_cent = conv_out - chan_mean
    chan_var = seq_total(jnp.sum(chan_cent * chan_cent, axis=1, keepdims=True)) / frames_all
    chan_rstd = lax.rsqrt(chan_var + epsilon)
    chan_unit = chan_cent * chan_rstd
    shifted = chan_unit * bn_gain[:, None] + bn_bias[:, None]
    shift_sig = jax.nn.sigmoid(shifted)
    swished = (shifted * shift_sig).astype(jnp.bfloat16)

    def branch_term(first_row, row_total):
        return contract_lead(proj_weight, swished)

    branch = head_rows(branch_term, local_rows)
    output = (residual + branch).astype(jnp.bfloat16)
    grad_full = gather_heads(out_grad)
    swish_grad = jnp.dot(proj_weight, grad_full, preferred_element_type=jnp.float32)
    proj_part = contract_last(swished, grad_full)
    shift_grad = swish_grad * shift_sig * (1.0 + shifted * (1.0 - shift_sig))
    bn_pair = seq_total(
        jnp.stack([jnp.sum(shift_grad, axis=1), jnp.sum(shift_grad * chan_unit, axis=1)], axis=1)
    )
    bias_total = bn_pair[:, 0:1]
    gain_total = bn_pair[:, 1:2]
    conv_grad = (
        chan_rstd
        * bn_gain[:, None]
        * (shift_grad - bias_total / frames_all - chan_unit * gain_total / frames_all)
    ).astype(jnp.bfloat16)
    conv_float = conv_grad.astype(jnp.float32)
    grad_wide = extend_time(conv_grad, half_width).astype(jnp.float32)
    gated_grad = depth_kernel[:, 0:1] * grad_wide[:, 2 * half_width : 2 * half_width + local_frames]
    kernel_cols = [jnp.sum(conv_float * widened[:, 0:local_frames], axis=1)]
    for tap_index in range(1, kernel_width):
        back_index = 2 * half_width - tap_index
        gated_grad = (
            gated_grad
            + depth_kernel[:, tap_index : tap_index + 1]
            * grad_wide[:, back_index : back_index + local_frames]
        )
        kernel_cols.append(
            jnp.sum(conv_float * widened[:, tap_index : tap_index + local_frames], axis=1)
        )
    kernel_part = jnp.stack(kernel_cols, axis=1)
    pair_grad = jnp.stack(
        [gated_grad * gate_sig, gated_grad * glu_value * gate_sig * (1.0 - gate_sig)]
    ).astype(jnp.bfloat16)
    glu_part = jnp.einsum("jct,dt->jcd", pair_grad, normed, preferred_element_type=jnp.float32)

    def normed_term(first_row, row_total):
        return jnp.einsum("jcd,jct->dt", glu_weight, pair_grad, preferred_element_type=jnp.float32)

    normed_grad = head_rows(normed_term, local_rows)
    scaled = normed_grad * gain_rows[:, None]
    frame_pair = frame_total(
        jnp.concatenate(
            [
                jnp.sum(scaled, axis=0, keepdims=True),
                jnp.sum(scaled * standard, axis=0, keepdims=True),
            ],
            axis=0,
        )
    )
    stream_rows = out_grad.astype(jnp.float32) + frame_rstd * (
        scaled - frame_pair[0:1] / model_width - standard * frame_pair[1:2] / model_width
    )
    stream_grad = stream_rows.astype(jnp.bfloat16)
    stream_full = gather_heads(stream_grad)
    context_grad = jnp.dot(out_weight, stream_full, preferred_element_type=jnp.float32).astype(
        jnp.bfloat16
    )
    out_part = contract_last(context, stream_full)
    out_weight_grad = seq_total(out_part)
    glu_weight_grad = seq_total(glu_part)
    kernel_grad = seq_total(kernel_part)
    proj_weight_grad = seq_total(proj_part)
    return (
        output,
        stream_grad,
        context_grad,
        out_weight_grad,
        glu_weight_grad,
        kernel_grad,
        bn_pair[:, 1],
        bn_pair[:, 0],
        proj_weight_grad,
    )


def solution(mesh):
    return jax.shard_map(
        on_device,
        mesh=mesh,
        in_specs=(
            P("head", "seq"),
            P("head", "seq"),
            P("head", None),
            P(),
            P(),
            P(None, "head", None),
            P("head", None),
            P("head"),
            P("head"),
            P("head", None),
            P("head", "seq"),
        ),
        out_specs=(
            P("head", "seq"),
            P("head", "seq"),
            P("head", "seq"),
            P("head", None),
            P(None, "head", None),
            P("head", None),
            P("head"),
            P("head"),
            P("head", None),
        ),
        check_vma=False,
    )
```

profile of v0, /device:TPU:1, one launch (start us, length us, event | category | flops | bytes accessed | tf_op | source)
XLA Modules:
  0.0 1307.7 jit_solution(3739211114070087332)
XLA Ops:
  7.2 2.8 convolution_convert_fusion
  11.8 212.5 %reduce-scatter.10.cloned.1.call-done = bf16[96,448]{1,0:T(8,128)(2,1)} async-done(((bf16[1536,448]{1,0:T(8,128)(2,1)}), bf16[96,448]{1,0:T(8,128)(2,1)}) %reduce-scatter.10.cloned.1.call-update) | async-done | bytes 86032
  225.5 32.0 %psum.70 = f32[1,448]{1,0:T(1,128)S(1)} all-reduce(f32[1,448]{1,0:T(1,128)S(1)} %bitcast.186), channel_id=1, replica_groups=mesh['head'=16,'seq'=32] {'head'}, use_global_device_ids=true, to_apply=%region_2.0 | all-reduce | flops 448 | bytes 3584 | tf_op jit(solution)/shard_map/psum | solution.py:48
  257.7 30.1 %psum.71 = f32[1,448]{1,0:T(1,128)S(1)} all-reduce(f32[1,448]{1,0:T(1,128)S(1)} %bitcast.189), channel_id=1, replica_groups=mesh['head'=16,'seq'=32] {'head'}, use_global_device_ids=true, to_apply=%region_4.0 | all-reduce | flops 448 | bytes 3584 | tf_op jit(solution)/shard_map/psum | solution.py:48
  289.6 99.7 %all-gather.4.cloned.1.call-done = bf16[1536,448]{1,0:T(8,128)(2,1)} async-done(((bf16[96,448]{1,0:T(8,128)(2,1)}), bf16[1536,448]{1,0:T(8,128)(2,1)}) %all-gather.4.cloned.1.call-update) | async-done | bytes 1376272 | tf_op jit(solution)/shard_map/all_gather | solution.py:44
  389.4 1.9 fusion.7
  391.4 7.4 collective-permute-start
  398.8 1.9 collective-permute-start.1
  400.7 3.2 collective-permute-done.1
  404.1 2.3 fusion.102
  406.3 50.6 %psum.72 = f32[96,1]{0,1:T(1,128)S(1)} all-reduce(f32[96,1]{0,1:T(1,128)S(1)} %bitcast.223), channel_id=1, replica_groups=mesh['head'=16,'seq'=32] {'seq'}, use_global_device_ids=true, to_apply=%region_6.0 | all-reduce | flops 96 | bytes 768 | tf_op jit(solution)/shard_map/psum | solution.py:52
  457.1 55.5 %psum.73 = f32[96,1]{0,1:T(1,128)S(1)} all-reduce(f32[96,1]{0,1:T(1,128)S(1)} %bitcast.224), channel_id=1, replica_groups=mesh['head'=16,'seq'=32] {'seq'}, use_global_device_ids=true, to_apply=%region_8.0 | all-reduce | flops 96 | bytes 768 | tf_op jit(solution)/shard_map/psum | solution.py:52
  513.3 1.6 copy.38
  514.9 1.9 fusion.100
  516.9 53.0 %psum.74 = f32[96,2]{0,1:T(2,128)S(1)} all-reduce(f32[96,2]{0,1:T(2,128)S(1)} %pad_maximum_fusion.4), channel_id=1, replica_groups=mesh['head'=16,'seq'=32] {'seq'}, use_global_device_ids=true, to_apply=%region_12.0 | all-reduce | flops 192 | bytes 1536 | tf_op jit(solution)/shard_map/psum | solution.py:52
  570.4 2.2 fusion.58
  572.7 1.9 collective-permute-start.2
  574.6 2.4 collective-permute-start.3
  577.0 3.1 collective-permute-done.3
  580.2 2.4 fusion.93
  583.3 1.6 copy.40
  585.1 131.8 %reduce-scatter.12.cloned.1.call-done = bf16[96,448]{1,0:T(8,128)(2,1)} async-done(((bf16[1536,448]{1,0:T(8,128)(2,1)}), bf16[96,448]{1,0:T(8,128)(2,1)}) %reduce-scatter.12.cloned.1.call-update) | async-done | bytes 86032
  717.9 212.4 %reduce-scatter.14.cloned.1.call-done = bf16[96,448]{1,0:T(8,128)(2,1)} async-done(((bf16[1536,448]{1,0:T(8,128)(2,1)}), bf16[96,448]{1,0:T(8,128)(2,1)}) %reduce-scatter.14.cloned.1.call-update) | async-done | bytes 86032
  931.7 31.8 %psum.75 = f32[2,448]{1,0:T(2,128)S(1)} all-reduce(f32[2,448]{1,0:T(2,128)S(1)} %pad_maximum_fusion.3), channel_id=1, replica_groups=mesh['head'=16,'seq'=32] {'head'}, use_global_device_ids=true, to_apply=%region_16.0 | all-reduce | flops 896 | bytes 7168 | tf_op jit(solution)/shard_map/psum | solution.py:48
  963.6 1.1 fusion.24
  965.7 2.9 fusion.99
  968.6 1.7 fusion.3
  970.2 87.8 %all-gather.8.cloned.1.call-done = bf16[1536,448]{1,0:T(8,128)(2,1)} async-done(((bf16[96,448]{1,0:T(8,128)(2,1)}), bf16[1536,448]{1,0:T(8,128)(2,1)}) %all-gather.8.cloned.1.call-update) | async-done | bytes 1376272 | tf_op jit(solution)/shard_map/all_gather | solution.py:44
  1058.0 2.8 convolution_bitcast_fusion.1
  1062.4 104.4 %psum.78 = f32[96,31]{0,1:T(8,128)} all-reduce(f32[96,31]{0,1:T(8,128)S(1)} %stack.154), channel_id=1, replica_groups=mesh['head'=16,'seq'=32] {'seq'}, use_global_device_ids=true, to_apply=%region_50.0 | all-reduce | flops 2976 | bytes 23808 | tf_op jit(solution)/shard_map/psum | solution.py:52
  1168.6 128.4 %all-reduce.3.cloned.1.call-done = (f32[96,1536]{1,0:T(8,128)}, f32[2,96,1536]{2,1,0:T(8,128)}, f32[96,1536]{1,0:T(8,128)}) async-done(((f32[96,1536]{1,0:T(8,128)}, f32[2,96,1536]{2,1,0:T(8,128)}, f32[96,1536]{1,0:T(8,128)}), (f32[96,1536]{1,0:T(8,128)}, f32[2,96,1536]{2,1,0:T(8,128)}, f32[96,1536]{1,0:T(8,128)})) %all-reduce.3.cloned.1.call-update) | async-done | bytes 2359312 | tf_op jit(solution)/shard_map/psum | solution.py:52
  1297.0 2.0 copy.45
  (121 shorter events, 16.0 us)
Async XLA Ops:
  7.2 382.2 %copy-start = (bf16[2,96,1536]{2,1,0:T(8,128)(2,1)S(1)}, bf16[2,96,1536]{2,1,0:T(8,128)(2,1)}, u32[]{:S(2)}) copy-start(bf16[2,96,1536]{2,1,0:T(8,128)(2,1)} %param.16) | copy-start | bytes 1769476
  7.2 4.5 copy-start.9
  7.2 217.1 %reduce-scatter.10.cloned.1.call-start = ((), (), s32[]{:S(2)}) async-start(), calls=%async_computation.6 | async-start | bytes 1671168
  10.0 279.6 %copy-start.10 = (f32[96,31]{0,1:T(8,128)S(1)}, f32[96,31]{0,1:T(8,128)}, u32[]{:S(2)}) copy-start(f32[96,31]{0,1:T(8,128)} %param.17) | copy-start | bytes 35716
  10.1 379.3 %all-gather.4.cloned.1.call-start = ((), (), s32[]{:S(2)}) async-start(), calls=%async_computation.3 | async-start | bytes 1671168 | tf_op jit(solution)/shard_map/all_gather | solution.py:44
  10.9 920.5 %copy-start.11 = (f32[96]{0:T(128)}, f32[96]{0:T(128)S(1)}, u32[]{:S(2)}) copy-start(f32[96]{0:T(128)S(1)} %dynamic_slice.6) | copy-start | bytes 1156
  288.8 226.1 %all-gather.6.cloned.1.call-start = ((), (), s32[]{:S(2)}) async-start(), calls=%async_computation.4 | async-start | bytes 1671168 | tf_op jit(solution)/shard_map/all_gather | solution.py:44
  289.6 427.3 %reduce-scatter.12.cloned.1.call-start = ((), (), s32[]{:S(2)}) async-start(), calls=%async_computation.7 | async-start | bytes 1671168
  391.4 9.3 collective-permute-start
  398.8 5.1 collective-permute-start.1
  404.0 108.5 %copy-start.12 = (f32[96]{0:T(128)S(1)}, f32[96]{0:T(128)}, u32[]{:S(2)}) copy-start(f32[96]{0:T(128)} %param.18) | copy-start | bytes 1156
  404.0 108.5 %copy-start.8 = (bf16[96,1536]{1,0:T(8,128)(2,1)S(1)}, bf16[96,1536]{1,0:T(8,128)(2,1)}, u32[]{:S(2)}) copy-start(bf16[96,1536]{1,0:T(8,128)(2,1)} %param.20) | copy-start | bytes 884740
  404.0 108.5 %copy-start.32 = (f32[96]{0:T(128)S(1)}, f32[96]{0:T(128)}, u32[]{:S(2)}) copy-start(f32[96]{0:T(128)} %param.19) | copy-start | bytes 1156
  514.9 415.5 %reduce-scatter.14.cloned.1.call-start = ((), (), s32[]{:S(2)}) async-start(), calls=%async_computation.8 | async-start | bytes 1671168
  570.4 2.2 copy-start.31
  572.7 4.3 collective-permute-start.2
  574.6 5.5 collective-permute-start.3
  583.3 1.7 copy-start.7
  585.0 473.0 %all-gather.8.cloned.1.call-start = ((), (), s32[]{:S(2)}) async-start(), calls=%async_computation.5 | async-start | bytes 1671168 | tf_op jit(solution)/shard_map/all_gather | solution.py:44
  963.6 5.0 copy-start.2
  965.4 331.6 %all-reduce.3.cloned.1.call-start = ((), (), s32[]{:S(2)}) async-start(), calls=%async_computation.9 | async-start | bytes 4718592 | tf_op jit(solution)/shard_map/psum | solution.py:52
  968.6 89.5 %copy-start.6 = (bf16[96,448]{1,0:T(8,128)(2,1)S(1)}, bf16[96,448]{1,0:T(8,128)(2,1)}, u32[]{:S(2)}) copy-start(bf16[96,448]{1,0:T(8,128)(2,1)} %param.11) | copy-start | bytes 258052
  1060.9 1.2 copy-start.13
  1060.9 1.2 copy-start.14
  1060.9 1.2 copy-start.15
  1060.9 1.2 copy-start.16
  1060.9 1.2 copy-start.17
  1060.9 1.2 copy-start.18
  1061.0 106.5 %copy-start.1 = (bf16[1536,448]{1,0:T(8,128)(2,1)S(1)}, bf16[1536,448]{1,0:T(8,128)(2,1)}, u32[]{:S(2)}) copy-start(bf16[1536,448]{1,0:T(8,128)(2,1)} %all-gather.8.cloned.1.call-done) | copy-start | bytes 4128772
  1061.1 106.5 %copy-start.4 = (bf16[96,1536]{1,0:T(8,128)(2,1)S(1)}, bf16[96,1536]{1,0:T(8,128)(2,1)}, u32[]{:S(2)}) copy-start(bf16[96,1536]{1,0:T(8,128)(2,1)} %param.13) | copy-start | bytes 884740
  1297.0 2.1 copy-start.3
  1297.0 3.1 copy-start.5
  (12 other events, 14.9 us)
Sparse Core Ops, SparseCore 0:
  12.5 211.7 reduce-scatter.9
  289.0 100.3 all-gather.3
  393.0 84.7 all-gather.5
  515.0 201.8 reduce-scatter.11
  721.2 209.0 reduce-scatter.13
  965.6 92.3 all-gather.7
  1062.6 234.3 all-reduce.2
where the time goes:
time: 1310 us
  waiting for transfers between devices  880 us (67%)
  blocking collectives  357 us (27%)
  matrix products  16.2 us (1%)
  between operations  14.7 us (1%)
  local copies, waits for them, and re-layouts  14.6 us (1%)
  starting transfers between devices  14.1 us (1%)
    unnamed x10, waiting for transfers between devices  557 us
    psum x4, blocking collectives, seq_total(): return lax.psum(operand, 'seq')  264 us
    all_gather x3, waiting for transfers between devices, gather_heads(): return lax.all_gather(operand, 'head', axis=0, tiled=True)  187 us
    psum x1, waiting for transfers between devices, seq_total(): return lax.psum(operand, 'seq')  128 us
    psum x3, blocking collectives, frame_total(): return lax.psum(operand, 'head')  93.9 us
  transfers between devices with their start and end apart: 11, of which 8 were waited for; matrix products, arithmetic and copies ran while one was open for 2% of the time, Pallas kernels for 0%

commit v1 on v0

v1 whole, which is shorter than its diff:
```python
import jax
import jax.numpy as jnp
from jax import lax
from jax.sharding import PartitionSpec as P

epsilon = 1e-05
f32 = jnp.float32
bf16 = jnp.bfloat16


def contract_lead(first_op, second_op):
    return lax.dot_general(
        first_op, second_op, (((0,), (0,)), ((), ())), preferred_element_type=f32
    )


def contract_last(first_op, second_op):
    return lax.dot_general(
        first_op, second_op, (((1,), (1,)), ((), ())), preferred_element_type=f32
    )


def exchange(blocks, axis):
    return lax.all_to_all(blocks, axis, 0, 0, tiled=True)


def gather(block, axis):
    count = lax.axis_size(axis)
    copies = jnp.broadcast_to(block[None], (count, *block.shape))
    return exchange(copies, axis)


def neighbours(operand, half_width):
    count, length = lax.axis_size("seq"), operand.shape[1]
    up = [(i, (i + 1) % count) for i in range(count - 1)]
    down = [(j, i) for i, j in up]
    before = lax.ppermute(operand[:, length - half_width :], "seq", up)
    after = lax.ppermute(operand[:, :half_width], "seq", down)
    return jnp.concatenate([before, operand, after], axis=1)


def on_device(
    context,
    stream,
    out_weight,
    ln_gain,
    ln_bias,
    glu_weight,
    depth_kernel,
    bn_gain,
    bn_bias,
    proj_weight,
    out_grad,
):
    rows, frames = stream.shape
    width = ln_gain.shape[0]
    heads = lax.axis_size("head")
    parts = lax.axis_size("seq")
    frames_all = frames * parts
    taps = depth_kernel.shape[1]
    half = taps // 2
    me = lax.axis_index("head")
    gain_col = ln_gain[:, None]
    bias_col = ln_bias[:, None]

    att_part = contract_lead(out_weight, context).astype(bf16).reshape(heads, rows, frames)
    attention = jnp.sum(exchange(att_part, "head").astype(f32), axis=0)
    hidden = (stream.astype(f32) + attention).astype(bf16)

    hidden_full = gather(hidden, "head").reshape(width, frames)
    grad_full = lax.all_gather(out_grad, "head", axis=0, tiled=True)
    hidden_full, grad_full = lax.optimization_barrier((hidden_full, grad_full))
    wide = hidden_full.astype(f32)
    centered = wide - jnp.mean(wide, axis=0, keepdims=True)
    frame_rstd = lax.rsqrt(jnp.mean(centered * centered, axis=0, keepdims=True) + epsilon)
    standard = centered * frame_rstd
    normed = (standard * gain_col + bias_col).astype(bf16)

    pair_out = jnp.einsum("jcd,dt->jct", glu_weight, normed, preferred_element_type=f32)
    glu_value, glu_gate = pair_out[0], pair_out[1]
    gate_sig = jax.nn.sigmoid(glu_gate)
    gated_out = (glu_value * gate_sig).astype(bf16)
    widened = neighbours(gated_out, half).astype(f32)
    conv_out = depth_kernel[:, 0:1] * widened[:, 0:frames]
    for tap in range(1, taps):
        conv_out = conv_out + depth_kernel[:, tap : tap + 1] * widened[:, tap : tap + frames]

    block_mean = jnp.mean(conv_out, axis=1)
    block_cent = conv_out - block_mean[:, None]
    block_square = jnp.sum(block_cent * block_cent, axis=1)
    moments = gather(jnp.stack([block_mean, block_square]), "seq")
    chan_mean = jnp.mean(moments[:, 0], axis=0)
    mean_gap = moments[:, 0] - chan_mean
    chan_var = (
        jnp.sum(moments[:, 1], axis=0) + frames * jnp.sum(mean_gap * mean_gap, axis=0)
    ) / frames_all
    chan_rstd = lax.rsqrt(chan_var + epsilon)[:, None]
    chan_unit = (conv_out - chan_mean[:, None]) * chan_rstd
    shifted = chan_unit * bn_gain[:, None] + bn_bias[:, None]
    shift_sig = jax.nn.sigmoid(shifted)
    swished = (shifted * shift_sig).astype(bf16)

    swish_grad = jnp.dot(proj_weight, grad_full, preferred_element_type=f32)
    shift_grad = swish_grad * shift_sig * (1.0 + shifted * (1.0 - shift_sig))
    sums = gather(
        jnp.stack([jnp.sum(shift_grad, axis=1), jnp.sum(shift_grad * chan_unit, axis=1)]), "seq"
    )
    bias_total, gain_total = jnp.sum(sums[:, 0], axis=0), jnp.sum(sums[:, 1], axis=0)
    conv_grad = (
        chan_rstd
        * bn_gain[:, None]
        * (
            shift_grad
            - (bias_total / frames_all)[:, None]
            - chan_unit * (gain_total / frames_all)[:, None]
        )
    ).astype(bf16)
    conv_float = conv_grad.astype(f32)
    grad_wide = neighbours(conv_grad, half).astype(f32)
    gated_grad = depth_kernel[:, 0:1] * grad_wide[:, 2 * half : 2 * half + frames]
    kernel_cols = [jnp.sum(conv_float * widened[:, 0:frames], axis=1)]
    for tap in range(1, taps):
        back = 2 * half - tap
        gated_grad = (
            gated_grad + depth_kernel[:, tap : tap + 1] * grad_wide[:, back : back + frames]
        )
        kernel_cols.append(jnp.sum(conv_float * widened[:, tap : tap + frames], axis=1))
    kernel_part = jnp.stack(kernel_cols, axis=1)
    pair_grad = jnp.stack(
        [gated_grad * gate_sig, gated_grad * glu_value * gate_sig * (1.0 - gate_sig)]
    ).astype(bf16)

    branch_part = contract_lead(proj_weight, swished).astype(bf16)
    normed_part = jnp.einsum(
        "jcd,jct->dt", glu_weight, pair_grad, preferred_element_type=f32
    ).astype(bf16)
    both = jnp.stack(
        [branch_part.reshape(heads, rows, frames), normed_part.reshape(heads, rows, frames)],
        axis=1,
    )
    both = jnp.sum(exchange(both, "head").astype(f32), axis=0)
    output = (hidden.astype(f32) + both[0]).astype(bf16)

    normed_grad = gather(both[1].astype(bf16), "head").reshape(width, frames).astype(f32)
    scaled = normed_grad * gain_col
    stream_full = (
        grad_full.astype(f32)
        + frame_rstd
        * (
            scaled
            - jnp.mean(scaled, axis=0, keepdims=True)
            - standard * jnp.mean(scaled * standard, axis=0, keepdims=True)
        )
    ).astype(bf16)
    stream_grad = lax.dynamic_slice_in_dim(stream_full, me * rows, rows)
    context_grad = jnp.dot(out_weight, stream_full, preferred_element_type=f32).astype(bf16)

    proj_part = contract_last(swished, grad_full)
    glu_part = jnp.einsum("jct,dt->jcd", pair_grad, normed, preferred_element_type=f32)
    out_part = contract_last(context, stream_full)
    stacked = jnp.concatenate([proj_part[None], glu_part, out_part[None]]).astype(bf16)
    pieces = stacked.reshape(parts, -1, 1152)
    piece = jnp.sum(exchange(pieces, "seq").astype(f32), axis=0)
    totals = gather(piece.astype(bf16), "seq").reshape(4, rows, width).astype(f32)
    kernel_grad = jnp.sum(gather(kernel_part, "seq"), axis=0)
    return (
        output,
        stream_grad,
        context_grad,
        totals[3],
        totals[1:3],
        kernel_grad,
        gain_total,
        bias_total,
        totals[0],
    )


def solution(mesh):
    return jax.shard_map(
        on_device,
        mesh=mesh,
        in_specs=(
            P("head", "seq"),
            P("head", "seq"),
            P("head", None),
            P(),
            P(),
            P(None, "head", None),
            P("head", None),
            P("head"),
            P("head"),
            P("head", None),
            P("head", "seq"),
        ),
        out_specs=(
            P("head", "seq"),
            P("head", "seq"),
            P("head", "seq"),
            P("head", None),
            P(None, "head", None),
            P("head", None),
            P("head"),
            P("head"),
            P("head", None),
        ),
        check_vma=False,
    )
```

time: 1310 us -> 446 us (0.34)
  waiting for transfers between devices: 880 us -> 201 us
  blocking collectives: 357 us -> 107 us
  starting transfers between devices: 14.1 us -> 57.3 us
  other arithmetic: 11 us -> 24.8 us
    unnamed x10 -> x1, waiting for transfers between devices: 557 us -> 0.68 us
    psum x7 -> x0, blocking collectives: 357 us -> none  [the longest x4 264 us: seq_total(): return lax.psum(operand, 'seq')]
    all_to_all x0 -> x6, waiting for transfers between devices: none -> 142 us  [exchange(): return lax.all_to_all(blocks, axis, 0, 0, tiled=True)]
    all_gather x3 -> x1, waiting for transfers between devices: 187 us -> 57.1 us  [on_device(): grad_full = lax.all_gather(out_grad, 'head', axis=0, tiled=True)]
    psum x1 -> x0, waiting for transfers between devices: 128 us -> none  [seq_total(): return lax.psum(operand, 'seq')]
    all_to_all x0 -> x3, blocking collectives: none -> 107 us  [exchange(): return lax.all_to_all(blocks, axis, 0, 0, tiled=True)]
    all_to_all x0 -> x6, starting transfers between devices: none -> 43 us  [exchange(): return lax.all_to_all(blocks, axis, 0, 0, tiled=True)]
  transfers between devices with their start and end apart: 11 -> 11, of which waited for: 8 -> 7; matrix products, arithmetic and copies ran while one was open for 2% -> 4% of each run, Pallas kernels for 0% -> 0%
where the time goes in v1:
time: 446 us; the launch traced here: 443 us
  waiting for transfers between devices  201 us (45%)
  blocking collectives  107 us (24%)
  starting transfers between devices  57.3 us (13%)
  other arithmetic  24.8 us (6%)
  local copies, waits for them, and re-layouts  23 us (5%)
  between operations  15.7 us (4%)
  matrix products  14.1 us (3%)
    all_to_all x6, waiting for transfers between devices, exchange(): return lax.all_to_all(blocks, axis, 0, 0, tiled=True)  142 us
    all_to_all x3, blocking collectives, exchange(): return lax.all_to_all(blocks, axis, 0, 0, tiled=True)  107 us
    all_gather x1, waiting for transfers between devices, on_device(): grad_full = lax.all_gather(out_grad, 'head', axis=0, tiled=True)  57.1 us
    all_to_all x6, starting transfers between devices, exchange(): return lax.all_to_all(blocks, axis, 0, 0, tiled=True)  43 us
  transfers between devices with their start and end apart: 11, of which 7 were waited for; matrix products, arithmetic and copies ran while one was open for 4% of the time, Pallas kernels for 0%

profile of v1, /device:TPU:1, one launch (start us, length us, event | category | flops | bytes accessed | tf_op | source)
XLA Modules:
  0.0 443.2 jit_solution(8046332122449887351)
XLA Ops:
  10.4 13.6 %all-to-all-start = ((bf16[16,96,448]{2,1,0:T(8,128)(2,1)}), bf16[16,96,448]{2,1,0:T(8,128)(2,1)S(1)}, u32[]{:S(2)}, u32[]{:S(2)}) async-start(bf16[16,96,448]{2,1,0:T(8,128)(2,1)} %bitcast.190), calls=%async_computation | async-start | bytes 3145728 | tf_op jit(solution)/shard_map/all_to_all | solution.py:24
  24.7 39.6 %all-to-all-done = bf16[16,96,448]{2,1,0:T(8,128)(2,1)S(1)} async-done(((bf16[16,96,448]{2,1,0:T(8,128)(2,1)}), bf16[16,96,448]{2,1,0:T(8,128)(2,1)S(1)}, u32[]{:S(2)}, u32[]{:S(2)}) %all-to-all-start) | async-done | bytes 1376288 | tf_op jit(solution)/shard_map/all_to_all | solution.py:24
  66.5 6.0 %all-to-all-start.1 = ((bf16[16,96,448]{2,1,0:T(8,128)(2,1)}), bf16[16,96,448]{2,1,0:T(8,128)(2,1)S(1)}, u32[]{:S(2)}, u32[]{:S(2)}) async-start(bf16[16,96,448]{2,1,0:T(8,128)(2,1)} %broadcast_in_dim.20), calls=%async_computation.1 | async-start | bytes 3145728 | tf_op jit(solution)/shard_map/all_to_all | solution.py:24
  72.7 57.1 %all-gather.2.cloned.1.call-done = bf16[1536,448]{1,0:T(8,128)(2,1)} async-done(((bf16[96,448]{1,0:T(8,128)(2,1)}), bf16[1536,448]{1,0:T(8,128)(2,1)}) %all-gather.2.cloned.1.call-update) | async-done | bytes 1376272 | tf_op jit(solution)/shard_map/all_gather | solution.py:71
  131.7 5.6 %collective-permute-start.1 = (bf16[96,15]{1,0:T(8,128)(2,1)S(1)}, bf16[96,15]{1,0:T(8,128)(2,1)S(1)}, u32[]{:S(2)}, u32[]{:S(2)}) collective-permute-start(bf16[96,15]{1,0:T(8,128)(2,1)S(1)} %get-tuple-element.58), channel_id=1, source_target_pairs={{1,0},{2,1},{3,2},{4,3},{5,4},{6,5},{7,6},{8,7},{9,8},{10,9},{11,1... | collective-permute-start | bytes 8648 | tf_op jit(solution)/shard_map/ppermute | solution.py:38
  137.2 3.0 collective-permute-start
  141.5 2.3 fusion.100
  144.1 17.0 %all_to_all.45 = f32[32,2,96]{2,1,0:T(2,128)S(1)} all-to-all(f32[32,2,96]{2,1,0:T(2,128)S(1)} %broadcast_in_dim.21), channel_id=1, replica_groups=mesh['head'=16,'seq'=32] {'seq'}, dimensions={0} | all-to-all | bytes 49152 | tf_op jit(solution)/shard_map/all_to_all | solution.py:24
  161.8 1.9 fusion.97
  163.8 11.6 %all_to_all.46 = f32[32,2,96]{2,1,0:T(2,128)S(1)} all-to-all(f32[32,2,96]{2,1,0:T(2,128)S(1)} %broadcast_in_dim.22), channel_id=1, replica_groups=mesh['head'=16,'seq'=32] {'seq'}, dimensions={0} | all-to-all | bytes 49152 | tf_op jit(solution)/shard_map/all_to_all | solution.py:24
  175.9 3.0 fusion.54
  179.3 2.8 collective-permute-start.3
  182.1 2.9 collective-permute-start.2
  185.0 2.4 fusion.14
  187.5 2.6 copy.45
  190.4 3.0 fusion.91
  195.3 2.5 copy.48
  197.8 2.2 pad_maximum_fusion
  200.4 78.9 %all_to_all.47 = bf16[16,2,96,448]{3,2,1,0:T(8,128)(2,1)S(1)} all-to-all(bf16[16,2,96,448]{3,2,1,0:T(8,128)(2,1)S(1)} %copy.49), channel_id=1, replica_groups=mesh['head'=16,'seq'=32] {'head'}, dimensions={0} | all-to-all | bytes 5505024 | tf_op jit(solution)/shard_map/all_to_all | solution.py:24
  281.8 5.3 %all-to-all-start.5 = ((bf16[16,96,448]{2,1,0:T(8,128)(2,1)}), bf16[16,96,448]{2,1,0:T(8,128)(2,1)}, u32[]{:S(2)}, u32[]{:S(2)}) async-start(bf16[16,96,448]{2,1,0:T(8,128)(2,1)} %broadcast_in_dim.24), calls=%async_computation.5 | async-start | bytes 3145728 | tf_op jit(solution)/shard_map/all_to_all | solution.py:24
  287.2 2.0 fusion.16
  290.2 34.9 %all-to-all-done.5 = bf16[16,96,448]{2,1,0:T(8,128)(2,1)} async-done(((bf16[16,96,448]{2,1,0:T(8,128)(2,1)}), bf16[16,96,448]{2,1,0:T(8,128)(2,1)}, u32[]{:S(2)}, u32[]{:S(2)}) %all-to-all-start.5) | async-done | bytes 1376288 | tf_op jit(solution)/shard_map/all_to_all | solution.py:24
  325.1 2.3 fusion.7
  329.3 2.6 fusion.11
  335.8 6.2 %all-to-all-start.6 = ((bf16[32,16,1152]{2,1,0:T(8,128)(2,1)}), bf16[32,16,1152]{2,1,0:T(8,128)(2,1)S(1)}, u32[]{:S(2)}, u32[]{:S(2)}) async-start(bf16[32,16,1152]{2,1,0:T(8,128)(2,1)} %convert_element_type.117), calls=%async_computation.6 | async-start | bytes 2359296 | tf_op jit(solution)/shard_map/all_to_all | solution.py:24
  343.3 27.9 %all-to-all-done.6 = bf16[32,16,1152]{2,1,0:T(8,128)(2,1)S(1)} async-done(((bf16[32,16,1152]{2,1,0:T(8,128)(2,1)}), bf16[32,16,1152]{2,1,0:T(8,128)(2,1)S(1)}, u32[]{:S(2)}, u32[]{:S(2)}) %all-to-all-start.6) | async-done | bytes 1179680 | tf_op jit(solution)/shard_map/all_to_all | solution.py:24
  372.0 6.3 %all-to-all-start.8 = ((f32[32,96,31]{1,2,0:T(8,128)}), f32[32,96,31]{1,2,0:T(8,128)}, u32[]{:S(2)}, u32[]{:S(2)}) async-start(f32[32,96,31]{1,2,0:T(8,128)} %broadcast_in_dim.28), calls=%async_computation.8 | async-start | bytes 1048576 | tf_op jit(solution)/shard_map/all_to_all | solution.py:24
  378.5 16.6 %all-to-all-done.8 = f32[32,96,31]{1,2,0:T(8,128)} async-done(((f32[32,96,31]{1,2,0:T(8,128)}), f32[32,96,31]{1,2,0:T(8,128)}, u32[]{:S(2)}, u32[]{:S(2)}) %all-to-all-start.8) | async-done | bytes 380960 | tf_op jit(solution)/shard_map/all_to_all | solution.py:24
  396.2 5.7 %all-to-all-start.7 = ((bf16[32,16,1152]{2,1,0:T(8,128)(2,1)}), bf16[32,16,1152]{2,1,0:T(8,128)(2,1)S(1)}, u32[]{:S(2)}, u32[]{:S(2)}) async-start(bf16[32,16,1152]{2,1,0:T(8,128)(2,1)} %broadcast_in_dim.27), calls=%async_computation.7 | async-start | bytes 2359296 | tf_op jit(solution)/shard_map/all_to_all | solution.py:24
  405.8 2.0 fusion.21
  407.8 23.3 %all-to-all-done.7 = bf16[32,16,1152]{2,1,0:T(8,128)(2,1)S(1)} async-done(((bf16[32,16,1152]{2,1,0:T(8,128)(2,1)}), bf16[32,16,1152]{2,1,0:T(8,128)(2,1)S(1)}, u32[]{:S(2)}, u32[]{:S(2)}) %all-to-all-start.7) | async-done | bytes 1179680 | tf_op jit(solution)/shard_map/all_to_all | solution.py:24
  434.3 2.0 squeeze.25
  (266 shorter events, 32.3 us)
Async XLA Ops:
  7.2 123.5 %copy-start = (bf16[2,96,1536]{2,1,0:T(8,128)(2,1)S(1)}, bf16[2,96,1536]{2,1,0:T(8,128)(2,1)}, u32[]{:S(2)}) copy-start(bf16[2,96,1536]{2,1,0:T(8,128)(2,1)} %param.16) | copy-start | bytes 1769476
  10.4 53.9 %all-to-all-start = ((bf16[16,96,448]{2,1,0:T(8,128)(2,1)}), bf16[16,96,448]{2,1,0:T(8,128)(2,1)S(1)}, u32[]{:S(2)}, u32[]{:S(2)}) async-start(bf16[16,96,448]{2,1,0:T(8,128)(2,1)} %bitcast.190), calls=%async_computation | async-start | bytes 3145728 | tf_op jit(solution)/shard_map/all_to_all | solution.py:24
  23.9 105.9 %all-gather.2.cloned.1.call-start = ((), (), s32[]{:S(2)}) async-start(), calls=%async_computation.9 | async-start | bytes 1671168 | tf_op jit(solution)/shard_map/all_gather | solution.py:71
  66.5 64.2 %copy-start.98 = (f32[1536]{0:T(1024)S(1)}, f32[1536]{0:T(1024)}, u32[]{:S(2)}) copy-start(f32[1536]{0:T(1024)} %param.15) | copy-start | bytes 18436
  66.5 63.3 %all-to-all-start.1 = ((bf16[16,96,448]{2,1,0:T(8,128)(2,1)}), bf16[16,96,448]{2,1,0:T(8,128)(2,1)S(1)}, u32[]{:S(2)}, u32[]{:S(2)}) async-start(bf16[16,96,448]{2,1,0:T(8,128)(2,1)} %broadcast_in_dim.20), calls=%async_computation.1 | async-start | bytes 3145728 | tf_op jit(solution)/shard_map/all_to_all | solution.py:24
  72.5 68.8 %copy-start.14 = (f32[96]{0:T(128)}, f32[96]{0:T(128)S(1)}, u32[]{:S(2)}) copy-start(f32[96]{0:T(128)S(1)} %get-tuple-element.63) | copy-start | bytes 1156
  72.6 68.8 %copy-start.16 = (f32[96]{0:T(128)}, f32[96]{0:T(128)S(1)}, u32[]{:S(2)}) copy-start(f32[96]{0:T(128)S(1)} %get-tuple-element.64) | copy-start | bytes 1156
  72.6 68.8 %copy-start.18 = (f32[96]{0:T(128)}, f32[96]{0:T(128)S(1)}, u32[]{:S(2)}) copy-start(f32[96]{0:T(128)S(1)} %get-tuple-element.65) | copy-start | bytes 1156
  72.6 68.8 %copy-start.20 = (f32[96]{0:T(128)}, f32[96]{0:T(128)S(1)}, u32[]{:S(2)}) copy-start(f32[96]{0:T(128)S(1)} %get-tuple-element.66) | copy-start | bytes 1156
  72.6 68.8 %copy-start.22 = (f32[96]{0:T(128)}, f32[96]{0:T(128)S(1)}, u32[]{:S(2)}) copy-start(f32[96]{0:T(128)S(1)} %get-tuple-element.67) | copy-start | bytes 1156
  72.6 68.8 %copy-start.24 = (f32[96]{0:T(128)}, f32[96]{0:T(128)S(1)}, u32[]{:S(2)}) copy-start(f32[96]{0:T(128)S(1)} %get-tuple-element.68) | copy-start | bytes 1156
  72.6 68.8 %copy-start.26 = (f32[96]{0:T(128)}, f32[96]{0:T(128)S(1)}, u32[]{:S(2)}) copy-start(f32[96]{0:T(128)S(1)} %get-tuple-element.69) | copy-start | bytes 1156
  72.6 68.8 %copy-start.28 = (f32[96]{0:T(128)}, f32[96]{0:T(128)S(1)}, u32[]{:S(2)}) copy-start(f32[96]{0:T(128)S(1)} %get-tuple-element.70) | copy-start | bytes 1156
  72.6 68.8 %copy-start.30 = (f32[96]{0:T(128)}, f32[96]{0:T(128)S(1)}, u32[]{:S(2)}) copy-start(f32[96]{0:T(128)S(1)} %get-tuple-element.71) | copy-start | bytes 1156
  72.6 68.8 %copy-start.32 = (f32[96]{0:T(128)}, f32[96]{0:T(128)S(1)}, u32[]{:S(2)}) copy-start(f32[96]{0:T(128)S(1)} %get-tuple-element.72) | copy-start | bytes 1156
  72.6 68.8 %copy-start.34 = (f32[96]{0:T(128)}, f32[96]{0:T(128)S(1)}, u32[]{:S(2)}) copy-start(f32[96]{0:T(128)S(1)} %get-tuple-element.73) | copy-start | bytes 1156
  72.7 68.8 %copy-start.36 = (f32[96]{0:T(128)}, f32[96]{0:T(128)S(1)}, u32[]{:S(2)}) copy-start(f32[96]{0:T(128)S(1)} %get-tuple-element.74) | copy-start | bytes 1156
  72.7 68.8 %copy-start.38 = (f32[96]{0:T(128)}, f32[96]{0:T(128)S(1)}, u32[]{:S(2)}) copy-start(f32[96]{0:T(128)S(1)} %get-tuple-element.75) | copy-start | bytes 1156
  72.7 68.8 %copy-start.40 = (f32[96]{0:T(128)}, f32[96]{0:T(128)S(1)}, u32[]{:S(2)}) copy-start(f32[96]{0:T(128)S(1)} %get-tuple-element.76) | copy-start | bytes 1156
  72.7 68.8 %copy-start.42 = (f32[96]{0:T(128)}, f32[96]{0:T(128)S(1)}, u32[]{:S(2)}) copy-start(f32[96]{0:T(128)S(1)} %get-tuple-element.77) | copy-start | bytes 1156
  72.7 68.8 %copy-start.44 = (f32[96]{0:T(128)}, f32[96]{0:T(128)S(1)}, u32[]{:S(2)}) copy-start(f32[96]{0:T(128)S(1)} %get-tuple-element.78) | copy-start | bytes 1156
  72.7 68.8 %copy-start.46 = (f32[96]{0:T(128)}, f32[96]{0:T(128)S(1)}, u32[]{:S(2)}) copy-start(f32[96]{0:T(128)S(1)} %get-tuple-element.79) | copy-start | bytes 1156
  72.7 68.8 %copy-start.48 = (f32[96]{0:T(128)}, f32[96]{0:T(128)S(1)}, u32[]{:S(2)}) copy-start(f32[96]{0:T(128)S(1)} %get-tuple-element.80) | copy-start | bytes 1156
  72.7 68.8 %copy-start.50 = (f32[96]{0:T(128)}, f32[96]{0:T(128)S(1)}, u32[]{:S(2)}) copy-start(f32[96]{0:T(128)S(1)} %get-tuple-element.81) | copy-start | bytes 1156
  131.7 8.7 %collective-permute-start.1 = (bf16[96,15]{1,0:T(8,128)(2,1)S(1)}, bf16[96,15]{1,0:T(8,128)(2,1)S(1)}, u32[]{:S(2)}, u32[]{:S(2)}) collective-permute-start(bf16[96,15]{1,0:T(8,128)(2,1)S(1)} %get-tuple-element.58), channel_id=1, source_target_pairs={{1,0},{2,1},{3,2},{4,3},{5,4},{6,5},{7,6},{8,7},{9,8},{10,9},{11,1... | collective-permute-start | bytes 8648 | tf_op jit(solution)/shard_map/ppermute | solution.py:38
  137.2 4.0 collective-permute-start
  179.3 10.8 %collective-permute-start.3 = (bf16[96,15]{1,0:T(8,128)(2,1)S(1)}, bf16[96,15]{1,0:T(8,128)(2,1)S(1)}, u32[]{:S(2)}, u32[]{:S(2)}) collective-permute-start(bf16[96,15]{1,0:T(8,128)(2,1)S(1)} %get-tuple-element.56), channel_id=1, source_target_pairs={{1,0},{2,1},{3,2},{4,3},{5,4},{6,5},{7,6},{8,7},{9,8},{10,9},{11,1... | collective-permute-start | bytes 8648 | tf_op jit(solution)/shard_map/ppermute | solution.py:38
  182.1 8.0 %collective-permute-start.2 = (bf16[96,15]{1,0:T(8,128)(2,1)S(1)}, bf16[96,15]{1,0:T(8,128)(2,1)S(1)}, u32[]{:S(2)}, u32[]{:S(2)}) collective-permute-start(bf16[96,15]{1,0:T(8,128)(2,1)S(1)} %get-tuple-element.55), channel_id=1, source_target_pairs={{0,1},{1,2},{2,3},{3,4},{4,5},{5,6},{6,7},{7,8},{8,9},{9,10},{10,1... | collective-permute-start | bytes 8648 | tf_op jit(solution)/shard_map/ppermute | solution.py:37
  281.8 43.3 %all-to-all-start.5 = ((bf16[16,96,448]{2,1,0:T(8,128)(2,1)}), bf16[16,96,448]{2,1,0:T(8,128)(2,1)}, u32[]{:S(2)}, u32[]{:S(2)}) async-start(bf16[16,96,448]{2,1,0:T(8,128)(2,1)} %broadcast_in_dim.24), calls=%async_computation.5 | async-start | bytes 3145728 | tf_op jit(solution)/shard_map/all_to_all | solution.py:24
  335.8 35.4 %all-to-all-start.6 = ((bf16[32,16,1152]{2,1,0:T(8,128)(2,1)}), bf16[32,16,1152]{2,1,0:T(8,128)(2,1)S(1)}, u32[]{:S(2)}, u32[]{:S(2)}) async-start(bf16[32,16,1152]{2,1,0:T(8,128)(2,1)} %convert_element_type.117), calls=%async_computation.6 | async-start | bytes 2359296 | tf_op jit(solution)/shard_map/all_to_all | solution.py:24
  372.0 23.1 %all-to-all-start.8 = ((f32[32,96,31]{1,2,0:T(8,128)}), f32[32,96,31]{1,2,0:T(8,128)}, u32[]{:S(2)}, u32[]{:S(2)}) async-start(f32[32,96,31]{1,2,0:T(8,128)} %broadcast_in_dim.28), calls=%async_computation.8 | async-start | bytes 1048576 | tf_op jit(solution)/shard_map/all_to_all | solution.py:24
  396.2 34.9 %all-to-all-start.7 = ((bf16[32,16,1152]{2,1,0:T(8,128)(2,1)}), bf16[32,16,1152]{2,1,0:T(8,128)(2,1)S(1)}, u32[]{:S(2)}, u32[]{:S(2)}) async-start(bf16[32,16,1152]{2,1,0:T(8,128)(2,1)} %broadcast_in_dim.27), calls=%async_computation.7 | async-start | bytes 2359296 | tf_op jit(solution)/shard_map/all_to_all | solution.py:24
  (79 other events, 755.0 us)
Sparse Core Ops, SparseCore 0:
  28.0 101.8 all-gather.1

commit v2 on v1

v2 whole, which is shorter than its diff:
```python
import functools

import jax
import jax.numpy as jnp
from jax import lax
from jax.experimental import pallas as pl
from jax.experimental.pallas import tpu as pltpu
from jax.sharding import PartitionSpec as P

epsilon = 1e-05
f32 = jnp.float32
bf16 = jnp.bfloat16


def contract_lead(first_op, second_op):
    return lax.dot_general(
        first_op, second_op, (((0,), (0,)), ((), ())), preferred_element_type=f32
    )


def contract_last(first_op, second_op):
    return lax.dot_general(
        first_op, second_op, (((1,), (1,)), ((), ())), preferred_element_type=f32
    )


def exchange(blocks, axis):
    return lax.all_to_all(blocks, axis, 0, 0, tiled=True)


def gather(block, axis):
    count = lax.axis_size(axis)
    copies = jnp.broadcast_to(block[None], (count, *block.shape))
    return exchange(copies, axis)


def line_groups():
    half = lax.axis_size("head") // 2
    return [[side * half + i for i in range(half)] for side in range(2)]


def across(operand):
    count = lax.axis_size("head")
    return lax.ppermute(operand, "head", [(i, (i + count // 2) % count) for i in range(count)])


def swap_bit(operand, bit):
    count = lax.axis_size("seq")
    return lax.ppermute(operand, "seq", [(i, i ^ bit) for i in range(count)])


def halves(operand, bit):
    mine = (lax.axis_index("seq") // bit) % 2
    size = operand.shape[0] // 2
    keep = lax.dynamic_slice_in_dim(operand, mine * size, size)
    send = lax.dynamic_slice_in_dim(operand, (1 - mine) * size, size)
    return keep, send


def joined(mine_rows, other_rows, bit):
    low = (lax.axis_index("seq") // bit) % 2 == 0
    return jnp.concatenate(
        [jnp.where(low, mine_rows, other_rows), jnp.where(low, other_rows, mine_rows)]
    )


def shifted_left(operand, distance):
    lanes = operand.shape[1]
    return pltpu.roll(operand, (lanes - distance) % lanes, 1)


def conv_back_kernel(
    consts_ref, taps_ref, inside_ref, swish_ref, conv_ref, pair_out_ref, pair_ref, grad_ref, *, taps
):
    frames = pair_ref.shape[2]

    def chunk(index, carry):
        at = pl.ds(pl.multiple_of(index * 16, 16), 16)
        consts = consts_ref[at, :]
        mean, rstd, gain, bias = (consts[:, i : i + 1] for i in range(4))
        bias_mean, gain_mean = consts[:, 4:5], consts[:, 5:6]
        unit = (conv_ref[at, :] - mean) * rstd
        shifted = unit * gain + bias
        sig = jax.nn.sigmoid(shifted)
        shift_grad = swish_ref[at, :] * sig * (1.0 + shifted * (1.0 - sig))
        grad = rstd * gain * (shift_grad - bias_mean - unit * gain_mean)
        grad = jnp.where(inside_ref[...] > 0.0, grad, 0.0).astype(bf16).astype(f32)
        grad_ref[at, :] = grad
        kernel = taps_ref[at, :]
        total = kernel[:, 0:1] * shifted_left(grad, taps - 1)[:, :frames]
        for tap in range(1, taps):
            total = total + kernel[:, tap : tap + 1] * shifted_left(grad, taps - 1 - tap)[:, :frames]
        gate_sig = jax.nn.sigmoid(pair_out_ref[1, at, :])
        value_grad = total * gate_sig
        pair_ref[0, at, :] = value_grad.astype(bf16)
        pair_ref[1, at, :] = (value_grad * pair_out_ref[0, at, :] * (1.0 - gate_sig)).astype(bf16)
        return carry

    lax.fori_loop(0, pair_ref.shape[1] // 16, chunk, 0)


def taps_grad_kernel(grad_ref, widened_ref, out_ref, *, taps, frames):
    half = taps // 2
    column = lax.broadcasted_iota(jnp.int32, (16, out_ref.shape[1]), 1)

    def chunk(index, carry):
        at = pl.ds(pl.multiple_of(index * 16, 16), 16)
        grad = shifted_left(grad_ref[at, :], half)[:, :frames]
        widened = widened_ref[at, :]
        out = jnp.zeros(column.shape, f32)
        for tap in range(taps):
            near = shifted_left(widened, half + tap)[:, :frames]
            out = jnp.where(column == tap, jnp.sum(grad * near, axis=1, keepdims=True), out)
        out_ref[at, :] = out
        return carry

    lax.fori_loop(0, out_ref.shape[0] // 16, chunk, 0)


def conv_back(consts, kernel, inside, swish_wide, conv_wide, pair_out, taps):
    return pl.pallas_call(
        functools.partial(conv_back_kernel, taps=taps),
        out_shape=(
            jax.ShapeDtypeStruct(pair_out.shape, bf16),
            jax.ShapeDtypeStruct(conv_wide.shape, f32),
        ),
        name="conv_back",
    )(consts, kernel, inside, swish_wide, conv_wide, pair_out)


def taps_grad(grad_wide, widened, taps, frames):
    return pl.pallas_call(
        functools.partial(taps_grad_kernel, taps=taps, frames=frames),
        out_shape=jax.ShapeDtypeStruct((grad_wide.shape[0], 128), f32),
        name="taps_grad",
    )(grad_wide, widened)


def neighbours(operand, half_width, lanes):
    count, length = lax.axis_size("seq"), operand.shape[1]
    up = [(i, (i + 1) % count) for i in range(count - 1)]
    down = [(j, i) for i, j in up]
    before = lax.ppermute(operand[:, length - half_width :], "seq", up)
    after = lax.ppermute(operand[:, :half_width], "seq", down)
    spare = jnp.zeros((operand.shape[0], lanes - length - 2 * half_width), operand.dtype)
    return jnp.concatenate([before, operand, after, spare], axis=1)


def on_device(
    context,
    stream,
    out_weight,
    ln_gain,
    ln_bias,
    glu_weight,
    depth_kernel,
    bn_gain,
    bn_bias,
    proj_weight,
    out_grad,
):
    rows, frames = stream.shape
    width = ln_gain.shape[0]
    heads = lax.axis_size("head")
    parts = lax.axis_size("seq")
    frames_all = frames * parts
    taps = depth_kernel.shape[1]
    half = taps // 2
    lanes = -(-(frames + 4 * half) // 128) * 128
    me = lax.axis_index("head")
    line = heads // 2
    side = me // line
    gain_col = ln_gain[:, None]
    bias_col = ln_bias[:, None]

    def own_half(weight):
        keep = lax.dynamic_slice_in_dim(weight, side * (width // 2), width // 2, axis=1)
        send = lax.dynamic_slice_in_dim(weight, (1 - side) * (width // 2), width // 2, axis=1)
        return keep, across(send)

    def line_exchange(blocks):
        blocks = lax.all_to_all(
            blocks,
            "head",
            0,
            0,
            tiled=True,
            axis_index_groups=line_groups(),
        )
        return jnp.sum(blocks.astype(f32), axis=0)

    def line_gather(block):
        blocks = lax.all_to_all(
            jnp.broadcast_to(block[None], (line, *block.shape)),
            "head",
            0,
            0,
            tiled=True,
            axis_index_groups=line_groups(),
        )
        return blocks.reshape(line * block.shape[0], *block.shape[1:])

    context_pair = jnp.concatenate([context, across(context)])
    out_half = jnp.concatenate(own_half(out_weight))
    attention = line_exchange(
        contract_lead(out_half, context_pair).astype(bf16).reshape(line, rows, frames)
    )
    hidden = (stream.astype(f32) + attention).astype(bf16)

    glu_half = jnp.concatenate(own_half(glu_weight.reshape(2 * rows, width)))
    glu_turned, proj_turned = lax.optimization_barrier(
        (
            glu_half.T,
            jnp.transpose(proj_weight.reshape(rows, 2, line, rows), (2, 1, 3, 0)).reshape(
                width, rows
            ),
        )
    )

    grad_other = across(out_grad)
    hidden, grad_other = lax.optimization_barrier((hidden, grad_other))
    hidden_full = gather(hidden, "head").reshape(width, frames)
    grad_pair = jnp.stack(
        [jnp.where(side == 0, out_grad, grad_other), jnp.where(side == 0, grad_other, out_grad)]
    )
    grad_lines = lax.all_gather(
        grad_pair, "head", axis=1, tiled=False, axis_index_groups=line_groups()
    )
    wide = hidden_full.astype(f32)
    centered = wide - jnp.mean(wide, axis=0, keepdims=True)
    frame_rstd = lax.rsqrt(jnp.mean(centered * centered, axis=0, keepdims=True) + epsilon)
    standard = centered * frame_rstd
    normed = (standard * gain_col + bias_col).astype(bf16)

    pair_out = jnp.einsum("jcd,dt->jct", glu_weight, normed, preferred_element_type=f32)
    glu_value, glu_gate = pair_out[0], pair_out[1]
    gate_sig = jax.nn.sigmoid(glu_gate)
    gated_out = (glu_value * gate_sig).astype(bf16)
    widened = neighbours(gated_out, 2 * half, lanes).astype(f32)
    frames_wide = frames + 2 * half
    conv_wide = depth_kernel[:, 0:1] * widened[:, 0:frames_wide]
    for tap in range(1, taps):
        conv_wide = (
            conv_wide + depth_kernel[:, tap : tap + 1] * widened[:, tap : tap + frames_wide]
        )

    place = lax.axis_index("seq") * frames - half + jnp.arange(lanes)
    inside = (place >= 0) & (place < frames_all) & (jnp.arange(lanes) < frames_wide)
    inside = inside.astype(f32)[None, :]
    conv_wide = jnp.pad(conv_wide, ((0, 0), (0, lanes - frames_wide)))
    conv_out = conv_wide[:, half : half + frames]
    block_mean = jnp.mean(conv_out, axis=1)
    block_cent = conv_out - block_mean[:, None]
    block_square = jnp.sum(block_cent * block_cent, axis=1)
    block, grad_lines = lax.optimization_barrier(
        (jnp.stack([block_mean, block_square]), grad_lines)
    )
    moments = gather(block, "seq")
    grad_full = grad_lines.reshape(width, frames)
    swish_grad = jnp.dot(proj_weight, grad_full, preferred_element_type=f32)
    swish_wide = neighbours(swish_grad, half, lanes)
    chan_mean = jnp.mean(moments[:, 0], axis=0)
    mean_gap = moments[:, 0] - chan_mean
    chan_var = (
        jnp.sum(moments[:, 1], axis=0) + frames * jnp.sum(mean_gap * mean_gap, axis=0)
    ) / frames_all
    chan_rstd = lax.rsqrt(chan_var + epsilon)
    chan_unit = (conv_out - chan_mean[:, None]) * chan_rstd[:, None]
    shifted = chan_unit * bn_gain[:, None] + bn_bias[:, None]
    shift_sig = jax.nn.sigmoid(shifted)
    swished = (shifted * shift_sig).astype(bf16)
    shift_grad = swish_grad * shift_sig * (1.0 + shifted * (1.0 - shift_sig))

    sums = gather(
        jnp.stack([jnp.sum(shift_grad, axis=1), jnp.sum(shift_grad * chan_unit, axis=1)]), "seq"
    )
    bias_total, gain_total = jnp.sum(sums[:, 0], axis=0), jnp.sum(sums[:, 1], axis=0)
    consts = jnp.stack(
        [
            chan_mean,
            chan_rstd,
            bn_gain,
            bn_bias,
            bias_total / frames_all,
            gain_total / frames_all,
        ],
        axis=1,
    )
    pair_grad, grad_wide = conv_back(
        consts, depth_kernel, inside, swish_wide, conv_wide, pair_out, taps
    )

    branch_part = jnp.dot(proj_turned, swished, preferred_element_type=f32).astype(bf16)
    branch_sum = lax.psum_scatter(
        branch_part, "head", scatter_dimension=0, tiled=True, axis_index_groups=line_groups()
    ).reshape(2, rows, frames)
    pair_rows = pair_grad.reshape(2 * rows, frames)
    pair_both = jnp.concatenate([pair_rows, across(pair_rows)])
    normed_part = jnp.dot(glu_turned, pair_both, preferred_element_type=f32).astype(bf16)
    bias_out = jnp.einsum("jcd,d->jc", glu_weight.astype(f32), ln_bias)
    gain_out = jnp.einsum("jcd,d->jc", glu_weight.astype(f32), ln_gain)
    pair_float = pair_grad.astype(f32)
    frame_sums = jnp.stack(
        [
            jnp.sum(pair_float * gain_out[:, :, None], axis=(0, 1)),
            jnp.sum(pair_float * (pair_out - bias_out[:, :, None]), axis=(0, 1)),
        ]
    )
    frame_sums = jnp.pad(frame_sums.astype(bf16), ((0, 14), (0, 0)))
    normed_rows = line_exchange(
        jnp.concatenate(
            [
                normed_part.reshape(line, rows, frames),
                jnp.broadcast_to(frame_sums[None], (line, 16, frames)),
            ],
            axis=1,
        )
    )

    proj_part = contract_last(swished, grad_full)
    glu_part = jnp.einsum("jct,dt->jcd", pair_grad, normed, preferred_element_type=f32)
    early = jnp.concatenate([proj_part[None], glu_part]).reshape(3 * rows, width)
    for bit in (1, parts // 2):
        keep, send = halves(early, bit)
        early = keep + swap_bit(send.astype(bf16), bit).astype(f32)
    normed_rows, early, branch_sum = lax.optimization_barrier((normed_rows, early, branch_sum))

    branch_keep = lax.dynamic_index_in_dim(branch_sum, side, 0, keepdims=False)
    branch_send = lax.dynamic_index_in_dim(branch_sum, 1 - side, 0, keepdims=False)
    branch = branch_keep.astype(f32) + across(branch_send).astype(f32)
    columns = [
        [x * (parts // 2) + 2 * y + core for y in range(parts // 4)]
        for x in range(2)
        for core in range(2)
    ]
    early = lax.all_gather(early.astype(bf16), "seq", axis=0, axis_index_groups=columns)
    kernel_part = taps_grad(grad_wide, widened, taps, frames)[:, :taps]

    def side_half(array):
        return lax.dynamic_slice_in_dim(array, side * (width // 2), width // 2)

    line_sums = normed_rows[rows : rows + 2]
    frame_means = (line_sums + across(line_sums)) / width
    normed_grad = line_gather(normed_rows[:rows].astype(bf16)).astype(f32)
    scaled = normed_grad * side_half(gain_col)
    stream_half = (
        side_half(grad_full).astype(f32)
        + frame_rstd
        * (scaled - frame_means[0:1] - side_half(standard) * frame_means[1:2])
    ).astype(bf16)
    stream_grad = lax.dynamic_slice_in_dim(stream_half, (me % line) * rows, rows)
    context_pair_grad = jnp.dot(out_half, stream_half, preferred_element_type=f32)
    context_grad = (
        context_pair_grad[:rows] + across(context_pair_grad[rows:].astype(bf16)).astype(f32)
    ).astype(bf16)

    out_part = contract_last(context_pair, stream_half)
    out_sides = jnp.concatenate(
        [
            jnp.where(side == 0, out_part[:rows], out_part[rows:]),
            jnp.where(side == 0, out_part[rows:], out_part[:rows]),
        ]
    ).reshape(parts, 2 * rows // parts, width // 2)
    tap_lanes = jnp.pad(kernel_part, ((0, 0), (0, 32 - taps)))
    tap_lanes = tap_lanes.reshape(parts, 2 * rows // parts, 16)
    late = jnp.pad(
        jnp.concatenate([out_sides, tap_lanes], axis=2), ((0, 0), (0, 0), (0, 112))
    ).astype(bf16)
    late, early, branch = lax.optimization_barrier((late, early, branch))
    output = (hidden.astype(f32) + branch).astype(bf16)
    early = jnp.sum(early.astype(f32), axis=0).astype(bf16)
    for bit in (parts // 2, 1):
        early = joined(early, swap_bit(early, bit), bit)
    early = early.astype(f32).reshape(3, rows, width)
    piece = jnp.sum(exchange(late, "seq").astype(f32), axis=0).astype(bf16)
    stays = (lax.axis_index("seq") // (parts // 2)) == side
    moves = [
        (h * parts + s, (h + line) % heads * parts + (s + parts // 2) % parts)
        for h in range(heads)
        for s in range(parts)
        if s // (parts // 2) != h // line
    ]
    moved = lax.ppermute(piece, ("head", "seq"), moves)
    out_lanes = lax.broadcasted_iota(jnp.int32, piece.shape, 1) < width // 2
    piece = jnp.where(out_lanes & ~stays, moved, piece)
    late = gather(piece, "seq")
    out_weight_grad = (
        jnp.swapaxes(late[:, :, : width // 2].reshape(2, rows, width // 2), 0, 1)
        .reshape(rows, width)
        .astype(f32)
    )
    kernel_grad = late[:, :, width // 2 : width // 2 + 16].reshape(rows, 32)[:, :taps].astype(f32)
    return (
        output,
        stream_grad,
        context_grad,
        out_weight_grad,
        early[1:],
        kernel_grad,
        gain_total,
        bias_total,
        early[0],
    )


def solution(mesh):
    return jax.shard_map(
        on_device,
        mesh=mesh,
        in_specs=(
            P("head", "seq"),
            P("head", "seq"),
            P("head", None),
            P(),
            P(),
            P(None, "head", None),
            P("head", None),
            P("head"),
            P("head"),
            P("head", None),
            P("head", "seq"),
        ),
        out_specs=(
            P("head", "seq"),
            P("head", "seq"),
            P("head", "seq"),
            P("head", None),
            P(None, "head", None),
            P("head", None),
            P("head"),
            P("head"),
            P("head", None),
        ),
        check_vma=False,
    )
```

time: 446 us -> 324 us (0.73)
  blocking collectives: 107 us -> 0 us
  waiting for transfers between devices: 201 us -> 117 us
  starting transfers between devices: 57.3 us -> 109 us
  Pallas kernels: 0 us -> 21.4 us
    all_to_all x3 -> x0, blocking collectives: 107 us -> none  [exchange(): return lax.all_to_all(blocks, axis, 0, 0, tiled=True)]
    all_to_all x6 -> x5, waiting for transfers between devices: 142 us -> 63.5 us  [exchange(): return lax.all_to_all(blocks, axis, 0, 0, tiled=True)]
    all_gather x1 -> x2, waiting for transfers between devices: 57.1 us -> 0.02 us  [the longest x1 0.02 us: on_device(): lax.all_gather(grad_pair, 'head', axis=1, tiled=False, axis_index_groups=...]
    ppermute x0 -> x13, starting transfers between devices: none -> 41.3 us  [the longest x8 27.6 us: across(): lax.ppermute(operand, 'head', [(i, (i + count // 2) % count) for i in ran...]
    all_to_all x0 -> x3, waiting for transfers between devices: none -> 37.8 us  [the longest x2 37.8 us: line_exchange(): lax.all_to_all(blocks, 'head', 0, 0, tiled=True, axis_index_groups=line_g...]
    pallas_call x0 -> x2, Pallas kernels: none -> 21.4 us  [the longest x1 16.7 us: taps_grad(): pl.pallas_call(functools.partial(taps_grad_kernel, taps=taps, frames=fram...]
    all_to_all x0 -> x3, starting transfers between devices: none -> 17.8 us  [the longest x2 13.3 us: line_exchange(): lax.all_to_all(blocks, 'head', 0, 0, tiled=True, axis_index_groups=line_g...]
    ppermute x0 -> x13, waiting for transfers between devices: none -> 15.9 us  [the longest x8 11.9 us: across(): lax.ppermute(operand, 'head', [(i, (i + count // 2) % count) for i in ran...]
  transfers between devices with their start and end apart: 11 -> 28, of which waited for: 7 -> 10; matrix products, arithmetic and copies ran while one was open for 4% -> 14% of each run, Pallas kernels for 0% -> 7%
where the time goes in v2:
time: 324 us; the launch traced here: 321 us
  waiting for transfers between devices  117 us (36%)
  starting transfers between devices  109 us (34%)
  other arithmetic  23.2 us (7%)
  local copies, waits for them, and re-layouts  22.8 us (7%)
  Pallas kernels  21.4 us (7%)
  between operations  14.8 us (5%)
  matrix products  12.7 us (4%)
    all_to_all x5, waiting for transfers between devices, exchange(): return lax.all_to_all(blocks, axis, 0, 0, tiled=True)  63.5 us
    all_to_all x2, waiting for transfers between devices, line_exchange(): lax.all_to_all(blocks, 'head', 0, 0, tiled=True, axis_index_groups=line_g...  37.8 us
    all_to_all x5, starting transfers between devices, exchange(): return lax.all_to_all(blocks, axis, 0, 0, tiled=True)  33.1 us
    ppermute x8, starting transfers between devices, across(): lax.ppermute(operand, 'head', [(i, (i + count // 2) % count) for i in ran...  27.6 us
    pallas_call x1, Pallas kernels, taps_grad(): pl.pallas_call(functools.partial(taps_grad_kernel, taps=taps, frames=fram...  16.7 us
    all_to_all x2, starting transfers between devices, line_exchange(): lax.all_to_all(blocks, 'head', 0, 0, tiled=True, axis_index_groups=line_g...  13.3 us
    ppermute x4, starting transfers between devices, swap_bit(): return lax.ppermute(operand, 'seq', [(i, i ^ bit) for i in range(count)])  13 us
    ppermute x8, waiting for transfers between devices, across(): lax.ppermute(operand, 'head', [(i, (i + count // 2) % count) for i in ran...  11.9 us
  transfers between devices with their start and end apart: 28, of which 10 were waited for; matrix products, arithmetic and copies ran while one was open for 14% of the time, Pallas kernels for 7%

profile of v2, /device:TPU:1, one launch (start us, length us, event | category | flops | bytes accessed | tf_op | source)
XLA Modules:
  0.0 321.4 jit_solution(930386170302936254)
XLA Ops:
  7.2 5.5 %collective-permute-start.1 = (bf16[96,448]{1,0:T(8,128)(2,1)}, bf16[96,448]{1,0:T(8,128)(2,1)S(1)}, u32[]{:S(2)}, u32[]{:S(2)}) collective-permute-start(bf16[96,448]{1,0:T(8,128)(2,1)} %param.11), channel_id=1, source_target_pairs={{0,256},{32,288},{64,320},{96,352},{128,384},{160,416},{192,448},{... | collective-permute-start | bytes 258056 | tf_op jit(solution)/shard_map/ppermute | solution.py:44
  16.6 5.4 %collective-permute-done = bf16[96,768]{1,0:T(8,128)(2,1)S(1)} collective-permute-done((bf16[96,768]{1,0:T(8,128)(2,1)S(1)}, bf16[96,768]{1,0:T(8,128)(2,1)S(1)}, u32[]{:S(2)}, u32[]{:S(2)}) %collective-permute-start) | collective-permute-done | bytes 147488 | tf_op jit(solution)/shard_map/ppermute | solution.py:44
  24.2 9.7 %all-to-all-start = ((bf16[8,96,448]{2,1,0:T(8,128)(2,1)}), bf16[8,96,448]{2,1,0:T(8,128)(2,1)S(1)}, u32[]{:S(2)}, u32[]{:S(2)}) async-start(bf16[8,96,448]{2,1,0:T(8,128)(2,1)} %bitcast), calls=%async_computation | async-start | bytes 1572864 | tf_op jit(solution)/shard_map/all_to_all | solution.py:182
  36.1 19.6 %all-to-all-done = bf16[8,96,448]{2,1,0:T(8,128)(2,1)S(1)} async-done(((bf16[8,96,448]{2,1,0:T(8,128)(2,1)}), bf16[8,96,448]{2,1,0:T(8,128)(2,1)S(1)}, u32[]{:S(2)}, u32[]{:S(2)}) %all-to-all-start) | async-done | bytes 688160 | tf_op jit(solution)/shard_map/all_to_all | solution.py:182
  57.8 3.9 %all-to-all-start.1 = ((bf16[16,96,448]{2,1,0:T(8,128)(2,1)}), bf16[16,96,448]{2,1,0:T(8,128)(2,1)S(1)}, u32[]{:S(2)}, u32[]{:S(2)}) async-start(bf16[16,96,448]{2,1,0:T(8,128)(2,1)} %broadcast_in_dim.18), calls=%async_computation.1 | async-start | bytes 3145728 | tf_op jit(solution)/shard_map/all_to_all | solution.py:28
  62.6 4.7 %collective-permute-start.5 = (bf16[192,768]{1,0:T(8,128)(2,1)}, bf16[192,768]{1,0:T(8,128)(2,1)}, u32[]{:S(2)}, u32[]{:S(2)}) collective-permute-start(bf16[192,768]{1,0:T(8,128)(2,1)} %get-tuple-element.91), channel_id=1, source_target_pairs={{0,256},{32,288},{64,320},{96,352},{128,384},{160,416},{192,448},{... | collective-permute-start | bytes 884744 | tf_op jit(solution)/shard_map/ppermute | solution.py:44
  69.9 32.1 %all-to-all-done.1 = bf16[16,96,448]{2,1,0:T(8,128)(2,1)S(1)} async-done(((bf16[16,96,448]{2,1,0:T(8,128)(2,1)}), bf16[16,96,448]{2,1,0:T(8,128)(2,1)S(1)}, u32[]{:S(2)}, u32[]{:S(2)}) %all-to-all-start.1) | async-done | bytes 1376288 | tf_op jit(solution)/shard_map/all_to_all | solution.py:28
  105.6 8.0 %collective-permute-start.4 = (bf16[96,30]{1,0:T(8,128)(2,1)S(1)}, bf16[96,30]{1,0:T(8,128)(2,1)S(1)}, u32[]{:S(2)}, u32[]{:S(2)}) collective-permute-start(bf16[96,30]{1,0:T(8,128)(2,1)S(1)} %get-tuple-element.103), channel_id=1, source_target_pairs={{1,0},{2,1},{3,2},{4,3},{5,4},{6,5},{7,6},{8,7},{9,8},{10,9},{11,1... | collective-permute-start | bytes 17288 | tf_op jit(solution)/shard_map/ppermute | solution.py:144
  113.7 3.1 collective-permute-start.3
  124.0 6.7 %all-to-all-start.2 = ((f32[32,2,96]{2,1,0:T(2,128)}), f32[32,2,96]{2,1,0:T(2,128)S(1)}, u32[]{:S(2)}, u32[]{:S(2)}) async-start(f32[32,2,96]{2,1,0:T(2,128)} %broadcast_in_dim.20), calls=%async_computation.2 | async-start | bytes 65536 | tf_op jit(solution)/shard_map/all_to_all | solution.py:28
  133.4 5.3 %all-to-all-done.2 = f32[32,2,96]{2,1,0:T(2,128)S(1)} async-done(((f32[32,2,96]{2,1,0:T(2,128)}), f32[32,2,96]{2,1,0:T(2,128)S(1)}, u32[]{:S(2)}, u32[]{:S(2)}) %all-to-all-start.2) | async-done | bytes 24608 | tf_op jit(solution)/shard_map/all_to_all | solution.py:28
  143.7 4.4 %all-to-all-start.3 = ((f32[32,2,96]{2,1,0:T(2,128)}), f32[32,2,96]{2,1,0:T(2,128)S(1)}, u32[]{:S(2)}, u32[]{:S(2)}) async-start(f32[32,2,96]{2,1,0:T(2,128)} %broadcast_in_dim.21), calls=%async_computation.3 | async-start | bytes 65536 | tf_op jit(solution)/shard_map/all_to_all | solution.py:28
  149.1 2.2 collective-permute-start.7
  151.4 3.4 %collective-permute-start.6 = (f32[96,15]{1,0:T(8,128)S(1)}, f32[96,15]{1,0:T(8,128)S(1)}, u32[]{:S(2)}, u32[]{:S(2)}) collective-permute-start(f32[96,15]{1,0:T(8,128)S(1)} %get-tuple-element.98), channel_id=1, source_target_pairs={{0,1},{1,2},{2,3},{3,4},{4,5},{5,6},{6,7},{7,8},{8,9},{9,10},{10,1... | collective-permute-start | bytes 17288 | tf_op jit(solution)/shard_map/ppermute | solution.py:143
  154.9 2.9 convolution_convert_fusion
  159.5 4.7 %conv_back.1 = (bf16[2,96,448]{2,1,0:T(8,128)(2,1)}, f32[96,512]{1,0:T(8,128)}) custom-call(f32[96,6]{1,0:T(8,128)} %copy.81.consts_ref, f32[96,31]{1,0:T(8,128)} %copy.82.taps_ref, f32[1,512]{1,0:T(1,128)} %and_convert_fusion.inside_ref, f32[96,512]{1,0:T(8,128)} %maximum_maximum_fusion.swish_ref, f32[96,512]{1,0:T(8,128)} %pad.17.conv_ref, ...), custom_call_target="tpu_custom_call" | custom-call | tf_op jit(solution)/shard_map/conv_back/pallas_call | solution.py:121
  165.9 4.0 %collective-permute-start.8 = (bf16[192,448]{1,0:T(8,128)(2,1)S(1)}, bf16[192,448]{1,0:T(8,128)(2,1)S(1)}, u32[]{:S(2)}, u32[]{:S(2)}) collective-permute-start(bf16[192,448]{1,0:T(8,128)(2,1)S(1)} %bitcast.164), channel_id=1, source_target_pairs={{0,256},{32,288},{64,320},{96,352},{128,384},{160,416},{192,448},{... | collective-permute-start | bytes 516104 | tf_op jit(solution)/shard_map/ppermute | solution.py:44
  173.2 2.5 collective-permute-done.8
  177.6 3.6 %all-to-all-start.4 = ((bf16[8,112,448]{2,1,0:T(8,128)(2,1)}), bf16[8,112,448]{2,1,0:T(8,128)(2,1)S(1)}, u32[]{:S(2)}, u32[]{:S(2)}) async-start(bf16[8,112,448]{2,1,0:T(8,128)(2,1)} %pad_maximum_fusion.1), calls=%async_computation.4 | async-start | bytes 1835008 | tf_op jit(solution)/shard_map/all_to_all | solution.py:182
  183.3 4.6 %collective-permute-start.10 = (bf16[72,1536]{1,0:T(8,128)(2,1)S(1)}, bf16[72,1536]{1,0:T(8,128)(2,1)S(1)}, u32[]{:S(2)}, u32[]{:S(2)}) collective-permute-start(bf16[72,1536]{1,0:T(8,128)(2,1)S(1)} %dynamic-slice_convert_fusion.1), channel_id=1, source_target_pairs={{0,16},{1,17},{2,18},{3,19},{4,20},{5,21},{6,22},{7,23},{8,24},{9,... | collective-permute-start | bytes 663560 | tf_op jit(solution)/shard_map/ppermute | solution.py:49
  187.9 3.9 %collective-permute-done.10 = bf16[72,1536]{1,0:T(8,128)(2,1)S(1)} collective-permute-done((bf16[72,1536]{1,0:T(8,128)(2,1)S(1)}, bf16[72,1536]{1,0:T(8,128)(2,1)S(1)}, u32[]{:S(2)}, u32[]{:S(2)}) %collective-permute-start.10) | collective-permute-done | bytes 221216 | tf_op jit(solution)/shard_map/ppermute | solution.py:49
  193.6 18.1 %all-to-all-done.4 = bf16[8,112,448]{2,1,0:T(8,128)(2,1)S(1)} async-done(((bf16[8,112,448]{2,1,0:T(8,128)(2,1)}), bf16[8,112,448]{2,1,0:T(8,128)(2,1)S(1)}, u32[]{:S(2)}, u32[]{:S(2)}) %all-to-all-start.4) | async-done | bytes 802848 | tf_op jit(solution)/shard_map/all_to_all | solution.py:182
  212.9 4.5 %all-to-all-start.5 = ((bf16[8,96,448]{2,1,0:T(8,128)(2,1)}), bf16[8,96,448]{2,1,0:T(8,128)(2,1)S(1)}, u32[]{:S(2)}, u32[]{:S(2)}) async-start(bf16[8,96,448]{2,1,0:T(8,128)(2,1)} %broadcast_in_dim.25), calls=%async_computation.6 | async-start | bytes 1572864 | tf_op jit(solution)/shard_map/all_to_all | solution.py:193
  218.7 16.7 %taps_grad.1 = f32[96,128]{1,0:T(8,128)} custom-call(f32[96,512]{1,0:T(8,128)} %get-tuple-element.31.grad_ref, f32[96,512]{1,0:T(8,128)} %copy-done), custom_call_target="tpu_custom_call" | custom-call | tf_op jit(solution)/shard_map/taps_grad/pallas_call | solution.py:132
  236.3 4.6 %collective-permute-start.11 = (f32[2,448]{1,0:T(2,128)S(1)}, f32[2,448]{1,0:T(2,128)S(1)}, u32[]{:S(2)}, u32[]{:S(2)}) collective-permute-start(f32[2,448]{1,0:T(2,128)S(1)} %slice.346), channel_id=1, source_target_pairs={{0,256},{32,288},{64,320},{96,352},{128,384},{160,416},{192,448},{... | collective-permute-start | bytes 10760 | tf_op jit(solution)/shard_map/ppermute | solution.py:44
  243.8 4.1 %collective-permute-done.12 = bf16[96,448]{1,0:T(8,128)(2,1)S(1)} collective-permute-done((bf16[96,448]{1,0:T(8,128)(2,1)S(1)}, bf16[96,448]{1,0:T(8,128)(2,1)S(1)}, u32[]{:S(2)}, u32[]{:S(2)}) %collective-permute-start.12) | collective-permute-done | bytes 86048 | tf_op jit(solution)/shard_map/ppermute | solution.py:44
  251.2 2.6 collective-permute-start.13
  257.1 4.1 %collective-permute-start.15 = (bf16[72,1536]{1,0:T(8,128)(2,1)S(1)}, bf16[72,1536]{1,0:T(8,128)(2,1)S(1)}, u32[]{:S(2)}, u32[]{:S(2)}) collective-permute-start(bf16[72,1536]{1,0:T(8,128)(2,1)S(1)} %reduce_sum.175), channel_id=1, source_target_pairs={{0,16},{1,17},{2,18},{3,19},{4,20},{5,21},{6,22},{7,23},{8,24},{9,... | collective-permute-start | bytes 663560 | tf_op jit(solution)/shard_map/ppermute | solution.py:49
  261.9 9.4 %all-to-all-start.6 = ((bf16[32,6,896]{2,1,0:T(8,128)(2,1)}), bf16[32,6,896]{2,1,0:T(8,128)(2,1)S(1)}, u32[]{:S(2)}, u32[]{:S(2)}) async-start(bf16[32,6,896]{2,1,0:T(8,128)(2,1)} %fusion.9), calls=%async_computation.7 | async-start | bytes 917504 | tf_op jit(solution)/shard_map/all_to_all | solution.py:28
  273.6 13.1 %all-to-all-done.6 = bf16[32,6,896]{2,1,0:T(8,128)(2,1)S(1)} async-done(((bf16[32,6,896]{2,1,0:T(8,128)(2,1)}), bf16[32,6,896]{2,1,0:T(8,128)(2,1)S(1)}, u32[]{:S(2)}, u32[]{:S(2)}) %all-to-all-start.6) | async-done | bytes 344096 | tf_op jit(solution)/shard_map/all_to_all | solution.py:28
  289.0 8.7 %all-to-all-start.7 = ((bf16[32,6,896]{2,1,0:T(8,128)(2,1)}), bf16[32,6,896]{2,1,0:T(8,128)(2,1)S(1)}, u32[]{:S(2)}, u32[]{:S(2)}) async-start(bf16[32,6,896]{2,1,0:T(8,128)(2,1)} %broadcast_in_dim.26), calls=%async_computation.8 | async-start | bytes 917504 | tf_op jit(solution)/shard_map/all_to_all | solution.py:28
  300.0 13.0 %all-to-all-done.7 = bf16[32,6,896]{2,1,0:T(8,128)(2,1)S(1)} async-done(((bf16[32,6,896]{2,1,0:T(8,128)(2,1)}), bf16[32,6,896]{2,1,0:T(8,128)(2,1)S(1)}, u32[]{:S(2)}, u32[]{:S(2)}) %all-to-all-start.7) | async-done | bytes 344096 | tf_op jit(solution)/shard_map/all_to_all | solution.py:28
  (217 shorter events, 67.3 us)
Async XLA Ops:
  7.2 9.4 %collective-permute-start.1 = (bf16[96,448]{1,0:T(8,128)(2,1)}, bf16[96,448]{1,0:T(8,128)(2,1)S(1)}, u32[]{:S(2)}, u32[]{:S(2)}) collective-permute-start(bf16[96,448]{1,0:T(8,128)(2,1)} %param.11), channel_id=1, source_target_pairs={{0,256},{32,288},{64,320},{96,352},{128,384},{160,416},{192,448},{... | collective-permute-start | bytes 258056 | tf_op jit(solution)/shard_map/ppermute | solution.py:44
  13.7 8.2 %collective-permute-start = (bf16[96,768]{1,0:T(8,128)(2,1)S(1)}, bf16[96,768]{1,0:T(8,128)(2,1)S(1)}, u32[]{:S(2)}, u32[]{:S(2)}) collective-permute-start(bf16[96,768]{1,0:T(8,128)(2,1)S(1)} %get-tuple-element.97), channel_id=1, source_target_pairs={{0,256},{32,288},{64,320},{96,352},{128,384},{160,416},{192,448},{... | collective-permute-start | bytes 442376 | tf_op jit(solution)/shard_map/ppermute | solution.py:44
  24.2 31.6 %copy-start.20 = (bf16[96,448]{1,0:T(8,128)(2,1)S(1)}, bf16[96,448]{1,0:T(8,128)(2,1)}, u32[]{:S(2)}) copy-start(bf16[96,448]{1,0:T(8,128)(2,1)} %param.12) | copy-start | bytes 258052
  24.2 31.5 %all-to-all-start = ((bf16[8,96,448]{2,1,0:T(8,128)(2,1)}), bf16[8,96,448]{2,1,0:T(8,128)(2,1)S(1)}, u32[]{:S(2)}, u32[]{:S(2)}) async-start(bf16[8,96,448]{2,1,0:T(8,128)(2,1)} %bitcast), calls=%async_computation | async-start | bytes 1572864 | tf_op jit(solution)/shard_map/all_to_all | solution.py:182
  33.9 22.0 %collective-permute-start.2 = (bf16[96,448]{1,0:T(8,128)(2,1)S(1)}, bf16[96,448]{1,0:T(8,128)(2,1)S(1)}, u32[]{:S(2)}, u32[]{:S(2)}) collective-permute-start(bf16[96,448]{1,0:T(8,128)(2,1)S(1)} %copy-done.21), channel_id=1, source_target_pairs={{0,256},{32,288},{64,320},{96,352},{128,384},{160,416},{192,448},{... | collective-permute-start | bytes 258056 | tf_op jit(solution)/shard_map/ppermute | solution.py:44
  57.8 44.2 %all-to-all-start.1 = ((bf16[16,96,448]{2,1,0:T(8,128)(2,1)}), bf16[16,96,448]{2,1,0:T(8,128)(2,1)S(1)}, u32[]{:S(2)}, u32[]{:S(2)}) async-start(bf16[16,96,448]{2,1,0:T(8,128)(2,1)} %broadcast_in_dim.18), calls=%async_computation.1 | async-start | bytes 3145728 | tf_op jit(solution)/shard_map/all_to_all | solution.py:28
  61.7 61.7 %all-gather.5.cloned.1.call-start = ((), (), s32[]{:S(2)}) async-start(), calls=%async_computation.10 | async-start | bytes 1769472 | tf_op jit(solution)/shard_map/all_gather | solution.py:226
  62.6 68.1 %collective-permute-start.5 = (bf16[192,768]{1,0:T(8,128)(2,1)}, bf16[192,768]{1,0:T(8,128)(2,1)}, u32[]{:S(2)}, u32[]{:S(2)}) collective-permute-start(bf16[192,768]{1,0:T(8,128)(2,1)} %get-tuple-element.91), channel_id=1, source_target_pairs={{0,256},{32,288},{64,320},{96,352},{128,384},{160,416},{192,448},{... | collective-permute-start | bytes 884744 | tf_op jit(solution)/shard_map/ppermute | solution.py:44
  105.6 15.0 %collective-permute-start.4 = (bf16[96,30]{1,0:T(8,128)(2,1)S(1)}, bf16[96,30]{1,0:T(8,128)(2,1)S(1)}, u32[]{:S(2)}, u32[]{:S(2)}) collective-permute-start(bf16[96,30]{1,0:T(8,128)(2,1)S(1)} %get-tuple-element.103), channel_id=1, source_target_pairs={{1,0},{2,1},{3,2},{4,3},{5,4},{6,5},{7,6},{8,7},{9,8},{10,9},{11,1... | collective-permute-start | bytes 17288 | tf_op jit(solution)/shard_map/ppermute | solution.py:144
  113.7 6.9 %collective-permute-start.3 = (bf16[96,30]{1,0:T(8,128)(2,1)S(1)}, bf16[96,30]{1,0:T(8,128)(2,1)S(1)}, u32[]{:S(2)}, u32[]{:S(2)}) collective-permute-start(bf16[96,30]{1,0:T(8,128)(2,1)S(1)} %get-tuple-element.102), channel_id=1, source_target_pairs={{0,1},{1,2},{2,3},{3,4},{4,5},{5,6},{6,7},{7,8},{8,9},{9,10},{10,1... | collective-permute-start | bytes 17288 | tf_op jit(solution)/shard_map/ppermute | solution.py:143
  124.0 14.6 %all-to-all-start.2 = ((f32[32,2,96]{2,1,0:T(2,128)}), f32[32,2,96]{2,1,0:T(2,128)S(1)}, u32[]{:S(2)}, u32[]{:S(2)}) async-start(f32[32,2,96]{2,1,0:T(2,128)} %broadcast_in_dim.20), calls=%async_computation.2 | async-start | bytes 65536 | tf_op jit(solution)/shard_map/all_to_all | solution.py:28
  143.7 14.9 %all-to-all-start.3 = ((f32[32,2,96]{2,1,0:T(2,128)}), f32[32,2,96]{2,1,0:T(2,128)S(1)}, u32[]{:S(2)}, u32[]{:S(2)}) async-start(f32[32,2,96]{2,1,0:T(2,128)} %broadcast_in_dim.21), calls=%async_computation.3 | async-start | bytes 65536 | tf_op jit(solution)/shard_map/all_to_all | solution.py:28
  148.2 63.7 %reduce-scatter.2.cloned.1.call-start = ((), (), s32[]{:S(2)}) async-start(), calls=%async_computation.9 | async-start | bytes 1769472 | tf_op jit(solution)/shard_map/reduce_scatter | solution.py:294
  149.1 8.6 %collective-permute-start.7 = (f32[96,15]{1,0:T(8,128)S(1)}, f32[96,15]{1,0:T(8,128)S(1)}, u32[]{:S(2)}, u32[]{:S(2)}) collective-permute-start(f32[96,15]{1,0:T(8,128)S(1)} %get-tuple-element.99), channel_id=1, source_target_pairs={{1,0},{2,1},{3,2},{4,3},{5,4},{6,5},{7,6},{8,7},{9,8},{10,9},{11,1... | collective-permute-start | bytes 17288 | tf_op jit(solution)/shard_map/ppermute | solution.py:144
  151.4 6.4 %collective-permute-start.6 = (f32[96,15]{1,0:T(8,128)S(1)}, f32[96,15]{1,0:T(8,128)S(1)}, u32[]{:S(2)}, u32[]{:S(2)}) collective-permute-start(f32[96,15]{1,0:T(8,128)S(1)} %get-tuple-element.98), channel_id=1, source_target_pairs={{0,1},{1,2},{2,3},{3,4},{4,5},{5,6},{6,7},{7,8},{8,9},{9,10},{10,1... | collective-permute-start | bytes 17288 | tf_op jit(solution)/shard_map/ppermute | solution.py:143
  165.9 9.8 %collective-permute-start.8 = (bf16[192,448]{1,0:T(8,128)(2,1)S(1)}, bf16[192,448]{1,0:T(8,128)(2,1)S(1)}, u32[]{:S(2)}, u32[]{:S(2)}) collective-permute-start(bf16[192,448]{1,0:T(8,128)(2,1)S(1)} %bitcast.164), channel_id=1, source_target_pairs={{0,256},{32,288},{64,320},{96,352},{128,384},{160,416},{192,448},{... | collective-permute-start | bytes 516104 | tf_op jit(solution)/shard_map/ppermute | solution.py:44
  171.0 10.2 %collective-permute-start.9 = (bf16[144,1536]{1,0:T(8,128)(2,1)}, bf16[144,1536]{1,0:T(8,128)(2,1)}, u32[]{:S(2)}, u32[]{:S(2)}) collective-permute-start(bf16[144,1536]{1,0:T(8,128)(2,1)} %dynamic-slice_convert_fusion), channel_id=1, source_target_pairs={{0,1},{1,0},{2,3},{3,2},{4,5},{5,4},{6,7},{7,6},{8,9},{9,8},{10,11... | collective-permute-start | bytes 1327112 | tf_op jit(solution)/shard_map/ppermute | solution.py:49
  177.6 34.1 %all-to-all-start.4 = ((bf16[8,112,448]{2,1,0:T(8,128)(2,1)}), bf16[8,112,448]{2,1,0:T(8,128)(2,1)S(1)}, u32[]{:S(2)}, u32[]{:S(2)}) async-start(bf16[8,112,448]{2,1,0:T(8,128)(2,1)} %pad_maximum_fusion.1), calls=%async_computation.4 | async-start | bytes 1835008 | tf_op jit(solution)/shard_map/all_to_all | solution.py:182
  181.1 74.2 %all-gather.7.cloned.1.call-start = ((), (), s32[]{:S(2)}) async-start(), calls=%async_computation.11 | async-start | bytes 1990656 | tf_op jit(solution)/shard_map/all_gather | solution.py:336
  183.3 8.5 %collective-permute-start.10 = (bf16[72,1536]{1,0:T(8,128)(2,1)S(1)}, bf16[72,1536]{1,0:T(8,128)(2,1)S(1)}, u32[]{:S(2)}, u32[]{:S(2)}) collective-permute-start(bf16[72,1536]{1,0:T(8,128)(2,1)S(1)} %dynamic-slice_convert_fusion.1), channel_id=1, source_target_pairs={{0,16},{1,17},{2,18},{3,19},{4,20},{5,21},{6,22},{7,23},{8,24},{9,... | collective-permute-start | bytes 663560 | tf_op jit(solution)/shard_map/ppermute | solution.py:49
  211.9 29.0 %copy-start.19 = (bf16[192,448]{1,0:T(8,128)(2,1)S(1)}, bf16[192,448]{1,0:T(8,128)(2,1)}, u32[]{:S(2)}) copy-start(bf16[192,448]{1,0:T(8,128)(2,1)} %reduce-scatter.2.cloned.1.call-done) | copy-start | bytes 516100
  212.9 35.0 %copy-start.6 = (bf16[2,768,448]{2,1,0:T(8,128)(2,1)S(1)}, bf16[2,768,448]{2,1,0:T(8,128)(2,1)}, u32[]{:S(2)}) copy-start(bf16[2,768,448]{2,1,0:T(8,128)(2,1)} %all-gather.5.cloned.1.call-done) | copy-start | bytes 4128772
  212.9 35.0 %all-to-all-start.5 = ((bf16[8,96,448]{2,1,0:T(8,128)(2,1)}), bf16[8,96,448]{2,1,0:T(8,128)(2,1)S(1)}, u32[]{:S(2)}, u32[]{:S(2)}) async-start(bf16[8,96,448]{2,1,0:T(8,128)(2,1)} %broadcast_in_dim.25), calls=%async_computation.6 | async-start | bytes 1572864 | tf_op jit(solution)/shard_map/all_to_all | solution.py:193
  236.3 6.8 %collective-permute-start.11 = (f32[2,448]{1,0:T(2,128)S(1)}, f32[2,448]{1,0:T(2,128)S(1)}, u32[]{:S(2)}, u32[]{:S(2)}) collective-permute-start(f32[2,448]{1,0:T(2,128)S(1)} %slice.346), channel_id=1, source_target_pairs={{0,256},{32,288},{64,320},{96,352},{128,384},{160,416},{192,448},{... | collective-permute-start | bytes 10760 | tf_op jit(solution)/shard_map/ppermute | solution.py:44
  241.0 6.9 %collective-permute-start.12 = (bf16[96,448]{1,0:T(8,128)(2,1)S(1)}, bf16[96,448]{1,0:T(8,128)(2,1)S(1)}, u32[]{:S(2)}, u32[]{:S(2)}) collective-permute-start(bf16[96,448]{1,0:T(8,128)(2,1)S(1)} %dynamic-slice_bitcast_fusion), channel_id=1, source_target_pairs={{0,256},{32,288},{64,320},{96,352},{128,384},{160,416},{192,448},{... | collective-permute-start | bytes 258056 | tf_op jit(solution)/shard_map/ppermute | solution.py:44
  251.2 10.0 %collective-permute-start.13 = (bf16[96,448]{1,0:T(8,128)(2,1)S(1)}, bf16[96,448]{1,0:T(8,128)(2,1)S(1)}, u32[]{:S(2)}, u32[]{:S(2)}) collective-permute-start(bf16[96,448]{1,0:T(8,128)(2,1)S(1)} %slice.639), channel_id=1, source_target_pairs={{0,256},{32,288},{64,320},{96,352},{128,384},{160,416},{192,448},{... | collective-permute-start | bytes 258056 | tf_op jit(solution)/shard_map/ppermute | solution.py:44
  257.1 14.3 %collective-permute-start.15 = (bf16[72,1536]{1,0:T(8,128)(2,1)S(1)}, bf16[72,1536]{1,0:T(8,128)(2,1)S(1)}, u32[]{:S(2)}, u32[]{:S(2)}) collective-permute-start(bf16[72,1536]{1,0:T(8,128)(2,1)S(1)} %reduce_sum.175), channel_id=1, source_target_pairs={{0,16},{1,17},{2,18},{3,19},{4,20},{5,21},{6,22},{7,23},{8,24},{9,... | collective-permute-start | bytes 663560 | tf_op jit(solution)/shard_map/ppermute | solution.py:49
  261.9 26.3 %copy-start.34 = (pred[896]{0:T(1024)(128)(4,1)S(1)}, pred[896]{0:T(1024)(128)(4,1)}, u32[]{:S(2)}) copy-start(pred[896]{0:T(1024)(128)(4,1)} %fusion.57) | copy-start | bytes 2692
  261.9 24.8 %all-to-all-start.6 = ((bf16[32,6,896]{2,1,0:T(8,128)(2,1)}), bf16[32,6,896]{2,1,0:T(8,128)(2,1)S(1)}, u32[]{:S(2)}, u32[]{:S(2)}) async-start(bf16[32,6,896]{2,1,0:T(8,128)(2,1)} %fusion.9), calls=%async_computation.7 | async-start | bytes 917504 | tf_op jit(solution)/shard_map/all_to_all | solution.py:28
  271.4 26.2 %collective-permute-start.16 = (bf16[144,1536]{1,0:T(8,128)(2,1)S(1)}, bf16[144,1536]{1,0:T(8,128)(2,1)S(1)}, u32[]{:S(2)}, u32[]{:S(2)}) collective-permute-start(bf16[144,1536]{1,0:T(8,128)(2,1)S(1)} %pad_maximum_fusion.2), channel_id=1, source_target_pairs={{0,1},{1,0},{2,3},{3,2},{4,5},{5,4},{6,7},{7,6},{8,9},{9,8},{10,11... | collective-permute-start | bytes 1327112 | tf_op jit(solution)/shard_map/ppermute | solution.py:49
  286.8 1.3 collective-permute-start.14
  289.0 24.0 %all-to-all-start.7 = ((bf16[32,6,896]{2,1,0:T(8,128)(2,1)}), bf16[32,6,896]{2,1,0:T(8,128)(2,1)S(1)}, u32[]{:S(2)}, u32[]{:S(2)}) async-start(bf16[32,6,896]{2,1,0:T(8,128)(2,1)} %broadcast_in_dim.26), calls=%async_computation.8 | async-start | bytes 917504 | tf_op jit(solution)/shard_map/all_to_all | solution.py:28
  (32 other events, 248.0 us)
Sparse Core Ops, SparseCore 0:
  70.0 47.9 all-gather.4
  157.9 47.7 reduce-scatter.1
  212.0 41.6 all-gather.6

commit v3 on v2

--- a/solution.py
+++ b/solution.py
@@ -99,22 +99,50 @@
     lax.fori_loop(0, pair_ref.shape[1] // 16, chunk, 0)
 
 
-def taps_grad_kernel(grad_ref, widened_ref, out_ref, *, taps, frames):
+def line_product_kernel(weight_ref, operand_ref, extra_ref, out_ref):
+    lines, held, _ = out_ref.shape
+    rows = weight_ref.shape[0] // lines
+    product = jnp.dot(weight_ref[...], operand_ref[...], preferred_element_type=f32).astype(bf16)
+    for index in range(lines):
+        out_ref[index, :rows, :] = product[index * rows : (index + 1) * rows]
+        out_ref[index, rows:held, :] = extra_ref[...]
+
+
+def line_product(weight, operand, extra, lines):
+    held = weight.shape[0] // lines + extra.shape[0]
+    return pl.pallas_call(
+        line_product_kernel,
+        out_shape=jax.ShapeDtypeStruct((lines, held, operand.shape[1]), bf16),
+        compiler_params=pltpu.CompilerParams(vmem_limit_bytes=32 * 1024 * 1024),
+        name="line_product",
+    )(weight, operand, extra)
+
+
+def taps_grad_kernel(grad_ref, widened_ref, out_ref, lane_sums, *, taps, frames):
     half = taps // 2
-    column = lax.broadcasted_iota(jnp.int32, (16, out_ref.shape[1]), 1)
+    rows, lanes = grad_ref.shape
+    inside = lax.broadcasted_iota(jnp.int32, (16, lanes), 1) < frames
 
     def chunk(index, carry):
-        at = pl.ds(pl.multiple_of(index * 16, 16), 16)
-        grad = shifted_left(grad_ref[at, :], half)[:, :frames]
-        widened = widened_ref[at, :]
-        out = jnp.zeros(column.shape, f32)
+        first = pl.multiple_of(index * 16, 16)
+        grad = jnp.where(inside, shifted_left(grad_ref[pl.ds(first, 16), :], half), 0.0)
+        widened = widened_ref[pl.ds(first, 16), :].astype(f32)
         for tap in range(taps):
-            near = shifted_left(widened, half + tap)[:, :frames]
-            out = jnp.where(column == tap, jnp.sum(grad * near, axis=1, keepdims=True), out)
-        out_ref[at, :] = out
+            product = grad * shifted_left(widened, half + tap)
+            total = product[:, :128]
+            for lane in range(128, lanes, 128):
+                total = total + product[:, lane : lane + 128]
+            lane_sums[pl.ds(pl.multiple_of(tap * rows + first, 16), 16), :] = total
         return carry
 
-    lax.fori_loop(0, out_ref.shape[0] // 16, chunk, 0)
+    lax.fori_loop(0, rows // 16, chunk, 0)
+    out_ref[...] = lax.dot_general(
+        jnp.ones((8, 128), f32),
+        lane_sums[...],
+        (((1,), (1,)), ((), ())),
+        preferred_element_type=f32,
+        precision=lax.Precision.HIGHEST,
+    )
 
 
 def conv_back(consts, kernel, inside, swish_wide, conv_wide, pair_out, taps):
@@ -129,21 +157,23 @@
 
 
 def taps_grad(grad_wide, widened, taps, frames):
-    return pl.pallas_call(
+    rows = grad_wide.shape[0]
+    sums = pl.pallas_call(
         functools.partial(taps_grad_kernel, taps=taps, frames=frames),
-        out_shape=jax.ShapeDtypeStruct((grad_wide.shape[0], 128), f32),
+        out_shape=jax.ShapeDtypeStruct((8, taps * rows), f32),
+        scratch_shapes=[pltpu.VMEM((taps * rows, 128), f32)],
         name="taps_grad",
     )(grad_wide, widened)
-
-
-def neighbours(operand, half_width, lanes):
+    return sums[0].reshape(taps, rows).T
+
+
+def neighbours(operand, half_width):
     count, length = lax.axis_size("seq"), operand.shape[1]
     up = [(i, (i + 1) % count) for i in range(count - 1)]
     down = [(j, i) for i, j in up]
     before = lax.ppermute(operand[:, length - half_width :], "seq", up)
     after = lax.ppermute(operand[:, :half_width], "seq", down)
-    spare = jnp.zeros((operand.shape[0], lanes - length - 2 * half_width), operand.dtype)
-    return jnp.concatenate([before, operand, after, spare], axis=1)
+    return jnp.concatenate([before, operand, after], axis=1)
 
 
 def on_device(
@@ -200,44 +230,71 @@
         )
         return blocks.reshape(line * block.shape[0], *block.shape[1:])
 
-    context_pair = jnp.concatenate([context, across(context)])
-    out_half = jnp.concatenate(own_half(out_weight))
+    out_keep = lax.dynamic_slice_in_dim(out_weight, side * (width // 2), width // 2, axis=1)
+    out_send = lax.dynamic_slice_in_dim(out_weight, (1 - side) * (width // 2), width // 2, axis=1)
+    swapped = across(jnp.concatenate([context, out_send], axis=1))
+    context_pair = jnp.concatenate([context, swapped[:, :frames]])
+    out_half = jnp.concatenate([out_keep, swapped[:, frames:]])
     attention = line_exchange(
         contract_lead(out_half, context_pair).astype(bf16).reshape(line, rows, frames)
     )
     hidden = (stream.astype(f32) + attention).astype(bf16)
 
     glu_half = jnp.concatenate(own_half(glu_weight.reshape(2 * rows, width)))
-    glu_turned, proj_turned = lax.optimization_barrier(
-        (
-            glu_half.T,
-            jnp.transpose(proj_weight.reshape(rows, 2, line, rows), (2, 1, 3, 0)).reshape(
-                width, rows
-            ),
-        )
-    )
-
-    grad_other = across(out_grad)
-    hidden, grad_other = lax.optimization_barrier((hidden, grad_other))
-    hidden_full = gather(hidden, "head").reshape(width, frames)
+    proj_half = jnp.concatenate(own_half(proj_weight))
+    glu_turned, proj_turned = lax.optimization_barrier((glu_half.T, proj_half.T))
+
+    frames_wide = frames + 2 * half
+    grad_mine = neighbours(out_grad, half)
+    grad_other = across(grad_mine)
     grad_pair = jnp.stack(
-        [jnp.where(side == 0, out_grad, grad_other), jnp.where(side == 0, grad_other, out_grad)]
-    )
+        [jnp.where(side == 0, grad_mine, grad_other), jnp.where(side == 0, grad_other, grad_mine)]
+    )
+    hidden, _ = lax.optimization_barrier((hidden, grad_pair))
     grad_lines = lax.all_gather(
         grad_pair, "head", axis=1, tiled=False, axis_index_groups=line_groups()
     )
-    wide = hidden_full.astype(f32)
-    centered = wide - jnp.mean(wide, axis=0, keepdims=True)
-    frame_rstd = lax.rsqrt(jnp.mean(centered * centered, axis=0, keepdims=True) + epsilon)
-    standard = centered * frame_rstd
-    normed = (standard * gain_col + bias_col).astype(bf16)
-
-    pair_out = jnp.einsum("jcd,dt->jct", glu_weight, normed, preferred_element_type=f32)
+
+    def side_half(array):
+        return lax.dynamic_slice_in_dim(array, side * (width // 2), width // 2)
+
+    def in_order(mine, other, axis):
+        return jnp.concatenate(
+            [jnp.where(side == 0, mine, other), jnp.where(side == 0, other, mine)], axis=axis
+        )
+
+    glu_own = glu_weight.astype(f32)
+    gain_outs = jnp.einsum("jcsd,sd->sjc", glu_own.reshape(2, rows, 2, -1), ln_gain.reshape(2, -1))
+    gain_gap = jnp.where(side == 0, gain_outs[0] - gain_outs[1], gain_outs[1] - gain_outs[0])
+    gain_out = gain_outs[0] + gain_outs[1]
+    bias_out = jnp.einsum("jcd,d->jc", glu_own, ln_bias)
+
+    hidden_half = line_gather(hidden)
+    half_float = hidden_half.astype(f32)
+    half_mean = jnp.mean(half_float, axis=0, keepdims=True)
+    half_cent = half_float - half_mean
+    half_square = jnp.sum(half_cent * half_cent, axis=0, keepdims=True)
+    half_moments = jnp.concatenate([half_mean, half_square])
+    other_moments = across(half_moments)
+    gained = (half_cent * side_half(gain_col)).astype(bf16)
+    products = jnp.dot(glu_half, gained, preferred_element_type=f32)
+    other_products = across(products[2 * rows :].astype(bf16)).astype(f32)
+    mean_gap = 0.5 * (half_moments[0:1] - other_moments[0:1])
+    frame_mean = half_moments[0:1] - mean_gap
+    frame_var = (
+        half_moments[1:2] + other_moments[1:2] + width * mean_gap * mean_gap
+    ) / width
+    frame_rstd = lax.rsqrt(frame_var + epsilon)
+    products = (products[: 2 * rows] + other_products).reshape(2, rows, frames)
+    pair_out = (
+        frame_rstd * (products + mean_gap * gain_gap[:, :, None]) + bias_out[:, :, None]
+    )
     glu_value, glu_gate = pair_out[0], pair_out[1]
     gate_sig = jax.nn.sigmoid(glu_gate)
     gated_out = (glu_value * gate_sig).astype(bf16)
-    widened = neighbours(gated_out, 2 * half, lanes).astype(f32)
-    frames_wide = frames + 2 * half
+    widened = neighbours(gated_out, 2 * half)
+    widened = jnp.pad(widened, ((0, 0), (0, lanes - widened.shape[1])))
+    widened = widened.astype(f32)
     conv_wide = depth_kernel[:, 0:1] * widened[:, 0:frames_wide]
     for tap in range(1, taps):
         conv_wide = (
@@ -252,13 +309,14 @@
     block_mean = jnp.mean(conv_out, axis=1)
     block_cent = conv_out - block_mean[:, None]
     block_square = jnp.sum(block_cent * block_cent, axis=1)
-    block, grad_lines = lax.optimization_barrier(
-        (jnp.stack([block_mean, block_square]), grad_lines)
-    )
-    moments = gather(block, "seq")
-    grad_full = grad_lines.reshape(width, frames)
-    swish_grad = jnp.dot(proj_weight, grad_full, preferred_element_type=f32)
-    swish_wide = neighbours(swish_grad, half, lanes)
+    moments = gather(jnp.stack([block_mean, block_square]), "seq")
+    moments, grad_lines = lax.optimization_barrier((moments, grad_lines))
+    grad_full = grad_lines.reshape(width, frames_wide)
+    swish_wide = jnp.dot(proj_weight, grad_full, preferred_element_type=f32)
+    swish_grad = swish_wide[:, half : half + frames]
+    swish_wide = jnp.pad(swish_wide, ((0, 0), (0, lanes - frames_wide)))
+    grad_half = lax.dynamic_index_in_dim(grad_lines, side, 0, keepdims=False)
+    grad_half = grad_half.reshape(width // 2, frames_wide)[:, half : half + frames]
     chan_mean = jnp.mean(moments[:, 0], axis=0)
     mean_gap = moments[:, 0] - chan_mean
     chan_var = (
@@ -290,15 +348,10 @@
         consts, depth_kernel, inside, swish_wide, conv_wide, pair_out, taps
     )
 
-    branch_part = jnp.dot(proj_turned, swished, preferred_element_type=f32).astype(bf16)
-    branch_sum = lax.psum_scatter(
-        branch_part, "head", scatter_dimension=0, tiled=True, axis_index_groups=line_groups()
-    ).reshape(2, rows, frames)
     pair_rows = pair_grad.reshape(2 * rows, frames)
-    pair_both = jnp.concatenate([pair_rows, across(pair_rows)])
-    normed_part = jnp.dot(glu_turned, pair_both, preferred_element_type=f32).astype(bf16)
-    bias_out = jnp.einsum("jcd,d->jc", glu_weight.astype(f32), ln_bias)
-    gain_out = jnp.einsum("jcd,d->jc", glu_weight.astype(f32), ln_gain)
+    other_rows = across(jnp.concatenate([pair_rows, swished]))
+    pair_both = jnp.concatenate([pair_rows, other_rows[: 2 * rows]])
+    swished_pair = jnp.concatenate([swished, other_rows[2 * rows :]])
     pair_float = pair_grad.astype(f32)
     frame_sums = jnp.stack(
         [
@@ -307,52 +360,48 @@
         ]
     )
     frame_sums = jnp.pad(frame_sums.astype(bf16), ((0, 14), (0, 0)))
-    normed_rows = line_exchange(
-        jnp.concatenate(
-            [
-                normed_part.reshape(line, rows, frames),
-                jnp.broadcast_to(frame_sums[None], (line, 16, frames)),
-            ],
-            axis=1,
-        )
-    )
-
-    proj_part = contract_last(swished, grad_full)
-    glu_part = jnp.einsum("jct,dt->jcd", pair_grad, normed, preferred_element_type=f32)
-    early = jnp.concatenate([proj_part[None], glu_part]).reshape(3 * rows, width)
+    normed_rows = line_exchange(line_product(glu_turned, pair_both, frame_sums, line))
+
+    standard = (half_float - frame_mean) * frame_rstd
+    normed_half = (standard * side_half(gain_col) + side_half(bias_col)).astype(bf16)
+    proj_part = contract_last(jnp.pad(swished, ((0, 0), (half, half))), grad_full)
+    glu_part = contract_last(pair_both, normed_half)
+    glu_part = jnp.concatenate([glu_part[: 2 * rows], glu_part[2 * rows :]], axis=1)
+    early = jnp.concatenate([proj_part, glu_part])
+    kernel_part = taps_grad(grad_wide, widened, taps, frames)
     for bit in (1, parts // 2):
         keep, send = halves(early, bit)
         early = keep + swap_bit(send.astype(bf16), bit).astype(f32)
-    normed_rows, early, branch_sum = lax.optimization_barrier((normed_rows, early, branch_sum))
-
-    branch_keep = lax.dynamic_index_in_dim(branch_sum, side, 0, keepdims=False)
-    branch_send = lax.dynamic_index_in_dim(branch_sum, 1 - side, 0, keepdims=False)
-    branch = branch_keep.astype(f32) + across(branch_send).astype(f32)
+    normed_rows, early = lax.optimization_barrier((normed_rows, early))
     columns = [
         [x * (parts // 2) + 2 * y + core for y in range(parts // 4)]
         for x in range(2)
         for core in range(2)
     ]
     early = lax.all_gather(early.astype(bf16), "seq", axis=0, axis_index_groups=columns)
-    kernel_part = taps_grad(grad_wide, widened, taps, frames)[:, :taps]
-
-    def side_half(array):
-        return lax.dynamic_slice_in_dim(array, side * (width // 2), width // 2)
 
     line_sums = normed_rows[rows : rows + 2]
     frame_means = (line_sums + across(line_sums)) / width
-    normed_grad = line_gather(normed_rows[:rows].astype(bf16)).astype(f32)
+    normed_grad = line_gather(normed_rows[:rows].astype(bf16))
+
+    branch_part = line_product(
+        proj_turned, swished_pair, jnp.zeros((rows, frames), bf16), line
+    ).reshape(2 * line * rows, frames)
+    normed_grad, branch_part = lax.optimization_barrier((normed_grad, branch_part))
+    branch = lax.psum_scatter(
+        branch_part, "head", scatter_dimension=0, tiled=True, axis_index_groups=line_groups()
+    )[:rows]
+    output = (hidden.astype(f32) + branch.astype(f32)).astype(bf16)
+
+    normed_grad = normed_grad.astype(f32)
     scaled = normed_grad * side_half(gain_col)
     stream_half = (
-        side_half(grad_full).astype(f32)
+        grad_half.astype(f32)
         + frame_rstd
-        * (scaled - frame_means[0:1] - side_half(standard) * frame_means[1:2])
+        * (scaled - frame_means[0:1] - standard * frame_means[1:2])
     ).astype(bf16)
     stream_grad = lax.dynamic_slice_in_dim(stream_half, (me % line) * rows, rows)
     context_pair_grad = jnp.dot(out_half, stream_half, preferred_element_type=f32)
-    context_grad = (
-        context_pair_grad[:rows] + across(context_pair_grad[rows:].astype(bf16)).astype(f32)
-    ).astype(bf16)
 
     out_part = contract_last(context_pair, stream_half)
     out_sides = jnp.concatenate(
@@ -366,13 +415,20 @@
     late = jnp.pad(
         jnp.concatenate([out_sides, tap_lanes], axis=2), ((0, 0), (0, 0), (0, 112))
     ).astype(bf16)
-    late, early, branch = lax.optimization_barrier((late, early, branch))
-    output = (hidden.astype(f32) + branch).astype(bf16)
     early = jnp.sum(early.astype(f32), axis=0).astype(bf16)
-    for bit in (parts // 2, 1):
-        early = joined(early, swap_bit(early, bit), bit)
+    early_other = across(early[:, width // 2 :])
+    seq = lax.axis_index("seq")
+    first_row = (seq % 2) * (2 * early.shape[0]) + (seq // (parts // 2)) * early.shape[0]
+    is_glu = (first_row + jnp.arange(early.shape[0]) >= rows)[:, None]
+    early = jnp.where(is_glu, in_order(early[:, : width // 2], early_other, 1), early)
+    piece = jnp.sum(exchange(late, "seq").astype(f32), axis=0).astype(bf16)
+    context_send = context_pair_grad[rows:].astype(bf16)
+    piece, early = lax.optimization_barrier((piece, early))
+    early = joined(early, swap_bit(early, parts // 2), parts // 2)
+    context_send, early = lax.optimization_barrier((context_send, early))
+    context_grad = (context_pair_grad[:rows] + across(context_send).astype(f32)).astype(bf16)
+    early = joined(early, swap_bit(early, 1), 1)
     early = early.astype(f32).reshape(3, rows, width)
-    piece = jnp.sum(exchange(late, "seq").astype(f32), axis=0).astype(bf16)
     stays = (lax.axis_index("seq") // (parts // 2)) == side
     moves = [
         (h * parts + s, (h + line) % heads * parts + (s + parts // 2) % parts)

time: 324 us -> 310 us (0.957)
  waiting for transfers between devices: 117 us -> 107 us
  starting transfers between devices: 109 us -> 118 us
  Pallas kernels: 21.4 us -> 12.7 us
  matrix products: 12.7 us -> 6.18 us
    all_to_all x5 -> x4, waiting for transfers between devices: 63.5 us -> 32.9 us  [exchange(): return lax.all_to_all(blocks, axis, 0, 0, tiled=True)]
    all_to_all x1 -> x2, waiting for transfers between devices: 0.01 us -> 24.8 us  [line_gather(): lax.all_to_all(jnp.broadcast_to(block[None], (line, *block.shape)), 'head...]
    all_to_all x2, waiting for transfers between devices: 37.8 us -> 17.3 us  [line_exchange(): lax.all_to_all(blocks, 'head', 0, 0, tiled=True, axis_index_groups=line_g...]
    ppermute x8 -> x10, starting transfers between devices: 27.6 us -> 43 us  [across(): lax.ppermute(operand, 'head', [(i, (i + count // 2) % count) for i in ran...]
    pallas_call x1, Pallas kernels: 16.7 us -> 5.08 us  [taps_grad(): pl.pallas_call(functools.partial(taps_grad_kernel, taps=taps, frames=fram...]
    all_to_all x5 -> x4, starting transfers between devices: 33.1 us -> 21.7 us  [exchange(): return lax.all_to_all(blocks, axis, 0, 0, tiled=True)]
    ppermute x2, waiting for transfers between devices: 0.01 us -> 6.68 us  [neighbours(): after = lax.ppermute(operand[:, :half_width], 'seq', down)]
    ppermute x2, starting transfers between devices: 10.3 us -> 3.84 us  [neighbours(): after = lax.ppermute(operand[:, :half_width], 'seq', down)]
  transfers between devices with their start and end apart: 28 -> 30, of which waited for: 10 -> 18; matrix products, arithmetic and copies ran while one was open for 14% -> 13% of each run, Pallas kernels for 7% -> 3%
where the time goes in v3:
time: 310 us; the launch traced here: 308 us
  starting transfers between devices  118 us (38%)
  waiting for transfers between devices  107 us (35%)
  other arithmetic  26.1 us (8%)
  local copies, waits for them, and re-layouts  22.9 us (7%)
  between operations  15.1 us (5%)
  Pallas kernels  12.7 us (4%)
  matrix products  6.18 us (2%)
    ppermute x10, starting transfers between devices, across(): lax.ppermute(operand, 'head', [(i, (i + count // 2) % count) for i in ran...  43 us
    all_to_all x4, waiting for transfers between devices, exchange(): return lax.all_to_all(blocks, axis, 0, 0, tiled=True)  32.9 us
    all_to_all x2, waiting for transfers between devices, line_gather(): lax.all_to_all(jnp.broadcast_to(block[None], (line, *block.shape)), 'head...  24.8 us
    all_to_all x4, starting transfers between devices, exchange(): return lax.all_to_all(blocks, axis, 0, 0, tiled=True)  21.7 us
    all_to_all x2, waiting for transfers between devices, line_exchange(): lax.all_to_all(blocks, 'head', 0, 0, tiled=True, axis_index_groups=line_g...  17.3 us
    all_to_all x2, starting transfers between devices, line_exchange(): lax.all_to_all(blocks, 'head', 0, 0, tiled=True, axis_index_groups=line_g...  16.4 us
    ppermute x10, waiting for transfers between devices, across(): lax.ppermute(operand, 'head', [(i, (i + count // 2) % count) for i in ran...  15.9 us
    ppermute x4, starting transfers between devices, swap_bit(): return lax.ppermute(operand, 'seq', [(i, i ^ bit) for i in range(count)])  13.9 us
  transfers between devices with their start and end apart: 30, of which 18 were waited for; matrix products, arithmetic and copies ran while one was open for 13% of the time, Pallas kernels for 3%

profile of v3, /device:TPU:1, one launch (start us, length us, event | category | flops | bytes accessed | tf_op | source)
XLA Modules:
  0.0 307.7 jit_solution(16836274807898184765)
XLA Ops:
  9.5 5.5 %collective-permute-start = (bf16[96,1216]{1,0:T(8,128)(2,1)S(1)}, bf16[96,1216]{1,0:T(8,128)(2,1)S(1)}, u32[]{:S(2)}, u32[]{:S(2)}) collective-permute-start(bf16[96,1216]{1,0:T(8,128)(2,1)S(1)} %pad_maximum_fusion.7), channel_id=1, source_target_pairs={{0,256},{32,288},{64,320},{96,352},{128,384},{160,416},{192,448},{... | collective-permute-start | bytes 700424 | tf_op jit(solution)/shard_map/ppermute | solution.py:44
  20.9 12.2 %all-to-all-start = ((bf16[8,96,448]{2,1,0:T(8,128)(2,1)}), bf16[8,96,448]{2,1,0:T(8,128)(2,1)S(1)}, u32[]{:S(2)}, u32[]{:S(2)}) async-start(bf16[8,96,448]{2,1,0:T(8,128)(2,1)} %bitcast), calls=%async_computation | async-start | bytes 1572864 | tf_op jit(solution)/shard_map/all_to_all | solution.py:212
  33.1 4.9 %collective-permute-start.1 = (bf16[96,15]{1,0:T(8,128)(2,1)S(1)}, bf16[96,15]{1,0:T(8,128)(2,1)S(1)}, u32[]{:S(2)}, u32[]{:S(2)}) collective-permute-start(bf16[96,15]{1,0:T(8,128)(2,1)S(1)} %get-tuple-element.112), channel_id=1, source_target_pairs={{0,1},{1,2},{2,3},{3,4},{4,5},{5,6},{6,7},{7,8},{8,9},{9,10},{10,1... | collective-permute-start | bytes 8648 | tf_op jit(solution)/shard_map/ppermute | solution.py:174
  43.6 4.7 %collective-permute-start.3 = (bf16[96,478]{1,0:T(8,128)(2,1)S(1)}, bf16[96,478]{1,0:T(8,128)(2,1)S(1)}, u32[]{:S(2)}, u32[]{:S(2)}) collective-permute-start(bf16[96,478]{1,0:T(8,128)(2,1)S(1)} %pad_maximum_fusion.15), channel_id=1, source_target_pairs={{0,256},{32,288},{64,320},{96,352},{128,384},{160,416},{192,448},{... | collective-permute-start | bytes 275336 | tf_op jit(solution)/shard_map/ppermute | solution.py:44
  51.3 4.2 %all-to-all-done = bf16[8,96,448]{2,1,0:T(8,128)(2,1)S(1)} async-done(((bf16[8,96,448]{2,1,0:T(8,128)(2,1)}), bf16[8,96,448]{2,1,0:T(8,128)(2,1)S(1)}, u32[]{:S(2)}, u32[]{:S(2)}) %all-to-all-start) | async-done | bytes 688160 | tf_op jit(solution)/shard_map/all_to_all | solution.py:212
  56.6 3.7 %all-to-all-start.1 = ((bf16[8,96,448]{2,1,0:T(8,128)(2,1)}), bf16[8,96,448]{2,1,0:T(8,128)(2,1)S(1)}, u32[]{:S(2)}, u32[]{:S(2)}) async-start(bf16[8,96,448]{2,1,0:T(8,128)(2,1)} %broadcast_in_dim.19), calls=%async_computation.1 | async-start | bytes 1572864 | tf_op jit(solution)/shard_map/all_to_all | solution.py:223
  61.1 4.6 %collective-permute-start.5 = (bf16[96,768]{0,1:T(8,128)(2,1)}, bf16[96,768]{0,1:T(8,128)(2,1)}, u32[]{:S(2)}, u32[]{:S(2)}) collective-permute-start(bf16[96,768]{0,1:T(8,128)(2,1)} %copy.106), channel_id=1, source_target_pairs={{0,256},{32,288},{64,320},{96,352},{128,384},{160,416},{192,448},{... | collective-permute-start | bytes 442376 | tf_op jit(solution)/shard_map/ppermute | solution.py:44
  68.8 15.0 %all-to-all-done.1 = bf16[8,96,448]{2,1,0:T(8,128)(2,1)S(1)} async-done(((bf16[8,96,448]{2,1,0:T(8,128)(2,1)}), bf16[8,96,448]{2,1,0:T(8,128)(2,1)S(1)}, u32[]{:S(2)}, u32[]{:S(2)}) %all-to-all-start.1) | async-done | bytes 688160 | tf_op jit(solution)/shard_map/all_to_all | solution.py:223
  84.2 4.7 %collective-permute-start.6 = (f32[2,448]{1,0:T(2,128)S(1)}, f32[2,448]{1,0:T(2,128)S(1)}, u32[]{:S(2)}, u32[]{:S(2)}) collective-permute-start(f32[2,448]{1,0:T(2,128)S(1)} %pad_maximum_fusion.16), channel_id=1, source_target_pairs={{0,256},{32,288},{64,320},{96,352},{128,384},{160,416},{192,448},{... | collective-permute-start | bytes 10760 | tf_op jit(solution)/shard_map/ppermute | solution.py:44
  92.3 4.7 %collective-permute-start.7 = (bf16[192,448]{0,1:T(8,128)(2,1)S(1)}, bf16[192,448]{0,1:T(8,128)(2,1)S(1)}, u32[]{:S(2)}, u32[]{:S(2)}) collective-permute-start(bf16[192,448]{0,1:T(8,128)(2,1)S(1)} %slice.748), channel_id=1, source_target_pairs={{0,256},{32,288},{64,320},{96,352},{128,384},{160,416},{192,448},{... | collective-permute-start | bytes 516104 | tf_op jit(solution)/shard_map/ppermute | solution.py:44
  102.4 5.2 %collective-permute-start.8 = (bf16[96,30]{1,0:T(8,128)(2,1)S(1)}, bf16[96,30]{1,0:T(8,128)(2,1)S(1)}, u32[]{:S(2)}, u32[]{:S(2)}) collective-permute-start(bf16[96,30]{1,0:T(8,128)(2,1)S(1)} %get-tuple-element.110), channel_id=1, source_target_pairs={{0,1},{1,2},{2,3},{3,4},{4,5},{5,6},{6,7},{7,8},{8,9},{9,10},{10,1... | collective-permute-start | bytes 17288 | tf_op jit(solution)/shard_map/ppermute | solution.py:174
  116.2 8.9 %all-to-all-start.2 = ((f32[32,2,96]{2,1,0:T(2,128)}), f32[32,2,96]{2,1,0:T(2,128)S(1)}, u32[]{:S(2)}, u32[]{:S(2)}) async-start(f32[32,2,96]{2,1,0:T(2,128)} %broadcast_in_dim.21), calls=%async_computation.2 | async-start | bytes 65536 | tf_op jit(solution)/shard_map/all_to_all | solution.py:28
  127.3 5.8 %all-to-all-done.2 = f32[32,2,96]{2,1,0:T(2,128)S(1)} async-done(((f32[32,2,96]{2,1,0:T(2,128)}), f32[32,2,96]{2,1,0:T(2,128)S(1)}, u32[]{:S(2)}, u32[]{:S(2)}) %all-to-all-start.2) | async-done | bytes 24608 | tf_op jit(solution)/shard_map/all_to_all | solution.py:28
  137.3 5.0 %all-to-all-start.3 = ((f32[32,2,96]{2,1,0:T(2,128)}), f32[32,2,96]{2,1,0:T(2,128)}, u32[]{:S(2)}, u32[]{:S(2)}) async-start(f32[32,2,96]{2,1,0:T(2,128)} %broadcast_in_dim.22), calls=%async_computation.3 | async-start | bytes 65536 | tf_op jit(solution)/shard_map/all_to_all | solution.py:28
  145.1 5.3 %all-to-all-done.3 = f32[32,2,96]{2,1,0:T(2,128)} async-done(((f32[32,2,96]{2,1,0:T(2,128)}), f32[32,2,96]{2,1,0:T(2,128)}, u32[]{:S(2)}, u32[]{:S(2)}) %all-to-all-start.3) | async-done | bytes 24608 | tf_op jit(solution)/shard_map/all_to_all | solution.py:28
  152.8 4.7 %conv_back.1 = (bf16[2,96,448]{2,1,0:T(8,128)(2,1)}, f32[96,512]{1,0:T(8,128)}) custom-call(f32[96,6]{1,0:T(8,128)} %copy.94.consts_ref, f32[96,31]{1,0:T(8,128)} %copy.95.taps_ref, f32[1,512]{1,0:T(1,128)} %and_convert_fusion.inside_ref, f32[96,512]{1,0:T(8,128)} %pad.30.swish_ref, f32[96,512]{1,0:T(8,128)} %pad.31.conv_ref, f32[2,96,448]{2,1,0:T(8,128)} %copy-done.3), custom_call_target="tpu_custom_call" | custom-call | tf_op jit(solution)/shard_map/conv_back/pallas_call | solution.py:149
  158.6 4.2 %collective-permute-start.10 = (bf16[288,448]{1,0:T(8,128)(2,1)S(1)}, bf16[288,448]{1,0:T(8,128)(2,1)S(1)}, u32[]{:S(2)}, u32[]{:S(2)}) collective-permute-start(bf16[288,448]{1,0:T(8,128)(2,1)S(1)} %pad_maximum_fusion.4), channel_id=1, source_target_pairs={{0,256},{32,288},{64,320},{96,352},{128,384},{160,416},{192,448},{... | collective-permute-start | bytes 774152 | tf_op jit(solution)/shard_map/ppermute | solution.py:44
  164.3 5.3 %collective-permute-done.10 = bf16[288,448]{1,0:T(8,128)(2,1)S(1)} collective-permute-done((bf16[288,448]{1,0:T(8,128)(2,1)S(1)}, bf16[288,448]{1,0:T(8,128)(2,1)S(1)}, u32[]{:S(2)}, u32[]{:S(2)}) %collective-permute-start.10) | collective-permute-done | bytes 258080 | tf_op jit(solution)/shard_map/ppermute | solution.py:44
  171.4 3.7 %collective-permute-start.11 = (bf16[144,1536]{1,0:T(8,128)(2,1)}, bf16[144,1536]{1,0:T(8,128)(2,1)}, u32[]{:S(2)}, u32[]{:S(2)}) collective-permute-start(bf16[144,1536]{1,0:T(8,128)(2,1)} %dynamic-slice_convert_fusion), channel_id=1, source_target_pairs={{0,1},{1,0},{2,3},{3,2},{4,5},{5,4},{6,7},{7,6},{8,9},{9,8},{10,11... | collective-permute-start | bytes 1327112 | tf_op jit(solution)/shard_map/ppermute | solution.py:49
  177.2 4.2 %all-to-all-start.4 = ((bf16[8,112,448]{2,1,0:T(8,128)(2,1)}), bf16[8,112,448]{2,1,0:T(8,128)(2,1)}, u32[]{:S(2)}, u32[]{:S(2)}) async-start(bf16[8,112,448]{2,1,0:T(8,128)(2,1)} %line_product.2), calls=%async_computation.4 | async-start | bytes 1835008 | tf_op jit(solution)/shard_map/all_to_all | solution.py:212
  186.6 6.5 %collective-permute-done.12 = bf16[72,1536]{1,0:T(8,128)(2,1)S(1)} collective-permute-done((bf16[72,1536]{1,0:T(8,128)(2,1)S(1)}, bf16[72,1536]{1,0:T(8,128)(2,1)S(1)}, u32[]{:S(2)}, u32[]{:S(2)}) %collective-permute-start.12) | collective-permute-done | bytes 221216 | tf_op jit(solution)/shard_map/ppermute | solution.py:49
  194.8 13.1 %all-to-all-done.4 = bf16[8,112,448]{2,1,0:T(8,128)(2,1)} async-done(((bf16[8,112,448]{2,1,0:T(8,128)(2,1)}), bf16[8,112,448]{2,1,0:T(8,128)(2,1)}, u32[]{:S(2)}, u32[]{:S(2)}) %all-to-all-start.4) | async-done | bytes 802848 | tf_op jit(solution)/shard_map/all_to_all | solution.py:212
  210.2 4.2 %all-to-all-start.5 = ((bf16[8,96,448]{2,1,0:T(8,128)(2,1)}), bf16[8,96,448]{2,1,0:T(8,128)(2,1)}, u32[]{:S(2)}, u32[]{:S(2)}) async-start(bf16[8,96,448]{2,1,0:T(8,128)(2,1)} %broadcast_in_dim.23), calls=%async_computation.5 | async-start | bytes 1572864 | tf_op jit(solution)/shard_map/all_to_all | solution.py:223
  215.5 5.1 %taps_grad.1 = f32[8,2976]{1,0:T(8,128)} custom-call(f32[96,512]{1,0:T(8,128)} %get-tuple-element.33.grad_ref, f32[96,512]{1,0:T(8,128)} %copy-done), custom_call_target="tpu_custom_call" | custom-call | tf_op jit(solution)/shard_map/taps_grad/pallas_call | solution.py:161
  221.9 4.3 %collective-permute-start.13 = (f32[2,448]{1,0:T(2,128)S(1)}, f32[2,448]{1,0:T(2,128)S(1)}, u32[]{:S(2)}, u32[]{:S(2)}) collective-permute-start(f32[2,448]{1,0:T(2,128)S(1)} %slice.417), channel_id=1, source_target_pairs={{0,256},{32,288},{64,320},{96,352},{128,384},{160,416},{192,448},{... | collective-permute-start | bytes 10760 | tf_op jit(solution)/shard_map/ppermute | solution.py:44
  228.3 9.8 %all-to-all-done.5 = bf16[8,96,448]{2,1,0:T(8,128)(2,1)} async-done(((bf16[8,96,448]{2,1,0:T(8,128)(2,1)}), bf16[8,96,448]{2,1,0:T(8,128)(2,1)}, u32[]{:S(2)}, u32[]{:S(2)}) %all-to-all-start.5) | async-done | bytes 688160 | tf_op jit(solution)/shard_map/all_to_all | solution.py:223
  241.7 4.0 %all-to-all-start.6 = ((bf16[32,6,896]{2,1,0:T(8,128)(2,1)}), bf16[32,6,896]{2,1,0:T(8,128)(2,1)S(1)}, u32[]{:S(2)}, u32[]{:S(2)}) async-start(bf16[32,6,896]{2,1,0:T(8,128)(2,1)} %fusion.18), calls=%async_computation.7 | async-start | bytes 917504 | tf_op jit(solution)/shard_map/all_to_all | solution.py:28
  247.7 4.2 %collective-permute-start.14 = (bf16[72,768]{1,0:T(8,128)(2,1)S(1)}, bf16[72,768]{1,0:T(8,128)(2,1)S(1)}, u32[]{:S(2)}, u32[]{:S(2)}) collective-permute-start(bf16[72,768]{1,0:T(8,128)(2,1)S(1)} %slice.495), channel_id=1, source_target_pairs={{0,256},{32,288},{64,320},{96,352},{128,384},{160,416},{192,448},{... | collective-permute-start | bytes 331784 | tf_op jit(solution)/shard_map/ppermute | solution.py:44
  251.9 9.3 %all-to-all-done.6 = bf16[32,6,896]{2,1,0:T(8,128)(2,1)S(1)} async-done(((bf16[32,6,896]{2,1,0:T(8,128)(2,1)}), bf16[32,6,896]{2,1,0:T(8,128)(2,1)S(1)}, u32[]{:S(2)}, u32[]{:S(2)}) %all-to-all-start.6) | async-done | bytes 344096 | tf_op jit(solution)/shard_map/all_to_all | solution.py:28
  268.3 4.2 %collective-permute-start.16 = (bf16[96,448]{1,0:T(8,128)(2,1)S(1)}, bf16[96,448]{1,0:T(8,128)(2,1)S(1)}, u32[]{:S(2)}, u32[]{:S(2)}) collective-permute-start(bf16[96,448]{1,0:T(8,128)(2,1)S(1)} %slice.749), channel_id=1, source_target_pairs={{0,256},{32,288},{64,320},{96,352},{128,384},{160,416},{192,448},{... | collective-permute-start | bytes 258056 | tf_op jit(solution)/shard_map/ppermute | solution.py:44
  272.4 5.4 %collective-permute-start.18 = (bf16[144,1536]{1,0:T(8,128)(2,1)S(1)}, bf16[144,1536]{1,0:T(8,128)(2,1)S(1)}, u32[]{:S(2)}, u32[]{:S(2)}) collective-permute-start(bf16[144,1536]{1,0:T(8,128)(2,1)S(1)} %pad_maximum_fusion.1), channel_id=1, source_target_pairs={{0,1},{1,0},{2,3},{3,2},{4,5},{5,4},{6,7},{7,6},{8,9},{9,8},{10,11... | collective-permute-start | bytes 1327112 | tf_op jit(solution)/shard_map/ppermute | solution.py:49
  285.3 12.4 %all-to-all-done.7 = bf16[32,6,896]{2,1,0:T(8,128)(2,1)S(1)} async-done(((bf16[32,6,896]{2,1,0:T(8,128)(2,1)}), bf16[32,6,896]{2,1,0:T(8,128)(2,1)S(1)}, u32[]{:S(2)}, u32[]{:S(2)}) %all-to-all-start.7) | async-done | bytes 344096 | tf_op jit(solution)/shard_map/all_to_all | solution.py:28
  (252 shorter events, 93.7 us)
Async XLA Ops:
  9.5 9.1 %collective-permute-start = (bf16[96,1216]{1,0:T(8,128)(2,1)S(1)}, bf16[96,1216]{1,0:T(8,128)(2,1)S(1)}, u32[]{:S(2)}, u32[]{:S(2)}) collective-permute-start(bf16[96,1216]{1,0:T(8,128)(2,1)S(1)} %pad_maximum_fusion.7), channel_id=1, source_target_pairs={{0,256},{32,288},{64,320},{96,352},{128,384},{160,416},{192,448},{... | collective-permute-start | bytes 700424 | tf_op jit(solution)/shard_map/ppermute | solution.py:44
  20.9 34.7 %copy-start.27 = (bf16[96,448]{1,0:T(8,128)(2,1)S(1)}, bf16[96,448]{1,0:T(8,128)(2,1)}, u32[]{:S(2)}) copy-start(bf16[96,448]{1,0:T(8,128)(2,1)} %param.12) | copy-start | bytes 258052
  20.9 34.6 %all-to-all-start = ((bf16[8,96,448]{2,1,0:T(8,128)(2,1)}), bf16[8,96,448]{2,1,0:T(8,128)(2,1)S(1)}, u32[]{:S(2)}, u32[]{:S(2)}) async-start(bf16[8,96,448]{2,1,0:T(8,128)(2,1)} %bitcast), calls=%async_computation | async-start | bytes 1572864 | tf_op jit(solution)/shard_map/all_to_all | solution.py:212
  33.1 6.8 %collective-permute-start.1 = (bf16[96,15]{1,0:T(8,128)(2,1)S(1)}, bf16[96,15]{1,0:T(8,128)(2,1)S(1)}, u32[]{:S(2)}, u32[]{:S(2)}) collective-permute-start(bf16[96,15]{1,0:T(8,128)(2,1)S(1)} %get-tuple-element.112), channel_id=1, source_target_pairs={{0,1},{1,2},{2,3},{3,4},{4,5},{5,6},{6,7},{7,8},{8,9},{9,10},{10,1... | collective-permute-start | bytes 8648 | tf_op jit(solution)/shard_map/ppermute | solution.py:174
  38.1 5.4 %collective-permute-start.2 = (bf16[96,15]{1,0:T(8,128)(2,1)S(1)}, bf16[96,15]{1,0:T(8,128)(2,1)S(1)}, u32[]{:S(2)}, u32[]{:S(2)}) collective-permute-start(bf16[96,15]{1,0:T(8,128)(2,1)S(1)} %get-tuple-element.113), channel_id=1, source_target_pairs={{1,0},{2,1},{3,2},{4,3},{5,4},{6,5},{7,6},{8,7},{9,8},{10,9},{11,1... | collective-permute-start | bytes 8648 | tf_op jit(solution)/shard_map/ppermute | solution.py:175
  43.6 6.9 %collective-permute-start.3 = (bf16[96,478]{1,0:T(8,128)(2,1)S(1)}, bf16[96,478]{1,0:T(8,128)(2,1)S(1)}, u32[]{:S(2)}, u32[]{:S(2)}) collective-permute-start(bf16[96,478]{1,0:T(8,128)(2,1)S(1)} %pad_maximum_fusion.15), channel_id=1, source_target_pairs={{0,256},{32,288},{64,320},{96,352},{128,384},{160,416},{192,448},{... | collective-permute-start | bytes 275336 | tf_op jit(solution)/shard_map/ppermute | solution.py:44
  56.6 27.2 %all-to-all-start.1 = ((bf16[8,96,448]{2,1,0:T(8,128)(2,1)}), bf16[8,96,448]{2,1,0:T(8,128)(2,1)S(1)}, u32[]{:S(2)}, u32[]{:S(2)}) async-start(bf16[8,96,448]{2,1,0:T(8,128)(2,1)} %broadcast_in_dim.19), calls=%async_computation.1 | async-start | bytes 1572864 | tf_op jit(solution)/shard_map/all_to_all | solution.py:223
  60.3 67.0 %all-gather.5.cloned.1.call-start = ((), (), s32[]{:S(2)}) async-start(), calls=%async_computation.10 | async-start | bytes 1769472 | tf_op jit(solution)/shard_map/all_gather | solution.py:254
  61.1 81.2 %collective-permute-start.5 = (bf16[96,768]{0,1:T(8,128)(2,1)}, bf16[96,768]{0,1:T(8,128)(2,1)}, u32[]{:S(2)}, u32[]{:S(2)}) collective-permute-start(bf16[96,768]{0,1:T(8,128)(2,1)} %copy.106), channel_id=1, source_target_pairs={{0,256},{32,288},{64,320},{96,352},{128,384},{160,416},{192,448},{... | collective-permute-start | bytes 442376 | tf_op jit(solution)/shard_map/ppermute | solution.py:44
  66.0 25.4 %collective-permute-start.4 = (bf16[192,768]{0,1:T(8,128)(2,1)S(1)}, bf16[192,768]{0,1:T(8,128)(2,1)S(1)}, u32[]{:S(2)}, u32[]{:S(2)}) collective-permute-start(bf16[192,768]{0,1:T(8,128)(2,1)S(1)} %copy.104), channel_id=1, source_target_pairs={{0,256},{32,288},{64,320},{96,352},{128,384},{160,416},{192,448},{... | collective-permute-start | bytes 884744 | tf_op jit(solution)/shard_map/ppermute | solution.py:44
  68.5 32.9 %copy-start.31 = (f32[1,2,96]{2,0,1:T(1,128)}, f32[1,2,96]{2,0,1:T(1,128)S(1)}, u32[]{:S(2)}) copy-start(f32[1,2,96]{2,0,1:T(1,128)S(1)} %fusion.93) | copy-start | bytes 2308
  84.2 5.9 %collective-permute-start.6 = (f32[2,448]{1,0:T(2,128)S(1)}, f32[2,448]{1,0:T(2,128)S(1)}, u32[]{:S(2)}, u32[]{:S(2)}) collective-permute-start(f32[2,448]{1,0:T(2,128)S(1)} %pad_maximum_fusion.16), channel_id=1, source_target_pairs={{0,256},{32,288},{64,320},{96,352},{128,384},{160,416},{192,448},{... | collective-permute-start | bytes 10760 | tf_op jit(solution)/shard_map/ppermute | solution.py:44
  92.3 8.8 %collective-permute-start.7 = (bf16[192,448]{0,1:T(8,128)(2,1)S(1)}, bf16[192,448]{0,1:T(8,128)(2,1)S(1)}, u32[]{:S(2)}, u32[]{:S(2)}) collective-permute-start(bf16[192,448]{0,1:T(8,128)(2,1)S(1)} %slice.748), channel_id=1, source_target_pairs={{0,256},{32,288},{64,320},{96,352},{128,384},{160,416},{192,448},{... | collective-permute-start | bytes 516104 | tf_op jit(solution)/shard_map/ppermute | solution.py:44
  102.4 7.2 %collective-permute-start.8 = (bf16[96,30]{1,0:T(8,128)(2,1)S(1)}, bf16[96,30]{1,0:T(8,128)(2,1)S(1)}, u32[]{:S(2)}, u32[]{:S(2)}) collective-permute-start(bf16[96,30]{1,0:T(8,128)(2,1)S(1)} %get-tuple-element.110), channel_id=1, source_target_pairs={{0,1},{1,2},{2,3},{3,4},{4,5},{5,6},{6,7},{7,8},{8,9},{9,10},{10,1... | collective-permute-start | bytes 17288 | tf_op jit(solution)/shard_map/ppermute | solution.py:174
  107.7 5.1 %collective-permute-start.9 = (bf16[96,30]{1,0:T(8,128)(2,1)S(1)}, bf16[96,30]{1,0:T(8,128)(2,1)S(1)}, u32[]{:S(2)}, u32[]{:S(2)}) collective-permute-start(bf16[96,30]{1,0:T(8,128)(2,1)S(1)} %get-tuple-element.111), channel_id=1, source_target_pairs={{1,0},{2,1},{3,2},{4,3},{5,4},{6,5},{7,6},{8,7},{9,8},{10,9},{11,1... | collective-permute-start | bytes 17288 | tf_op jit(solution)/shard_map/ppermute | solution.py:175
  116.2 16.8 %all-to-all-start.2 = ((f32[32,2,96]{2,1,0:T(2,128)}), f32[32,2,96]{2,1,0:T(2,128)S(1)}, u32[]{:S(2)}, u32[]{:S(2)}) async-start(f32[32,2,96]{2,1,0:T(2,128)} %broadcast_in_dim.21), calls=%async_computation.2 | async-start | bytes 65536 | tf_op jit(solution)/shard_map/all_to_all | solution.py:28
  137.3 13.1 %all-to-all-start.3 = ((f32[32,2,96]{2,1,0:T(2,128)}), f32[32,2,96]{2,1,0:T(2,128)}, u32[]{:S(2)}, u32[]{:S(2)}) async-start(f32[32,2,96]{2,1,0:T(2,128)} %broadcast_in_dim.22), calls=%async_computation.3 | async-start | bytes 65536 | tf_op jit(solution)/shard_map/all_to_all | solution.py:28
  158.6 11.0 %collective-permute-start.10 = (bf16[288,448]{1,0:T(8,128)(2,1)S(1)}, bf16[288,448]{1,0:T(8,128)(2,1)S(1)}, u32[]{:S(2)}, u32[]{:S(2)}) collective-permute-start(bf16[288,448]{1,0:T(8,128)(2,1)S(1)} %pad_maximum_fusion.4), channel_id=1, source_target_pairs={{0,256},{32,288},{64,320},{96,352},{128,384},{160,416},{192,448},{... | collective-permute-start | bytes 774152 | tf_op jit(solution)/shard_map/ppermute | solution.py:44
  171.4 10.3 %collective-permute-start.11 = (bf16[144,1536]{1,0:T(8,128)(2,1)}, bf16[144,1536]{1,0:T(8,128)(2,1)}, u32[]{:S(2)}, u32[]{:S(2)}) collective-permute-start(bf16[144,1536]{1,0:T(8,128)(2,1)} %dynamic-slice_convert_fusion), channel_id=1, source_target_pairs={{0,1},{1,0},{2,3},{3,2},{4,5},{5,4},{6,7},{7,6},{8,9},{9,8},{10,11... | collective-permute-start | bytes 1327112 | tf_op jit(solution)/shard_map/ppermute | solution.py:49
  177.2 30.7 %all-to-all-start.4 = ((bf16[8,112,448]{2,1,0:T(8,128)(2,1)}), bf16[8,112,448]{2,1,0:T(8,128)(2,1)}, u32[]{:S(2)}, u32[]{:S(2)}) async-start(bf16[8,112,448]{2,1,0:T(8,128)(2,1)} %line_product.2), calls=%async_computation.4 | async-start | bytes 1835008 | tf_op jit(solution)/shard_map/all_to_all | solution.py:212
  181.4 64.5 %all-gather.7.cloned.1.call-start = ((), (), s32[]{:S(2)}) async-start(), calls=%async_computation.11 | async-start | bytes 1990656 | tf_op jit(solution)/shard_map/all_gather | solution.py:381
  184.0 9.0 %collective-permute-start.12 = (bf16[72,1536]{1,0:T(8,128)(2,1)S(1)}, bf16[72,1536]{1,0:T(8,128)(2,1)S(1)}, u32[]{:S(2)}, u32[]{:S(2)}) collective-permute-start(bf16[72,1536]{1,0:T(8,128)(2,1)S(1)} %dynamic-slice_convert_fusion.1), channel_id=1, source_target_pairs={{0,16},{1,17},{2,18},{3,19},{4,20},{5,21},{6,22},{7,23},{8,24},{9,... | collective-permute-start | bytes 663560 | tf_op jit(solution)/shard_map/ppermute | solution.py:49
  210.2 27.8 %all-to-all-start.5 = ((bf16[8,96,448]{2,1,0:T(8,128)(2,1)}), bf16[8,96,448]{2,1,0:T(8,128)(2,1)}, u32[]{:S(2)}, u32[]{:S(2)}) async-start(bf16[8,96,448]{2,1,0:T(8,128)(2,1)} %broadcast_in_dim.23), calls=%async_computation.5 | async-start | bytes 1572864 | tf_op jit(solution)/shard_map/all_to_all | solution.py:223
  221.9 6.4 %collective-permute-start.13 = (f32[2,448]{1,0:T(2,128)S(1)}, f32[2,448]{1,0:T(2,128)S(1)}, u32[]{:S(2)}, u32[]{:S(2)}) collective-permute-start(f32[2,448]{1,0:T(2,128)S(1)} %slice.417), channel_id=1, source_target_pairs={{0,256},{32,288},{64,320},{96,352},{128,384},{160,416},{192,448},{... | collective-permute-start | bytes 10760 | tf_op jit(solution)/shard_map/ppermute | solution.py:44
  241.7 19.5 %all-to-all-start.6 = ((bf16[32,6,896]{2,1,0:T(8,128)(2,1)}), bf16[32,6,896]{2,1,0:T(8,128)(2,1)S(1)}, u32[]{:S(2)}, u32[]{:S(2)}) async-start(bf16[32,6,896]{2,1,0:T(8,128)(2,1)} %fusion.18), calls=%async_computation.7 | async-start | bytes 917504 | tf_op jit(solution)/shard_map/all_to_all | solution.py:28
  245.8 53.8 %reduce-scatter.2.cloned.1.call-start = ((), (), s32[]{:S(2)}) async-start(), calls=%async_computation.9 | async-start | bytes 1769472 | tf_op jit(solution)/shard_map/reduce_scatter | solution.py:391
  247.7 13.6 %collective-permute-start.14 = (bf16[72,768]{1,0:T(8,128)(2,1)S(1)}, bf16[72,768]{1,0:T(8,128)(2,1)S(1)}, u32[]{:S(2)}, u32[]{:S(2)}) collective-permute-start(bf16[72,768]{1,0:T(8,128)(2,1)S(1)} %slice.495), channel_id=1, source_target_pairs={{0,256},{32,288},{64,320},{96,352},{128,384},{160,416},{192,448},{... | collective-permute-start | bytes 331784 | tf_op jit(solution)/shard_map/ppermute | solution.py:44
  261.5 6.7 %collective-permute-start.15 = (bf16[72,1536]{1,0:T(8,128)(2,1)S(1)}, bf16[72,1536]{1,0:T(8,128)(2,1)S(1)}, u32[]{:S(2)}, u32[]{:S(2)}) collective-permute-start(bf16[72,1536]{1,0:T(8,128)(2,1)S(1)} %maximum_select_fusion), channel_id=1, source_target_pairs={{0,16},{1,17},{2,18},{3,19},{4,20},{5,21},{6,22},{7,23},{8,24},{9,... | collective-permute-start | bytes 663560 | tf_op jit(solution)/shard_map/ppermute | solution.py:49
  264.8 13.1 %collective-permute-start.17 = (bf16[6,896]{1,0:T(8,128)(2,1)S(1)}, bf16[6,896]{1,0:T(8,128)(2,1)S(1)}, u32[]{:S(2)}, u32[]{:S(2)}) collective-permute-start(bf16[6,896]{1,0:T(8,128)(2,1)S(1)} %reduce_sum.174), channel_id=1, source_target_pairs={{16,256},{17,257},{18,258},{19,259},{20,260},{21,261},{22,262},{23... | collective-permute-start | bytes 32264 | tf_op jit(solution)/shard_map/ppermute | solution.py:439
  268.3 14.1 %collective-permute-start.16 = (bf16[96,448]{1,0:T(8,128)(2,1)S(1)}, bf16[96,448]{1,0:T(8,128)(2,1)S(1)}, u32[]{:S(2)}, u32[]{:S(2)}) collective-permute-start(bf16[96,448]{1,0:T(8,128)(2,1)S(1)} %slice.749), channel_id=1, source_target_pairs={{0,256},{32,288},{64,320},{96,352},{128,384},{160,416},{192,448},{... | collective-permute-start | bytes 258056 | tf_op jit(solution)/shard_map/ppermute | solution.py:44
  272.4 10.6 %collective-permute-start.18 = (bf16[144,1536]{1,0:T(8,128)(2,1)S(1)}, bf16[144,1536]{1,0:T(8,128)(2,1)S(1)}, u32[]{:S(2)}, u32[]{:S(2)}) collective-permute-start(bf16[144,1536]{1,0:T(8,128)(2,1)S(1)} %pad_maximum_fusion.1), channel_id=1, source_target_pairs={{0,1},{1,0},{2,3},{3,2},{4,5},{5,4},{6,7},{7,6},{8,9},{9,8},{10,11... | collective-permute-start | bytes 1327112 | tf_op jit(solution)/shard_map/ppermute | solution.py:49
  278.7 19.0 %all-to-all-start.7 = ((bf16[32,6,896]{2,1,0:T(8,128)(2,1)}), bf16[32,6,896]{2,1,0:T(8,128)(2,1)S(1)}, u32[]{:S(2)}, u32[]{:S(2)}) async-start(bf16[32,6,896]{2,1,0:T(8,128)(2,1)} %broadcast_in_dim.26), calls=%async_computation.8 | async-start | bytes 917504 | tf_op jit(solution)/shard_map/all_to_all | solution.py:28
  (40 other events, 339.0 us)
Sparse Core Ops, SparseCore 0:
  89.4 33.9 all-gather.4
  209.4 29.6 all-gather.6
  264.2 33.0 reduce-scatter.1

commit v4 on v3

--- a/solution.py
+++ b/solution.py
@@ -100,19 +100,19 @@
 
 
 def line_product_kernel(weight_ref, operand_ref, extra_ref, out_ref):
-    lines, held, _ = out_ref.shape
-    rows = weight_ref.shape[0] // lines
+    lines, rows, lanes = out_ref.shape
+    frames = operand_ref.shape[1]
     product = jnp.dot(weight_ref[...], operand_ref[...], preferred_element_type=f32).astype(bf16)
     for index in range(lines):
-        out_ref[index, :rows, :] = product[index * rows : (index + 1) * rows]
-        out_ref[index, rows:held, :] = extra_ref[...]
+        out_ref[index, :, :frames] = product[index * rows : (index + 1) * rows]
+        out_ref[index, :, frames:lanes] = extra_ref[...]
 
 
 def line_product(weight, operand, extra, lines):
-    held = weight.shape[0] // lines + extra.shape[0]
+    rows, lanes = extra.shape[0], operand.shape[1] + extra.shape[1]
     return pl.pallas_call(
         line_product_kernel,
-        out_shape=jax.ShapeDtypeStruct((lines, held, operand.shape[1]), bf16),
+        out_shape=jax.ShapeDtypeStruct((lines, rows, lanes), bf16),
         compiler_params=pltpu.CompilerParams(vmem_limit_bytes=32 * 1024 * 1024),
         name="line_product",
     )(weight, operand, extra)
@@ -359,7 +359,11 @@
             jnp.sum(pair_float * (pair_out - bias_out[:, :, None]), axis=(0, 1)),
         ]
     )
-    frame_sums = jnp.pad(frame_sums.astype(bf16), ((0, 14), (0, 0)))
+    spare = lanes - frames
+    sum_rows = 2 * frames // spare
+    frame_sums = jnp.pad(
+        frame_sums.astype(bf16).reshape(sum_rows, spare), ((0, rows - sum_rows), (0, 0))
+    )
     normed_rows = line_exchange(line_product(glu_turned, pair_both, frame_sums, line))
 
     standard = (half_float - frame_mean) * frame_rstd
@@ -380,13 +384,14 @@
     ]
     early = lax.all_gather(early.astype(bf16), "seq", axis=0, axis_index_groups=columns)
 
-    line_sums = normed_rows[rows : rows + 2]
+    line_sums = normed_rows[:sum_rows, frames:].reshape(2, frames)
     frame_means = (line_sums + across(line_sums)) / width
-    normed_grad = line_gather(normed_rows[:rows].astype(bf16))
-
-    branch_part = line_product(
-        proj_turned, swished_pair, jnp.zeros((rows, frames), bf16), line
-    ).reshape(2 * line * rows, frames)
+    normed_grad = line_gather(normed_rows[:, :frames].astype(bf16))
+
+    branch_part = jnp.dot(proj_turned, swished_pair, preferred_element_type=f32).astype(bf16)
+    branch_part = jnp.pad(
+        branch_part.reshape(line, rows, frames), ((0, 0), (0, 2 * rows), (0, 0))
+    ).reshape(3 * line * rows, frames)
     normed_grad, branch_part = lax.optimization_barrier((normed_grad, branch_part))
     branch = lax.psum_scatter(
         branch_part, "head", scatter_dimension=0, tiled=True, axis_index_groups=line_groups()
@@ -422,12 +427,12 @@
     is_glu = (first_row + jnp.arange(early.shape[0]) >= rows)[:, None]
     early = jnp.where(is_glu, in_order(early[:, : width // 2], early_other, 1), early)
     piece = jnp.sum(exchange(late, "seq").astype(f32), axis=0).astype(bf16)
-    context_send = context_pair_grad[rows:].astype(bf16)
     piece, early = lax.optimization_barrier((piece, early))
     early = joined(early, swap_bit(early, parts // 2), parts // 2)
+    early = joined(early, swap_bit(early, 1), 1)
+    context_send = context_pair_grad[rows:].astype(bf16)
     context_send, early = lax.optimization_barrier((context_send, early))
     context_grad = (context_pair_grad[:rows] + across(context_send).astype(f32)).astype(bf16)
-    early = joined(early, swap_bit(early, 1), 1)
     early = early.astype(f32).reshape(3, rows, width)
     stays = (lax.axis_index("seq") // (parts // 2)) == side
     moves = [

time: 310 us -> 304 us (0.981)
  waiting for transfers between devices: 107 us -> 99.6 us
    all_to_all x4, starting transfers between devices: 21.7 us -> 26.6 us  [exchange(): return lax.all_to_all(blocks, axis, 0, 0, tiled=True)]
    all_to_all x2, waiting for transfers between devices: 17.3 us -> 12.5 us  [line_exchange(): lax.all_to_all(blocks, 'head', 0, 0, tiled=True, axis_index_groups=line_g...]
  transfers between devices with their start and end apart: 30 -> 30, of which waited for: 18 -> 17; matrix products, arithmetic and copies ran while one was open for 13% -> 15% of each run, Pallas kernels for 3% -> 2%
where the time goes in v4:
time: 304 us; the launch traced here: 303 us
  starting transfers between devices  120 us (39%)
  waiting for transfers between devices  99.6 us (33%)
  local copies, waits for them, and re-layouts  25.5 us (8%)
  other arithmetic  23.8 us (8%)
  between operations  15.1 us (5%)
  Pallas kernels  11.2 us (4%)
  matrix products  7.53 us (2%)
    ppermute x10, starting transfers between devices, across(): lax.ppermute(operand, 'head', [(i, (i + count // 2) % count) for i in ran...  42.1 us
    all_to_all x4, waiting for transfers between devices, exchange(): return lax.all_to_all(blocks, axis, 0, 0, tiled=True)  30.9 us
    all_to_all x4, starting transfers between devices, exchange(): return lax.all_to_all(blocks, axis, 0, 0, tiled=True)  26.6 us
    all_to_all x2, waiting for transfers between devices, line_gather(): lax.all_to_all(jnp.broadcast_to(block[None], (line, *block.shape)), 'head...  22 us
    all_to_all x2, starting transfers between devices, line_exchange(): lax.all_to_all(blocks, 'head', 0, 0, tiled=True, axis_index_groups=line_g...  15.7 us
    ppermute x10, waiting for transfers between devices, across(): lax.ppermute(operand, 'head', [(i, (i + count // 2) % count) for i in ran...  15.2 us
    ppermute x4, starting transfers between devices, swap_bit(): return lax.ppermute(operand, 'seq', [(i, i ^ bit) for i in range(count)])  13.4 us
    all_to_all x2, waiting for transfers between devices, line_exchange(): lax.all_to_all(blocks, 'head', 0, 0, tiled=True, axis_index_groups=line_g...  12.5 us
  transfers between devices with their start and end apart: 30, of which 17 were waited for; matrix products, arithmetic and copies ran while one was open for 15% of the time, Pallas kernels for 2%

profile of v4, /device:TPU:1, one launch (start us, length us, event | category | flops | bytes accessed | tf_op | source)
XLA Modules:
  0.0 302.7 jit_solution(127065172660849956)
XLA Ops:
  9.3 5.5 %collective-permute-start = (bf16[96,1216]{1,0:T(8,128)(2,1)S(1)}, bf16[96,1216]{1,0:T(8,128)(2,1)S(1)}, u32[]{:S(2)}, u32[]{:S(2)}) collective-permute-start(bf16[96,1216]{1,0:T(8,128)(2,1)S(1)} %pad_maximum_fusion.8), channel_id=1, source_target_pairs={{0,256},{32,288},{64,320},{96,352},{128,384},{160,416},{192,448},{... | collective-permute-start | bytes 700424 | tf_op jit(solution)/shard_map/ppermute | solution.py:44
  14.8 3.6 %collective-permute-done = bf16[96,1216]{1,0:T(8,128)(2,1)S(1)} collective-permute-done((bf16[96,1216]{1,0:T(8,128)(2,1)S(1)}, bf16[96,1216]{1,0:T(8,128)(2,1)S(1)}, u32[]{:S(2)}, u32[]{:S(2)}) %collective-permute-start) | collective-permute-done | bytes 233504 | tf_op jit(solution)/shard_map/ppermute | solution.py:44
  20.7 12.2 %all-to-all-start = ((bf16[8,96,448]{2,1,0:T(8,128)(2,1)}), bf16[8,96,448]{2,1,0:T(8,128)(2,1)S(1)}, u32[]{:S(2)}, u32[]{:S(2)}) async-start(bf16[8,96,448]{2,1,0:T(8,128)(2,1)} %bitcast), calls=%async_computation | async-start | bytes 1572864 | tf_op jit(solution)/shard_map/all_to_all | solution.py:212
  33.0 4.9 %collective-permute-start.1 = (bf16[96,15]{1,0:T(8,128)(2,1)S(1)}, bf16[96,15]{1,0:T(8,128)(2,1)S(1)}, u32[]{:S(2)}, u32[]{:S(2)}) collective-permute-start(bf16[96,15]{1,0:T(8,128)(2,1)S(1)} %get-tuple-element.112), channel_id=1, source_target_pairs={{0,1},{1,2},{2,3},{3,4},{4,5},{5,6},{6,7},{7,8},{8,9},{9,10},{10,1... | collective-permute-start | bytes 8648 | tf_op jit(solution)/shard_map/ppermute | solution.py:174
  43.4 4.7 %collective-permute-start.3 = (bf16[96,478]{1,0:T(8,128)(2,1)S(1)}, bf16[96,478]{1,0:T(8,128)(2,1)S(1)}, u32[]{:S(2)}, u32[]{:S(2)}) collective-permute-start(bf16[96,478]{1,0:T(8,128)(2,1)S(1)} %pad_maximum_fusion.15), channel_id=1, source_target_pairs={{0,256},{32,288},{64,320},{96,352},{128,384},{160,416},{192,448},{... | collective-permute-start | bytes 275336 | tf_op jit(solution)/shard_map/ppermute | solution.py:44
  51.1 4.1 %all-to-all-done = bf16[8,96,448]{2,1,0:T(8,128)(2,1)S(1)} async-done(((bf16[8,96,448]{2,1,0:T(8,128)(2,1)}), bf16[8,96,448]{2,1,0:T(8,128)(2,1)S(1)}, u32[]{:S(2)}, u32[]{:S(2)}) %all-to-all-start) | async-done | bytes 688160 | tf_op jit(solution)/shard_map/all_to_all | solution.py:212
  60.8 4.7 %collective-permute-start.5 = (bf16[96,768]{1,0:T(8,128)(2,1)}, bf16[96,768]{1,0:T(8,128)(2,1)}, u32[]{:S(2)}, u32[]{:S(2)}) collective-permute-start(bf16[96,768]{1,0:T(8,128)(2,1)} %get-tuple-element.103), channel_id=1, source_target_pairs={{0,256},{32,288},{64,320},{96,352},{128,384},{160,416},{192,448},{... | collective-permute-start | bytes 442376 | tf_op jit(solution)/shard_map/ppermute | solution.py:44
  68.4 13.9 %all-to-all-done.1 = bf16[8,96,448]{2,1,0:T(8,128)(2,1)S(1)} async-done(((bf16[8,96,448]{2,1,0:T(8,128)(2,1)}), bf16[8,96,448]{2,1,0:T(8,128)(2,1)S(1)}, u32[]{:S(2)}, u32[]{:S(2)}) %all-to-all-start.1) | async-done | bytes 688160 | tf_op jit(solution)/shard_map/all_to_all | solution.py:223
  82.8 5.8 %collective-permute-start.6 = (f32[2,448]{1,0:T(2,128)S(1)}, f32[2,448]{1,0:T(2,128)S(1)}, u32[]{:S(2)}, u32[]{:S(2)}) collective-permute-start(f32[2,448]{1,0:T(2,128)S(1)} %pad_maximum_fusion.16), channel_id=1, source_target_pairs={{0,256},{32,288},{64,320},{96,352},{128,384},{160,416},{192,448},{... | collective-permute-start | bytes 10760 | tf_op jit(solution)/shard_map/ppermute | solution.py:44
  91.8 4.9 %collective-permute-start.7 = (bf16[192,448]{0,1:T(8,128)(2,1)S(1)}, bf16[192,448]{0,1:T(8,128)(2,1)S(1)}, u32[]{:S(2)}, u32[]{:S(2)}) collective-permute-start(bf16[192,448]{0,1:T(8,128)(2,1)S(1)} %slice.748), channel_id=1, source_target_pairs={{0,256},{32,288},{64,320},{96,352},{128,384},{160,416},{192,448},{... | collective-permute-start | bytes 516104 | tf_op jit(solution)/shard_map/ppermute | solution.py:44
  101.1 5.6 %collective-permute-start.8 = (bf16[96,30]{1,0:T(8,128)(2,1)S(1)}, bf16[96,30]{1,0:T(8,128)(2,1)S(1)}, u32[]{:S(2)}, u32[]{:S(2)}) collective-permute-start(bf16[96,30]{1,0:T(8,128)(2,1)S(1)} %get-tuple-element.110), channel_id=1, source_target_pairs={{0,1},{1,2},{2,3},{3,4},{4,5},{5,6},{6,7},{7,8},{8,9},{9,10},{10,1... | collective-permute-start | bytes 17288 | tf_op jit(solution)/shard_map/ppermute | solution.py:174
  115.4 9.1 %all-to-all-start.2 = ((f32[32,2,96]{2,1,0:T(2,128)}), f32[32,2,96]{2,1,0:T(2,128)S(1)}, u32[]{:S(2)}, u32[]{:S(2)}) async-start(f32[32,2,96]{2,1,0:T(2,128)} %broadcast_in_dim.19), calls=%async_computation.2 | async-start | bytes 65536 | tf_op jit(solution)/shard_map/all_to_all | solution.py:28
  125.8 6.6 %all-to-all-done.2 = f32[32,2,96]{2,1,0:T(2,128)S(1)} async-done(((f32[32,2,96]{2,1,0:T(2,128)}), f32[32,2,96]{2,1,0:T(2,128)S(1)}, u32[]{:S(2)}, u32[]{:S(2)}) %all-to-all-start.2) | async-done | bytes 24608 | tf_op jit(solution)/shard_map/all_to_all | solution.py:28
  135.5 4.4 %all-to-all-start.3 = ((f32[32,2,96]{2,1,0:T(2,128)}), f32[32,2,96]{2,1,0:T(2,128)S(1)}, u32[]{:S(2)}, u32[]{:S(2)}) async-start(f32[32,2,96]{2,1,0:T(2,128)} %broadcast_in_dim.20), calls=%async_computation.3 | async-start | bytes 65536 | tf_op jit(solution)/shard_map/all_to_all | solution.py:28
  143.0 4.9 %all-to-all-done.3 = f32[32,2,96]{2,1,0:T(2,128)S(1)} async-done(((f32[32,2,96]{2,1,0:T(2,128)}), f32[32,2,96]{2,1,0:T(2,128)S(1)}, u32[]{:S(2)}, u32[]{:S(2)}) %all-to-all-start.3) | async-done | bytes 24608 | tf_op jit(solution)/shard_map/all_to_all | solution.py:28
  148.8 4.7 %conv_back.1 = (bf16[2,96,448]{2,1,0:T(8,128)(2,1)}, f32[96,512]{1,0:T(8,128)}) custom-call(f32[96,6]{1,0:T(8,128)} %copy.87.consts_ref, f32[96,31]{1,0:T(8,128)} %copy.88.taps_ref, f32[1,512]{1,0:T(1,128)} %and_convert_fusion.inside_ref, f32[96,512]{1,0:T(8,128)} %pad.34.swish_ref, f32[96,512]{1,0:T(8,128)} %pad.35.conv_ref, f32[2,96,448]{2,1,0:T(8,128)} %copy-done.3), custom_call_target="tpu_custom_call" | custom-call | tf_op jit(solution)/shard_map/conv_back/pallas_call | solution.py:149
  154.6 3.9 %collective-permute-start.10 = (bf16[288,448]{1,0:T(8,128)(2,1)S(1)}, bf16[288,448]{1,0:T(8,128)(2,1)S(1)}, u32[]{:S(2)}, u32[]{:S(2)}) collective-permute-start(bf16[288,448]{1,0:T(8,128)(2,1)S(1)} %pad_maximum_fusion.5), channel_id=1, source_target_pairs={{0,256},{32,288},{64,320},{96,352},{128,384},{160,416},{192,448},{... | collective-permute-start | bytes 774152 | tf_op jit(solution)/shard_map/ppermute | solution.py:44
  160.1 5.5 %collective-permute-done.10 = bf16[288,448]{1,0:T(8,128)(2,1)S(1)} collective-permute-done((bf16[288,448]{1,0:T(8,128)(2,1)S(1)}, bf16[288,448]{1,0:T(8,128)(2,1)S(1)}, u32[]{:S(2)}, u32[]{:S(2)}) %collective-permute-start.10) | collective-permute-done | bytes 258080 | tf_op jit(solution)/shard_map/ppermute | solution.py:44
  168.6 3.7 %collective-permute-start.11 = (bf16[144,1536]{1,0:T(8,128)(2,1)}, bf16[144,1536]{1,0:T(8,128)(2,1)}, u32[]{:S(2)}, u32[]{:S(2)}) collective-permute-start(bf16[144,1536]{1,0:T(8,128)(2,1)} %dynamic-slice_convert_fusion), channel_id=1, source_target_pairs={{0,1},{1,0},{2,3},{3,2},{4,5},{5,4},{6,7},{7,6},{8,9},{9,8},{10,11... | collective-permute-start | bytes 1327112 | tf_op jit(solution)/shard_map/ppermute | solution.py:49
  185.8 6.5 %collective-permute-done.12 = bf16[72,1536]{1,0:T(8,128)(2,1)} collective-permute-done((bf16[72,1536]{1,0:T(8,128)(2,1)}, bf16[72,1536]{1,0:T(8,128)(2,1)}, u32[]{:S(2)}, u32[]{:S(2)}) %collective-permute-start.12) | collective-permute-done | bytes 221216 | tf_op jit(solution)/shard_map/ppermute | solution.py:49
  194.2 8.4 %all-to-all-done.4 = bf16[8,96,512]{2,1,0:T(8,128)(2,1)S(1)} async-done(((bf16[8,96,512]{2,1,0:T(8,128)(2,1)}), bf16[8,96,512]{2,1,0:T(8,128)(2,1)S(1)}, u32[]{:S(2)}, u32[]{:S(2)}) %all-to-all-start.4) | async-done | bytes 786464 | tf_op jit(solution)/shard_map/all_to_all | solution.py:212
  203.6 3.5 %all-to-all-start.5 = ((bf16[8,96,448]{2,1,0:T(8,128)(2,1)}), bf16[8,96,448]{2,1,0:T(8,128)(2,1)S(1)}, u32[]{:S(2)}, u32[]{:S(2)}) async-start(bf16[8,96,448]{2,1,0:T(8,128)(2,1)} %broadcast_in_dim.21), calls=%async_computation.5 | async-start | bytes 1572864 | tf_op jit(solution)/shard_map/all_to_all | solution.py:223
  208.2 5.1 %taps_grad.1 = f32[8,2976]{1,0:T(8,128)} custom-call(f32[96,512]{1,0:T(8,128)} %get-tuple-element.33.grad_ref, f32[96,512]{1,0:T(8,128)} %copy-done), custom_call_target="tpu_custom_call" | custom-call | tf_op jit(solution)/shard_map/taps_grad/pallas_call | solution.py:161
  215.3 3.9 %collective-permute-start.13 = (f32[2,448]{1,0:T(2,128)S(1)}, f32[2,448]{1,0:T(2,128)S(1)}, u32[]{:S(2)}, u32[]{:S(2)}) collective-permute-start(f32[2,448]{1,0:T(2,128)S(1)} %reshape.265), channel_id=1, source_target_pairs={{0,256},{32,288},{64,320},{96,352},{128,384},{160,416},{192,448},{... | collective-permute-start | bytes 10760 | tf_op jit(solution)/shard_map/ppermute | solution.py:44
  222.6 8.1 %all-to-all-done.5 = bf16[8,96,448]{2,1,0:T(8,128)(2,1)S(1)} async-done(((bf16[8,96,448]{2,1,0:T(8,128)(2,1)}), bf16[8,96,448]{2,1,0:T(8,128)(2,1)S(1)}, u32[]{:S(2)}, u32[]{:S(2)}) %all-to-all-start.5) | async-done | bytes 688160 | tf_op jit(solution)/shard_map/all_to_all | solution.py:223
  233.5 4.0 %all-to-all-start.6 = ((bf16[32,6,896]{2,1,0:T(8,128)(2,1)}), bf16[32,6,896]{2,1,0:T(8,128)(2,1)S(1)}, u32[]{:S(2)}, u32[]{:S(2)}) async-start(bf16[32,6,896]{2,1,0:T(8,128)(2,1)} %fusion.18), calls=%async_computation.7 | async-start | bytes 917504 | tf_op jit(solution)/shard_map/all_to_all | solution.py:28
  240.1 3.9 %collective-permute-start.14 = (bf16[72,768]{1,0:T(8,128)(2,1)S(1)}, bf16[72,768]{1,0:T(8,128)(2,1)S(1)}, u32[]{:S(2)}, u32[]{:S(2)}) collective-permute-start(bf16[72,768]{1,0:T(8,128)(2,1)S(1)} %slice.495), channel_id=1, source_target_pairs={{0,256},{32,288},{64,320},{96,352},{128,384},{160,416},{192,448},{... | collective-permute-start | bytes 331784 | tf_op jit(solution)/shard_map/ppermute | solution.py:44
  244.0 9.0 %all-to-all-done.6 = bf16[32,6,896]{2,1,0:T(8,128)(2,1)S(1)} async-done(((bf16[32,6,896]{2,1,0:T(8,128)(2,1)}), bf16[32,6,896]{2,1,0:T(8,128)(2,1)S(1)}, u32[]{:S(2)}, u32[]{:S(2)}) %all-to-all-start.6) | async-done | bytes 344096 | tf_op jit(solution)/shard_map/all_to_all | solution.py:28
  255.6 4.8 %collective-permute-done.15 = bf16[72,1536]{1,0:T(8,128)(2,1)S(1)} collective-permute-done((bf16[72,1536]{1,0:T(8,128)(2,1)S(1)}, bf16[72,1536]{1,0:T(8,128)(2,1)S(1)}, u32[]{:S(2)}, u32[]{:S(2)}) %collective-permute-start.15) | collective-permute-done | bytes 221216 | tf_op jit(solution)/shard_map/ppermute | solution.py:49
  260.4 4.7 %collective-permute-start.16 = (bf16[144,1536]{1,0:T(8,128)(2,1)S(1)}, bf16[144,1536]{1,0:T(8,128)(2,1)S(1)}, u32[]{:S(2)}, u32[]{:S(2)}) collective-permute-start(bf16[144,1536]{1,0:T(8,128)(2,1)S(1)} %pad_maximum_fusion.2), channel_id=1, source_target_pairs={{0,1},{1,0},{2,3},{3,2},{4,5},{5,4},{6,7},{7,6},{8,9},{9,8},{10,11... | collective-permute-start | bytes 1327112 | tf_op jit(solution)/shard_map/ppermute | solution.py:49
  267.7 9.0 %all-to-all-start.7 = ((bf16[32,6,896]{2,1,0:T(8,128)(2,1)}), bf16[32,6,896]{2,1,0:T(8,128)(2,1)S(1)}, u32[]{:S(2)}, u32[]{:S(2)}) async-start(bf16[32,6,896]{2,1,0:T(8,128)(2,1)} %broadcast_in_dim.23), calls=%async_computation.8 | async-start | bytes 917504 | tf_op jit(solution)/shard_map/all_to_all | solution.py:28
  281.7 10.4 %all-to-all-done.7 = bf16[32,6,896]{2,1,0:T(8,128)(2,1)S(1)} async-done(((bf16[32,6,896]{2,1,0:T(8,128)(2,1)}), bf16[32,6,896]{2,1,0:T(8,128)(2,1)S(1)}, u32[]{:S(2)}, u32[]{:S(2)}) %all-to-all-start.7) | async-done | bytes 344096 | tf_op jit(solution)/shard_map/all_to_all | solution.py:28
  (255 shorter events, 93.4 us)
Async XLA Ops:
  9.3 9.1 %collective-permute-start = (bf16[96,1216]{1,0:T(8,128)(2,1)S(1)}, bf16[96,1216]{1,0:T(8,128)(2,1)S(1)}, u32[]{:S(2)}, u32[]{:S(2)}) collective-permute-start(bf16[96,1216]{1,0:T(8,128)(2,1)S(1)} %pad_maximum_fusion.8), channel_id=1, source_target_pairs={{0,256},{32,288},{64,320},{96,352},{128,384},{160,416},{192,448},{... | collective-permute-start | bytes 700424 | tf_op jit(solution)/shard_map/ppermute | solution.py:44
  20.7 34.6 %copy-start.29 = (bf16[96,448]{1,0:T(8,128)(2,1)S(1)}, bf16[96,448]{1,0:T(8,128)(2,1)}, u32[]{:S(2)}) copy-start(bf16[96,448]{1,0:T(8,128)(2,1)} %param.12) | copy-start | bytes 258052
  20.7 34.5 %all-to-all-start = ((bf16[8,96,448]{2,1,0:T(8,128)(2,1)}), bf16[8,96,448]{2,1,0:T(8,128)(2,1)S(1)}, u32[]{:S(2)}, u32[]{:S(2)}) async-start(bf16[8,96,448]{2,1,0:T(8,128)(2,1)} %bitcast), calls=%async_computation | async-start | bytes 1572864 | tf_op jit(solution)/shard_map/all_to_all | solution.py:212
  33.0 6.8 %collective-permute-start.1 = (bf16[96,15]{1,0:T(8,128)(2,1)S(1)}, bf16[96,15]{1,0:T(8,128)(2,1)S(1)}, u32[]{:S(2)}, u32[]{:S(2)}) collective-permute-start(bf16[96,15]{1,0:T(8,128)(2,1)S(1)} %get-tuple-element.112), channel_id=1, source_target_pairs={{0,1},{1,2},{2,3},{3,4},{4,5},{5,6},{6,7},{7,8},{8,9},{9,10},{10,1... | collective-permute-start | bytes 8648 | tf_op jit(solution)/shard_map/ppermute | solution.py:174
  37.9 5.4 %collective-permute-start.2 = (bf16[96,15]{1,0:T(8,128)(2,1)S(1)}, bf16[96,15]{1,0:T(8,128)(2,1)S(1)}, u32[]{:S(2)}, u32[]{:S(2)}) collective-permute-start(bf16[96,15]{1,0:T(8,128)(2,1)S(1)} %get-tuple-element.113), channel_id=1, source_target_pairs={{1,0},{2,1},{3,2},{4,3},{5,4},{6,5},{7,6},{8,7},{9,8},{10,9},{11,1... | collective-permute-start | bytes 8648 | tf_op jit(solution)/shard_map/ppermute | solution.py:175
  43.4 6.9 %collective-permute-start.3 = (bf16[96,478]{1,0:T(8,128)(2,1)S(1)}, bf16[96,478]{1,0:T(8,128)(2,1)S(1)}, u32[]{:S(2)}, u32[]{:S(2)}) collective-permute-start(bf16[96,478]{1,0:T(8,128)(2,1)S(1)} %pad_maximum_fusion.15), channel_id=1, source_target_pairs={{0,256},{32,288},{64,320},{96,352},{128,384},{160,416},{192,448},{... | collective-permute-start | bytes 275336 | tf_op jit(solution)/shard_map/ppermute | solution.py:44
  56.4 25.9 %all-to-all-start.1 = ((bf16[8,96,448]{2,1,0:T(8,128)(2,1)}), bf16[8,96,448]{2,1,0:T(8,128)(2,1)S(1)}, u32[]{:S(2)}, u32[]{:S(2)}) async-start(bf16[8,96,448]{2,1,0:T(8,128)(2,1)} %broadcast_in_dim.17), calls=%async_computation.1 | async-start | bytes 1572864 | tf_op jit(solution)/shard_map/all_to_all | solution.py:223
  59.9 65.9 %all-gather.5.cloned.1.call-start = ((), (), s32[]{:S(2)}) async-start(), calls=%async_computation.10 | async-start | bytes 1769472 | tf_op jit(solution)/shard_map/all_gather | solution.py:254
  60.8 79.2 %collective-permute-start.5 = (bf16[96,768]{1,0:T(8,128)(2,1)}, bf16[96,768]{1,0:T(8,128)(2,1)}, u32[]{:S(2)}, u32[]{:S(2)}) collective-permute-start(bf16[96,768]{1,0:T(8,128)(2,1)} %get-tuple-element.103), channel_id=1, source_target_pairs={{0,256},{32,288},{64,320},{96,352},{128,384},{160,416},{192,448},{... | collective-permute-start | bytes 442376 | tf_op jit(solution)/shard_map/ppermute | solution.py:44
  65.7 25.2 %collective-permute-start.4 = (bf16[192,768]{0,1:T(8,128)(2,1)S(1)}, bf16[192,768]{0,1:T(8,128)(2,1)S(1)}, u32[]{:S(2)}, u32[]{:S(2)}) collective-permute-start(bf16[192,768]{0,1:T(8,128)(2,1)S(1)} %copy.98), channel_id=1, source_target_pairs={{0,256},{32,288},{64,320},{96,352},{128,384},{160,416},{192,448},{... | collective-permute-start | bytes 884744 | tf_op jit(solution)/shard_map/ppermute | solution.py:44
  68.1 32.6 %copy-start.33 = (f32[1,2,96]{2,0,1:T(1,128)}, f32[1,2,96]{2,0,1:T(1,128)S(1)}, u32[]{:S(2)}) copy-start(f32[1,2,96]{2,0,1:T(1,128)S(1)} %fusion.94) | copy-start | bytes 2308
  82.8 6.8 %collective-permute-start.6 = (f32[2,448]{1,0:T(2,128)S(1)}, f32[2,448]{1,0:T(2,128)S(1)}, u32[]{:S(2)}, u32[]{:S(2)}) collective-permute-start(f32[2,448]{1,0:T(2,128)S(1)} %pad_maximum_fusion.16), channel_id=1, source_target_pairs={{0,256},{32,288},{64,320},{96,352},{128,384},{160,416},{192,448},{... | collective-permute-start | bytes 10760 | tf_op jit(solution)/shard_map/ppermute | solution.py:44
  91.8 8.7 %collective-permute-start.7 = (bf16[192,448]{0,1:T(8,128)(2,1)S(1)}, bf16[192,448]{0,1:T(8,128)(2,1)S(1)}, u32[]{:S(2)}, u32[]{:S(2)}) collective-permute-start(bf16[192,448]{0,1:T(8,128)(2,1)S(1)} %slice.748), channel_id=1, source_target_pairs={{0,256},{32,288},{64,320},{96,352},{128,384},{160,416},{192,448},{... | collective-permute-start | bytes 516104 | tf_op jit(solution)/shard_map/ppermute | solution.py:44
  101.1 7.6 %collective-permute-start.8 = (bf16[96,30]{1,0:T(8,128)(2,1)S(1)}, bf16[96,30]{1,0:T(8,128)(2,1)S(1)}, u32[]{:S(2)}, u32[]{:S(2)}) collective-permute-start(bf16[96,30]{1,0:T(8,128)(2,1)S(1)} %get-tuple-element.110), channel_id=1, source_target_pairs={{0,1},{1,2},{2,3},{3,4},{4,5},{5,6},{6,7},{7,8},{8,9},{9,10},{10,1... | collective-permute-start | bytes 17288 | tf_op jit(solution)/shard_map/ppermute | solution.py:174
  106.7 5.3 %collective-permute-start.9 = (bf16[96,30]{1,0:T(8,128)(2,1)S(1)}, bf16[96,30]{1,0:T(8,128)(2,1)S(1)}, u32[]{:S(2)}, u32[]{:S(2)}) collective-permute-start(bf16[96,30]{1,0:T(8,128)(2,1)S(1)} %get-tuple-element.111), channel_id=1, source_target_pairs={{1,0},{2,1},{3,2},{4,3},{5,4},{6,5},{7,6},{8,7},{9,8},{10,9},{11,1... | collective-permute-start | bytes 17288 | tf_op jit(solution)/shard_map/ppermute | solution.py:175
  115.4 17.1 %all-to-all-start.2 = ((f32[32,2,96]{2,1,0:T(2,128)}), f32[32,2,96]{2,1,0:T(2,128)S(1)}, u32[]{:S(2)}, u32[]{:S(2)}) async-start(f32[32,2,96]{2,1,0:T(2,128)} %broadcast_in_dim.19), calls=%async_computation.2 | async-start | bytes 65536 | tf_op jit(solution)/shard_map/all_to_all | solution.py:28
  135.5 12.5 %all-to-all-start.3 = ((f32[32,2,96]{2,1,0:T(2,128)}), f32[32,2,96]{2,1,0:T(2,128)S(1)}, u32[]{:S(2)}, u32[]{:S(2)}) async-start(f32[32,2,96]{2,1,0:T(2,128)} %broadcast_in_dim.20), calls=%async_computation.3 | async-start | bytes 65536 | tf_op jit(solution)/shard_map/all_to_all | solution.py:28
  154.6 11.0 %collective-permute-start.10 = (bf16[288,448]{1,0:T(8,128)(2,1)S(1)}, bf16[288,448]{1,0:T(8,128)(2,1)S(1)}, u32[]{:S(2)}, u32[]{:S(2)}) collective-permute-start(bf16[288,448]{1,0:T(8,128)(2,1)S(1)} %pad_maximum_fusion.5), channel_id=1, source_target_pairs={{0,256},{32,288},{64,320},{96,352},{128,384},{160,416},{192,448},{... | collective-permute-start | bytes 774152 | tf_op jit(solution)/shard_map/ppermute | solution.py:44
  168.6 10.4 %collective-permute-start.11 = (bf16[144,1536]{1,0:T(8,128)(2,1)}, bf16[144,1536]{1,0:T(8,128)(2,1)}, u32[]{:S(2)}, u32[]{:S(2)}) collective-permute-start(bf16[144,1536]{1,0:T(8,128)(2,1)} %dynamic-slice_convert_fusion), channel_id=1, source_target_pairs={{0,1},{1,0},{2,3},{3,2},{4,5},{5,4},{6,7},{7,6},{8,9},{9,8},{10,11... | collective-permute-start | bytes 1327112 | tf_op jit(solution)/shard_map/ppermute | solution.py:49
  175.4 27.1 %all-to-all-start.4 = ((bf16[8,96,512]{2,1,0:T(8,128)(2,1)}), bf16[8,96,512]{2,1,0:T(8,128)(2,1)S(1)}, u32[]{:S(2)}, u32[]{:S(2)}) async-start(bf16[8,96,512]{2,1,0:T(8,128)(2,1)} %line_product.1), calls=%async_computation.4 | async-start | bytes 1572864 | tf_op jit(solution)/shard_map/all_to_all | solution.py:212
  178.9 59.3 %all-gather.7.cloned.1.call-start = ((), (), s32[]{:S(2)}) async-start(), calls=%async_computation.11 | async-start | bytes 1990656 | tf_op jit(solution)/shard_map/all_gather | solution.py:385
  183.0 9.3 %collective-permute-start.12 = (bf16[72,1536]{1,0:T(8,128)(2,1)}, bf16[72,1536]{1,0:T(8,128)(2,1)}, u32[]{:S(2)}, u32[]{:S(2)}) collective-permute-start(bf16[72,1536]{1,0:T(8,128)(2,1)} %dynamic-slice_convert_fusion.1), channel_id=1, source_target_pairs={{0,16},{1,17},{2,18},{3,19},{4,20},{5,21},{6,22},{7,23},{8,24},{9,... | collective-permute-start | bytes 663560 | tf_op jit(solution)/shard_map/ppermute | solution.py:49
  203.6 27.1 %all-to-all-start.5 = ((bf16[8,96,448]{2,1,0:T(8,128)(2,1)}), bf16[8,96,448]{2,1,0:T(8,128)(2,1)S(1)}, u32[]{:S(2)}, u32[]{:S(2)}) async-start(bf16[8,96,448]{2,1,0:T(8,128)(2,1)} %broadcast_in_dim.21), calls=%async_computation.5 | async-start | bytes 1572864 | tf_op jit(solution)/shard_map/all_to_all | solution.py:223
  215.3 7.2 %collective-permute-start.13 = (f32[2,448]{1,0:T(2,128)S(1)}, f32[2,448]{1,0:T(2,128)S(1)}, u32[]{:S(2)}, u32[]{:S(2)}) collective-permute-start(f32[2,448]{1,0:T(2,128)S(1)} %reshape.265), channel_id=1, source_target_pairs={{0,256},{32,288},{64,320},{96,352},{128,384},{160,416},{192,448},{... | collective-permute-start | bytes 10760 | tf_op jit(solution)/shard_map/ppermute | solution.py:44
  233.5 19.5 %all-to-all-start.6 = ((bf16[32,6,896]{2,1,0:T(8,128)(2,1)}), bf16[32,6,896]{2,1,0:T(8,128)(2,1)S(1)}, u32[]{:S(2)}, u32[]{:S(2)}) async-start(bf16[32,6,896]{2,1,0:T(8,128)(2,1)} %fusion.18), calls=%async_computation.7 | async-start | bytes 917504 | tf_op jit(solution)/shard_map/all_to_all | solution.py:28
  237.5 57.1 %reduce-scatter.2.cloned.1.call-start = ((), (), s32[]{:S(2)}) async-start(), calls=%async_computation.9 | async-start | bytes 2654208 | tf_op jit(solution)/shard_map/reduce_scatter | solution.py:396
  240.1 13.1 %collective-permute-start.14 = (bf16[72,768]{1,0:T(8,128)(2,1)S(1)}, bf16[72,768]{1,0:T(8,128)(2,1)S(1)}, u32[]{:S(2)}, u32[]{:S(2)}) collective-permute-start(bf16[72,768]{1,0:T(8,128)(2,1)S(1)} %slice.495), channel_id=1, source_target_pairs={{0,256},{32,288},{64,320},{96,352},{128,384},{160,416},{192,448},{... | collective-permute-start | bytes 331784 | tf_op jit(solution)/shard_map/ppermute | solution.py:44
  253.3 7.1 %collective-permute-start.15 = (bf16[72,1536]{1,0:T(8,128)(2,1)S(1)}, bf16[72,1536]{1,0:T(8,128)(2,1)S(1)}, u32[]{:S(2)}, u32[]{:S(2)}) collective-permute-start(bf16[72,1536]{1,0:T(8,128)(2,1)S(1)} %maximum_select_fusion), channel_id=1, source_target_pairs={{0,16},{1,17},{2,18},{3,19},{4,20},{5,21},{6,22},{7,23},{8,24},{9,... | collective-permute-start | bytes 663560 | tf_op jit(solution)/shard_map/ppermute | solution.py:49
  260.4 16.3 %collective-permute-start.16 = (bf16[144,1536]{1,0:T(8,128)(2,1)S(1)}, bf16[144,1536]{1,0:T(8,128)(2,1)S(1)}, u32[]{:S(2)}, u32[]{:S(2)}) collective-permute-start(bf16[144,1536]{1,0:T(8,128)(2,1)S(1)} %pad_maximum_fusion.2), channel_id=1, source_target_pairs={{0,1},{1,0},{2,3},{3,2},{4,5},{5,4},{6,7},{7,6},{8,9},{9,8},{10,11... | collective-permute-start | bytes 1327112 | tf_op jit(solution)/shard_map/ppermute | solution.py:49
  265.5 1.3 collective-permute-start.18
  267.7 24.4 %all-to-all-start.7 = ((bf16[32,6,896]{2,1,0:T(8,128)(2,1)}), bf16[32,6,896]{2,1,0:T(8,128)(2,1)S(1)}, u32[]{:S(2)}, u32[]{:S(2)}) async-start(bf16[32,6,896]{2,1,0:T(8,128)(2,1)} %broadcast_in_dim.23), calls=%async_computation.8 | async-start | bytes 917504 | tf_op jit(solution)/shard_map/all_to_all | solution.py:28
  279.0 14.9 %collective-permute-start.17 = (bf16[96,448]{1,0:T(8,128)(2,1)S(1)}, bf16[96,448]{1,0:T(8,128)(2,1)S(1)}, u32[]{:S(2)}, u32[]{:S(2)}) collective-permute-start(bf16[96,448]{1,0:T(8,128)(2,1)S(1)} %slice.749), channel_id=1, source_target_pairs={{0,256},{32,288},{64,320},{96,352},{128,384},{160,416},{192,448},{... | collective-permute-start | bytes 258056 | tf_op jit(solution)/shard_map/ppermute | solution.py:44
  (41 other events, 327.3 us)
Sparse Core Ops, SparseCore 0:
  89.1 33.9 all-gather.4
  202.8 29.6 all-gather.6
  241.2 41.4 reduce-scatter.1

commit v5 on v4

--- a/solution.py
+++ b/solution.py
@@ -275,10 +275,13 @@
     half_cent = half_float - half_mean
     half_square = jnp.sum(half_cent * half_cent, axis=0, keepdims=True)
     half_moments = jnp.concatenate([half_mean, half_square])
-    other_moments = across(half_moments)
     gained = (half_cent * side_half(gain_col)).astype(bf16)
     products = jnp.dot(glu_half, gained, preferred_element_type=f32)
-    other_products = across(products[2 * rows :].astype(bf16)).astype(f32)
+    products_send, half_moments = lax.optimization_barrier(
+        (products[2 * rows :].astype(bf16), half_moments)
+    )
+    other_products = across(products_send).astype(f32)
+    other_moments = across(half_moments)
     mean_gap = 0.5 * (half_moments[0:1] - other_moments[0:1])
     frame_mean = half_moments[0:1] - mean_gap
     frame_var = (
@@ -429,11 +432,6 @@
     piece = jnp.sum(exchange(late, "seq").astype(f32), axis=0).astype(bf16)
     piece, early = lax.optimization_barrier((piece, early))
     early = joined(early, swap_bit(early, parts // 2), parts // 2)
-    early = joined(early, swap_bit(early, 1), 1)
-    context_send = context_pair_grad[rows:].astype(bf16)
-    context_send, early = lax.optimization_barrier((context_send, early))
-    context_grad = (context_pair_grad[:rows] + across(context_send).astype(f32)).astype(bf16)
-    early = early.astype(f32).reshape(3, rows, width)
     stays = (lax.axis_index("seq") // (parts // 2)) == side
     moves = [
         (h * parts + s, (h + line) % heads * parts + (s + parts // 2) % parts)
@@ -442,6 +440,12 @@
         if s // (parts // 2) != h // line
     ]
     moved = lax.ppermute(piece, ("head", "seq"), moves)
+    moved, early = lax.optimization_barrier((moved, early))
+    early = joined(early, swap_bit(early, 1), 1)
+    context_send = context_pair_grad[rows:].astype(bf16)
+    context_send, early = lax.optimization_barrier((context_send, early))
+    context_grad = (context_pair_grad[:rows] + across(context_send).astype(f32)).astype(bf16)
+    early = early.astype(f32).reshape(3, rows, width)
     out_lanes = lax.broadcasted_iota(jnp.int32, piece.shape, 1) < width // 2
     piece = jnp.where(out_lanes & ~stays, moved, piece)
     late = gather(piece, "seq")

time: 304 us -> 299 us (0.984)
  starting transfers between devices: 120 us -> 116 us
    all_to_all x4, waiting for transfers between devices: 30.9 us -> 23.6 us  [exchange(): return lax.all_to_all(blocks, axis, 0, 0, tiled=True)]
    ppermute x10, waiting for transfers between devices: 15.2 us -> 21.2 us  [across(): lax.ppermute(operand, 'head', [(i, (i + count // 2) % count) for i in ran...]
  transfers between devices with their start and end apart: 30 -> 30, of which waited for: 17 -> 18; matrix products, arithmetic and copies ran while one was open for 15% -> 13% of each run, Pallas kernels for 2% -> 2%
where the time goes in v5:
time: 299 us; the launch traced here: 297 us
  starting transfers between devices  116 us (39%)
  waiting for transfers between devices  99.3 us (33%)
  local copies, waits for them, and re-layouts  26.9 us (9%)
  other arithmetic  21.8 us (7%)
  between operations  15.4 us (5%)
  Pallas kernels  11.2 us (4%)
  matrix products  5.67 us (2%)
    ppermute x10, starting transfers between devices, across(): lax.ppermute(operand, 'head', [(i, (i + count // 2) % count) for i in ran...  42.3 us
    all_to_all x4, starting transfers between devices, exchange(): return lax.all_to_all(blocks, axis, 0, 0, tiled=True)  24.2 us
    all_to_all x4, waiting for transfers between devices, exchange(): return lax.all_to_all(blocks, axis, 0, 0, tiled=True)  23.6 us
    ppermute x10, waiting for transfers between devices, across(): lax.ppermute(operand, 'head', [(i, (i + count // 2) % count) for i in ran...  21.2 us
    all_to_all x2, waiting for transfers between devices, line_gather(): lax.all_to_all(jnp.broadcast_to(block[None], (line, *block.shape)), 'head...  20.7 us
    all_to_all x2, starting transfers between devices, line_exchange(): lax.all_to_all(blocks, 'head', 0, 0, tiled=True, axis_index_groups=line_g...  16.1 us
    all_to_all x2, waiting for transfers between devices, line_exchange(): lax.all_to_all(blocks, 'head', 0, 0, tiled=True, axis_index_groups=line_g...  13.9 us
    ppermute x4, starting transfers between devices, swap_bit(): return lax.ppermute(operand, 'seq', [(i, i ^ bit) for i in range(count)])  13.2 us
  transfers between devices with their start and end apart: 30, of which 18 were waited for; matrix products, arithmetic and copies ran while one was open for 13% of the time, Pallas kernels for 2%

profile of v5, /device:TPU:1, one launch (start us, length us, event | category | flops | bytes accessed | tf_op | source)
XLA Modules:
  0.0 296.5 jit_solution(4140969459655594627)
XLA Ops:
  9.3 5.5 %collective-permute-start = (bf16[96,1216]{1,0:T(8,128)(2,1)S(1)}, bf16[96,1216]{1,0:T(8,128)(2,1)S(1)}, u32[]{:S(2)}, u32[]{:S(2)}) collective-permute-start(bf16[96,1216]{1,0:T(8,128)(2,1)S(1)} %pad_maximum_fusion.8), channel_id=1, source_target_pairs={{0,256},{32,288},{64,320},{96,352},{128,384},{160,416},{192,448},{... | collective-permute-start | bytes 700424 | tf_op jit(solution)/shard_map/ppermute | solution.py:44
  20.7 12.2 %all-to-all-start = ((bf16[8,96,448]{2,1,0:T(8,128)(2,1)}), bf16[8,96,448]{2,1,0:T(8,128)(2,1)S(1)}, u32[]{:S(2)}, u32[]{:S(2)}) async-start(bf16[8,96,448]{2,1,0:T(8,128)(2,1)} %bitcast), calls=%async_computation | async-start | bytes 1572864 | tf_op jit(solution)/shard_map/all_to_all | solution.py:212
  33.0 4.9 %collective-permute-start.1 = (bf16[96,15]{1,0:T(8,128)(2,1)S(1)}, bf16[96,15]{1,0:T(8,128)(2,1)S(1)}, u32[]{:S(2)}, u32[]{:S(2)}) collective-permute-start(bf16[96,15]{1,0:T(8,128)(2,1)S(1)} %get-tuple-element.120), channel_id=1, source_target_pairs={{0,1},{1,2},{2,3},{3,4},{4,5},{5,6},{6,7},{7,8},{8,9},{9,10},{10,1... | collective-permute-start | bytes 8648 | tf_op jit(solution)/shard_map/ppermute | solution.py:174
  43.5 4.7 %collective-permute-start.3 = (bf16[96,478]{1,0:T(8,128)(2,1)S(1)}, bf16[96,478]{1,0:T(8,128)(2,1)S(1)}, u32[]{:S(2)}, u32[]{:S(2)}) collective-permute-start(bf16[96,478]{1,0:T(8,128)(2,1)S(1)} %pad_maximum_fusion.15), channel_id=1, source_target_pairs={{0,256},{32,288},{64,320},{96,352},{128,384},{160,416},{192,448},{... | collective-permute-start | bytes 275336 | tf_op jit(solution)/shard_map/ppermute | solution.py:44
  51.2 4.1 %all-to-all-done = bf16[8,96,448]{2,1,0:T(8,128)(2,1)S(1)} async-done(((bf16[8,96,448]{2,1,0:T(8,128)(2,1)}), bf16[8,96,448]{2,1,0:T(8,128)(2,1)S(1)}, u32[]{:S(2)}, u32[]{:S(2)}) %all-to-all-start) | async-done | bytes 688160 | tf_op jit(solution)/shard_map/all_to_all | solution.py:212
  60.7 4.7 %collective-permute-start.5 = (bf16[96,768]{1,0:T(8,128)(2,1)}, bf16[96,768]{1,0:T(8,128)(2,1)S(1)}, u32[]{:S(2)}, u32[]{:S(2)}) collective-permute-start(bf16[96,768]{1,0:T(8,128)(2,1)} %get-tuple-element.111), channel_id=1, source_target_pairs={{0,256},{32,288},{64,320},{96,352},{128,384},{160,416},{192,448},{... | collective-permute-start | bytes 442376 | tf_op jit(solution)/shard_map/ppermute | solution.py:44
  69.4 12.9 %all-to-all-done.1 = bf16[8,96,448]{2,1,0:T(8,128)(2,1)S(1)} async-done(((bf16[8,96,448]{2,1,0:T(8,128)(2,1)}), bf16[8,96,448]{2,1,0:T(8,128)(2,1)S(1)}, u32[]{:S(2)}, u32[]{:S(2)}) %all-to-all-start.1) | async-done | bytes 688160 | tf_op jit(solution)/shard_map/all_to_all | solution.py:223
  83.9 5.8 %collective-permute-start.6 = (f32[2,448]{1,0:T(2,128)S(1)}, f32[2,448]{1,0:T(2,128)S(1)}, u32[]{:S(2)}, u32[]{:S(2)}) collective-permute-start(f32[2,448]{1,0:T(2,128)S(1)} %pad_maximum_fusion.16), channel_id=1, source_target_pairs={{0,256},{32,288},{64,320},{96,352},{128,384},{160,416},{192,448},{... | collective-permute-start | bytes 10760 | tf_op jit(solution)/shard_map/ppermute | solution.py:44
  92.3 7.8 %collective-permute-done.7 = bf16[192,448]{0,1:T(8,128)(2,1)S(1)} collective-permute-done((bf16[192,448]{0,1:T(8,128)(2,1)S(1)}, bf16[192,448]{0,1:T(8,128)(2,1)S(1)}, u32[]{:S(2)}, u32[]{:S(2)}) %collective-permute-start.7) | collective-permute-done | bytes 172064 | tf_op jit(solution)/shard_map/ppermute | solution.py:44
  100.8 3.6 %collective-permute-start.8 = (bf16[96,30]{1,0:T(8,128)(2,1)S(1)}, bf16[96,30]{1,0:T(8,128)(2,1)S(1)}, u32[]{:S(2)}, u32[]{:S(2)}) collective-permute-start(bf16[96,30]{1,0:T(8,128)(2,1)S(1)} %get-tuple-element.118), channel_id=1, source_target_pairs={{0,1},{1,2},{2,3},{3,4},{4,5},{5,6},{6,7},{7,8},{8,9},{9,10},{10,1... | collective-permute-start | bytes 17288 | tf_op jit(solution)/shard_map/ppermute | solution.py:174
  113.5 7.6 %all-to-all-start.2 = ((f32[32,2,96]{2,1,0:T(2,128)}), f32[32,2,96]{2,1,0:T(2,128)S(1)}, u32[]{:S(2)}, u32[]{:S(2)}) async-start(f32[32,2,96]{2,1,0:T(2,128)} %broadcast_in_dim.19), calls=%async_computation.2 | async-start | bytes 65536 | tf_op jit(solution)/shard_map/all_to_all | solution.py:28
  124.9 4.2 %all-to-all-done.2 = f32[32,2,96]{2,1,0:T(2,128)S(1)} async-done(((f32[32,2,96]{2,1,0:T(2,128)}), f32[32,2,96]{2,1,0:T(2,128)S(1)}, u32[]{:S(2)}, u32[]{:S(2)}) %all-to-all-start.2) | async-done | bytes 24608 | tf_op jit(solution)/shard_map/all_to_all | solution.py:28
  132.1 8.2 %all-to-all-start.3 = ((f32[32,2,96]{2,1,0:T(2,128)}), f32[32,2,96]{2,1,0:T(2,128)S(1)}, u32[]{:S(2)}, u32[]{:S(2)}) async-start(f32[32,2,96]{2,1,0:T(2,128)} %broadcast_in_dim.20), calls=%async_computation.3 | async-start | bytes 65536 | tf_op jit(solution)/shard_map/all_to_all | solution.py:28
  142.9 5.3 %all-to-all-done.3 = f32[32,2,96]{2,1,0:T(2,128)S(1)} async-done(((f32[32,2,96]{2,1,0:T(2,128)}), f32[32,2,96]{2,1,0:T(2,128)S(1)}, u32[]{:S(2)}, u32[]{:S(2)}) %all-to-all-start.3) | async-done | bytes 24608 | tf_op jit(solution)/shard_map/all_to_all | solution.py:28
  149.1 4.7 %conv_back.1 = (bf16[2,96,448]{2,1,0:T(8,128)(2,1)}, f32[96,512]{1,0:T(8,128)}) custom-call(f32[96,6]{1,0:T(8,128)} %copy.87.consts_ref, f32[96,31]{1,0:T(8,128)} %copy.88.taps_ref, f32[1,512]{1,0:T(1,128)} %and_convert_fusion.inside_ref, f32[96,512]{1,0:T(8,128)} %pad.34.swish_ref, f32[96,512]{1,0:T(8,128)} %pad.35.conv_ref, f32[2,96,448]{2,1,0:T(8,128)} %copy-done.3), custom_call_target="tpu_custom_call" | custom-call | tf_op jit(solution)/shard_map/conv_back/pallas_call | solution.py:149
  154.9 4.3 %collective-permute-start.10 = (bf16[288,448]{1,0:T(8,128)(2,1)S(1)}, bf16[288,448]{1,0:T(8,128)(2,1)S(1)}, u32[]{:S(2)}, u32[]{:S(2)}) collective-permute-start(bf16[288,448]{1,0:T(8,128)(2,1)S(1)} %pad_maximum_fusion.5), channel_id=1, source_target_pairs={{0,256},{32,288},{64,320},{96,352},{128,384},{160,416},{192,448},{... | collective-permute-start | bytes 774152 | tf_op jit(solution)/shard_map/ppermute | solution.py:44
  159.9 6.0 %collective-permute-done.10 = bf16[288,448]{1,0:T(8,128)(2,1)S(1)} collective-permute-done((bf16[288,448]{1,0:T(8,128)(2,1)S(1)}, bf16[288,448]{1,0:T(8,128)(2,1)S(1)}, u32[]{:S(2)}, u32[]{:S(2)}) %collective-permute-start.10) | collective-permute-done | bytes 258080 | tf_op jit(solution)/shard_map/ppermute | solution.py:44
  168.9 3.7 %collective-permute-start.11 = (bf16[144,1536]{1,0:T(8,128)(2,1)}, bf16[144,1536]{1,0:T(8,128)(2,1)}, u32[]{:S(2)}, u32[]{:S(2)}) collective-permute-start(bf16[144,1536]{1,0:T(8,128)(2,1)} %dynamic-slice_convert_fusion), channel_id=1, source_target_pairs={{0,1},{1,0},{2,3},{3,2},{4,5},{5,4},{6,7},{7,6},{8,9},{9,8},{10,11... | collective-permute-start | bytes 1327112 | tf_op jit(solution)/shard_map/ppermute | solution.py:49
  175.7 3.9 %all-to-all-start.4 = ((bf16[8,96,512]{2,1,0:T(8,128)(2,1)}), bf16[8,96,512]{2,1,0:T(8,128)(2,1)S(1)}, u32[]{:S(2)}, u32[]{:S(2)}) async-start(bf16[8,96,512]{2,1,0:T(8,128)(2,1)} %line_product.1), calls=%async_computation.4 | async-start | bytes 1572864 | tf_op jit(solution)/shard_map/all_to_all | solution.py:212
  185.5 6.3 %collective-permute-done.12 = bf16[72,1536]{1,0:T(8,128)(2,1)S(1)} collective-permute-done((bf16[72,1536]{1,0:T(8,128)(2,1)}, bf16[72,1536]{1,0:T(8,128)(2,1)S(1)}, u32[]{:S(2)}, u32[]{:S(2)}) %collective-permute-start.12) | collective-permute-done | bytes 221216 | tf_op jit(solution)/shard_map/ppermute | solution.py:49
  193.5 9.8 %all-to-all-done.4 = bf16[8,96,512]{2,1,0:T(8,128)(2,1)S(1)} async-done(((bf16[8,96,512]{2,1,0:T(8,128)(2,1)}), bf16[8,96,512]{2,1,0:T(8,128)(2,1)S(1)}, u32[]{:S(2)}, u32[]{:S(2)}) %all-to-all-start.4) | async-done | bytes 786464 | tf_op jit(solution)/shard_map/all_to_all | solution.py:212
  209.0 5.1 %taps_grad.1 = f32[8,2976]{1,0:T(8,128)} custom-call(f32[96,512]{1,0:T(8,128)} %get-tuple-element.39.grad_ref, f32[96,512]{1,0:T(8,128)} %copy-done), custom_call_target="tpu_custom_call" | custom-call | tf_op jit(solution)/shard_map/taps_grad/pallas_call | solution.py:161
  217.1 4.3 %collective-permute-start.13 = (f32[2,448]{1,0:T(2,128)S(1)}, f32[2,448]{1,0:T(2,128)S(1)}, u32[]{:S(2)}, u32[]{:S(2)}) collective-permute-start(f32[2,448]{1,0:T(2,128)S(1)} %reshape.265), channel_id=1, source_target_pairs={{0,256},{32,288},{64,320},{96,352},{128,384},{160,416},{192,448},{... | collective-permute-start | bytes 10760 | tf_op jit(solution)/shard_map/ppermute | solution.py:44
  223.7 7.8 %all-to-all-done.5 = bf16[8,96,448]{2,1,0:T(8,128)(2,1)S(1)} async-done(((bf16[8,96,448]{2,1,0:T(8,128)(2,1)}), bf16[8,96,448]{2,1,0:T(8,128)(2,1)S(1)}, u32[]{:S(2)}, u32[]{:S(2)}) %all-to-all-start.5) | async-done | bytes 688160 | tf_op jit(solution)/shard_map/all_to_all | solution.py:223
  234.0 4.0 %all-to-all-start.6 = ((bf16[32,6,896]{2,1,0:T(8,128)(2,1)}), bf16[32,6,896]{2,1,0:T(8,128)(2,1)S(1)}, u32[]{:S(2)}, u32[]{:S(2)}) async-start(bf16[32,6,896]{2,1,0:T(8,128)(2,1)} %fusion.18), calls=%async_computation.7 | async-start | bytes 917504 | tf_op jit(solution)/shard_map/all_to_all | solution.py:28
  240.6 4.3 %collective-permute-start.14 = (bf16[72,768]{1,0:T(8,128)(2,1)S(1)}, bf16[72,768]{1,0:T(8,128)(2,1)S(1)}, u32[]{:S(2)}, u32[]{:S(2)}) collective-permute-start(bf16[72,768]{1,0:T(8,128)(2,1)S(1)} %slice.504), channel_id=1, source_target_pairs={{0,256},{32,288},{64,320},{96,352},{128,384},{160,416},{192,448},{... | collective-permute-start | bytes 331784 | tf_op jit(solution)/shard_map/ppermute | solution.py:44
  244.9 8.6 %all-to-all-done.6 = bf16[32,6,896]{2,1,0:T(8,128)(2,1)S(1)} async-done(((bf16[32,6,896]{2,1,0:T(8,128)(2,1)}), bf16[32,6,896]{2,1,0:T(8,128)(2,1)S(1)}, u32[]{:S(2)}, u32[]{:S(2)}) %all-to-all-start.6) | async-done | bytes 344096 | tf_op jit(solution)/shard_map/all_to_all | solution.py:28
  256.7 4.1 %collective-permute-done.16 = bf16[72,1536]{1,0:T(8,128)(2,1)S(1)} collective-permute-done((bf16[72,1536]{1,0:T(8,128)(2,1)S(1)}, bf16[72,1536]{1,0:T(8,128)(2,1)S(1)}, u32[]{:S(2)}, u32[]{:S(2)}) %collective-permute-start.16) | collective-permute-done | bytes 221216 | tf_op jit(solution)/shard_map/ppermute | solution.py:49
  261.0 4.7 %collective-permute-start.17 = (bf16[144,1536]{1,0:T(8,128)(2,1)S(1)}, bf16[144,1536]{1,0:T(8,128)(2,1)S(1)}, u32[]{:S(2)}, u32[]{:S(2)}) collective-permute-start(bf16[144,1536]{1,0:T(8,128)(2,1)S(1)} %pad_maximum_fusion.2), channel_id=1, source_target_pairs={{0,1},{1,0},{2,3},{3,2},{4,5},{5,4},{6,7},{7,6},{8,9},{9,8},{10,11... | collective-permute-start | bytes 1327112 | tf_op jit(solution)/shard_map/ppermute | solution.py:49
  266.9 4.3 %all-to-all-start.7 = ((bf16[32,6,896]{2,1,0:T(8,128)(2,1)}), bf16[32,6,896]{2,1,0:T(8,128)(2,1)S(1)}, u32[]{:S(2)}, u32[]{:S(2)}) async-start(bf16[32,6,896]{2,1,0:T(8,128)(2,1)} %broadcast_in_dim.23), calls=%async_computation.8 | async-start | bytes 917504 | tf_op jit(solution)/shard_map/all_to_all | solution.py:28
  271.4 4.7 %collective-permute-start.18 = (bf16[96,448]{1,0:T(8,128)(2,1)S(1)}, bf16[96,448]{1,0:T(8,128)(2,1)S(1)}, u32[]{:S(2)}, u32[]{:S(2)}) collective-permute-start(bf16[96,448]{1,0:T(8,128)(2,1)S(1)} %slice.757), channel_id=1, source_target_pairs={{0,256},{32,288},{64,320},{96,352},{128,384},{160,416},{192,448},{... | collective-permute-start | bytes 258056 | tf_op jit(solution)/shard_map/ppermute | solution.py:44
  281.1 5.5 %all-to-all-done.7 = bf16[32,6,896]{2,1,0:T(8,128)(2,1)S(1)} async-done(((bf16[32,6,896]{2,1,0:T(8,128)(2,1)}), bf16[32,6,896]{2,1,0:T(8,128)(2,1)S(1)}, u32[]{:S(2)}, u32[]{:S(2)}) %all-to-all-start.7) | async-done | bytes 344096 | tf_op jit(solution)/shard_map/all_to_all | solution.py:28
  (302 shorter events, 93.4 us)
Async XLA Ops:
  9.3 9.1 %collective-permute-start = (bf16[96,1216]{1,0:T(8,128)(2,1)S(1)}, bf16[96,1216]{1,0:T(8,128)(2,1)S(1)}, u32[]{:S(2)}, u32[]{:S(2)}) collective-permute-start(bf16[96,1216]{1,0:T(8,128)(2,1)S(1)} %pad_maximum_fusion.8), channel_id=1, source_target_pairs={{0,256},{32,288},{64,320},{96,352},{128,384},{160,416},{192,448},{... | collective-permute-start | bytes 700424 | tf_op jit(solution)/shard_map/ppermute | solution.py:44
  20.7 34.6 %copy-start.31 = (bf16[96,448]{1,0:T(8,128)(2,1)S(1)}, bf16[96,448]{1,0:T(8,128)(2,1)}, u32[]{:S(2)}) copy-start(bf16[96,448]{1,0:T(8,128)(2,1)} %param.12) | copy-start | bytes 258052
  20.7 34.5 %all-to-all-start = ((bf16[8,96,448]{2,1,0:T(8,128)(2,1)}), bf16[8,96,448]{2,1,0:T(8,128)(2,1)S(1)}, u32[]{:S(2)}, u32[]{:S(2)}) async-start(bf16[8,96,448]{2,1,0:T(8,128)(2,1)} %bitcast), calls=%async_computation | async-start | bytes 1572864 | tf_op jit(solution)/shard_map/all_to_all | solution.py:212
  33.0 6.8 %collective-permute-start.1 = (bf16[96,15]{1,0:T(8,128)(2,1)S(1)}, bf16[96,15]{1,0:T(8,128)(2,1)S(1)}, u32[]{:S(2)}, u32[]{:S(2)}) collective-permute-start(bf16[96,15]{1,0:T(8,128)(2,1)S(1)} %get-tuple-element.120), channel_id=1, source_target_pairs={{0,1},{1,2},{2,3},{3,4},{4,5},{5,6},{6,7},{7,8},{8,9},{9,10},{10,1... | collective-permute-start | bytes 8648 | tf_op jit(solution)/shard_map/ppermute | solution.py:174
  37.9 5.4 %collective-permute-start.2 = (bf16[96,15]{1,0:T(8,128)(2,1)S(1)}, bf16[96,15]{1,0:T(8,128)(2,1)S(1)}, u32[]{:S(2)}, u32[]{:S(2)}) collective-permute-start(bf16[96,15]{1,0:T(8,128)(2,1)S(1)} %get-tuple-element.121), channel_id=1, source_target_pairs={{1,0},{2,1},{3,2},{4,3},{5,4},{6,5},{7,6},{8,7},{9,8},{10,9},{11,1... | collective-permute-start | bytes 8648 | tf_op jit(solution)/shard_map/ppermute | solution.py:175
  43.5 6.9 %collective-permute-start.3 = (bf16[96,478]{1,0:T(8,128)(2,1)S(1)}, bf16[96,478]{1,0:T(8,128)(2,1)S(1)}, u32[]{:S(2)}, u32[]{:S(2)}) collective-permute-start(bf16[96,478]{1,0:T(8,128)(2,1)S(1)} %pad_maximum_fusion.15), channel_id=1, source_target_pairs={{0,256},{32,288},{64,320},{96,352},{128,384},{160,416},{192,448},{... | collective-permute-start | bytes 275336 | tf_op jit(solution)/shard_map/ppermute | solution.py:44
  56.4 25.9 %all-to-all-start.1 = ((bf16[8,96,448]{2,1,0:T(8,128)(2,1)}), bf16[8,96,448]{2,1,0:T(8,128)(2,1)S(1)}, u32[]{:S(2)}, u32[]{:S(2)}) async-start(bf16[8,96,448]{2,1,0:T(8,128)(2,1)} %broadcast_in_dim.17), calls=%async_computation.1 | async-start | bytes 1572864 | tf_op jit(solution)/shard_map/all_to_all | solution.py:223
  60.0 64.9 %all-gather.5.cloned.1.call-start = ((), (), s32[]{:S(2)}) async-start(), calls=%async_computation.10 | async-start | bytes 1769472 | tf_op jit(solution)/shard_map/all_gather | solution.py:254
  60.7 60.4 %collective-permute-start.5 = (bf16[96,768]{1,0:T(8,128)(2,1)}, bf16[96,768]{1,0:T(8,128)(2,1)S(1)}, u32[]{:S(2)}, u32[]{:S(2)}) collective-permute-start(bf16[96,768]{1,0:T(8,128)(2,1)} %get-tuple-element.111), channel_id=1, source_target_pairs={{0,256},{32,288},{64,320},{96,352},{128,384},{160,416},{192,448},{... | collective-permute-start | bytes 442376 | tf_op jit(solution)/shard_map/ppermute | solution.py:44
  65.7 17.1 %collective-permute-start.4 = (bf16[192,768]{0,1:T(8,128)(2,1)S(1)}, bf16[192,768]{0,1:T(8,128)(2,1)S(1)}, u32[]{:S(2)}, u32[]{:S(2)}) collective-permute-start(bf16[192,768]{0,1:T(8,128)(2,1)S(1)} %copy.98), channel_id=1, source_target_pairs={{0,256},{32,288},{64,320},{96,352},{128,384},{160,416},{192,448},{... | collective-permute-start | bytes 884744 | tf_op jit(solution)/shard_map/ppermute | solution.py:44
  69.1 31.4 %copy-start.37 = (f32[1,2,96]{2,0,1:T(1,128)}, f32[1,2,96]{2,0,1:T(1,128)S(1)}, u32[]{:S(2)}) copy-start(f32[1,2,96]{2,0,1:T(1,128)S(1)} %fusion.93) | copy-start | bytes 2308
  83.9 8.3 %collective-permute-start.6 = (f32[2,448]{1,0:T(2,128)S(1)}, f32[2,448]{1,0:T(2,128)S(1)}, u32[]{:S(2)}, u32[]{:S(2)}) collective-permute-start(f32[2,448]{1,0:T(2,128)S(1)} %pad_maximum_fusion.16), channel_id=1, source_target_pairs={{0,256},{32,288},{64,320},{96,352},{128,384},{160,416},{192,448},{... | collective-permute-start | bytes 10760 | tf_op jit(solution)/shard_map/ppermute | solution.py:44
  90.3 9.8 %collective-permute-start.7 = (bf16[192,448]{0,1:T(8,128)(2,1)S(1)}, bf16[192,448]{0,1:T(8,128)(2,1)S(1)}, u32[]{:S(2)}, u32[]{:S(2)}) collective-permute-start(bf16[192,448]{0,1:T(8,128)(2,1)S(1)} %slice.756), channel_id=1, source_target_pairs={{0,256},{32,288},{64,320},{96,352},{128,384},{160,416},{192,448},{... | collective-permute-start | bytes 516104 | tf_op jit(solution)/shard_map/ppermute | solution.py:44
  100.8 6.9 %collective-permute-start.8 = (bf16[96,30]{1,0:T(8,128)(2,1)S(1)}, bf16[96,30]{1,0:T(8,128)(2,1)S(1)}, u32[]{:S(2)}, u32[]{:S(2)}) collective-permute-start(bf16[96,30]{1,0:T(8,128)(2,1)S(1)} %get-tuple-element.118), channel_id=1, source_target_pairs={{0,1},{1,2},{2,3},{3,4},{4,5},{5,6},{6,7},{7,8},{8,9},{9,10},{10,1... | collective-permute-start | bytes 17288 | tf_op jit(solution)/shard_map/ppermute | solution.py:174
  104.4 5.5 %collective-permute-start.9 = (bf16[96,30]{1,0:T(8,128)(2,1)S(1)}, bf16[96,30]{1,0:T(8,128)(2,1)S(1)}, u32[]{:S(2)}, u32[]{:S(2)}) collective-permute-start(bf16[96,30]{1,0:T(8,128)(2,1)S(1)} %get-tuple-element.119), channel_id=1, source_target_pairs={{1,0},{2,1},{3,2},{4,3},{5,4},{6,5},{7,6},{8,7},{9,8},{10,9},{11,1... | collective-permute-start | bytes 17288 | tf_op jit(solution)/shard_map/ppermute | solution.py:175
  113.5 15.6 %all-to-all-start.2 = ((f32[32,2,96]{2,1,0:T(2,128)}), f32[32,2,96]{2,1,0:T(2,128)S(1)}, u32[]{:S(2)}, u32[]{:S(2)}) async-start(f32[32,2,96]{2,1,0:T(2,128)} %broadcast_in_dim.19), calls=%async_computation.2 | async-start | bytes 65536 | tf_op jit(solution)/shard_map/all_to_all | solution.py:28
  132.1 16.1 %all-to-all-start.3 = ((f32[32,2,96]{2,1,0:T(2,128)}), f32[32,2,96]{2,1,0:T(2,128)S(1)}, u32[]{:S(2)}, u32[]{:S(2)}) async-start(f32[32,2,96]{2,1,0:T(2,128)} %broadcast_in_dim.20), calls=%async_computation.3 | async-start | bytes 65536 | tf_op jit(solution)/shard_map/all_to_all | solution.py:28
  154.9 11.0 %collective-permute-start.10 = (bf16[288,448]{1,0:T(8,128)(2,1)S(1)}, bf16[288,448]{1,0:T(8,128)(2,1)S(1)}, u32[]{:S(2)}, u32[]{:S(2)}) collective-permute-start(bf16[288,448]{1,0:T(8,128)(2,1)S(1)} %pad_maximum_fusion.5), channel_id=1, source_target_pairs={{0,256},{32,288},{64,320},{96,352},{128,384},{160,416},{192,448},{... | collective-permute-start | bytes 774152 | tf_op jit(solution)/shard_map/ppermute | solution.py:44
  168.9 10.9 %collective-permute-start.11 = (bf16[144,1536]{1,0:T(8,128)(2,1)}, bf16[144,1536]{1,0:T(8,128)(2,1)}, u32[]{:S(2)}, u32[]{:S(2)}) collective-permute-start(bf16[144,1536]{1,0:T(8,128)(2,1)} %dynamic-slice_convert_fusion), channel_id=1, source_target_pairs={{0,1},{1,0},{2,3},{3,2},{4,5},{5,4},{6,7},{7,6},{8,9},{9,8},{10,11... | collective-permute-start | bytes 1327112 | tf_op jit(solution)/shard_map/ppermute | solution.py:49
  175.7 27.6 %all-to-all-start.4 = ((bf16[8,96,512]{2,1,0:T(8,128)(2,1)}), bf16[8,96,512]{2,1,0:T(8,128)(2,1)S(1)}, u32[]{:S(2)}, u32[]{:S(2)}) async-start(bf16[8,96,512]{2,1,0:T(8,128)(2,1)} %line_product.1), calls=%async_computation.4 | async-start | bytes 1572864 | tf_op jit(solution)/shard_map/all_to_all | solution.py:212
  179.6 59.2 %all-gather.7.cloned.1.call-start = ((), (), s32[]{:S(2)}) async-start(), calls=%async_computation.11 | async-start | bytes 1990656 | tf_op jit(solution)/shard_map/all_gather | solution.py:388
  182.9 8.8 %collective-permute-start.12 = (bf16[72,1536]{1,0:T(8,128)(2,1)}, bf16[72,1536]{1,0:T(8,128)(2,1)S(1)}, u32[]{:S(2)}, u32[]{:S(2)}) collective-permute-start(bf16[72,1536]{1,0:T(8,128)(2,1)} %dynamic-slice_convert_fusion.1), channel_id=1, source_target_pairs={{0,16},{1,17},{2,18},{3,19},{4,20},{5,21},{6,22},{7,23},{8,24},{9,... | collective-permute-start | bytes 663560 | tf_op jit(solution)/shard_map/ppermute | solution.py:49
  204.4 27.1 %all-to-all-start.5 = ((bf16[8,96,448]{2,1,0:T(8,128)(2,1)}), bf16[8,96,448]{2,1,0:T(8,128)(2,1)S(1)}, u32[]{:S(2)}, u32[]{:S(2)}) async-start(bf16[8,96,448]{2,1,0:T(8,128)(2,1)} %broadcast_in_dim.21), calls=%async_computation.5 | async-start | bytes 1572864 | tf_op jit(solution)/shard_map/all_to_all | solution.py:223
  217.1 6.6 %collective-permute-start.13 = (f32[2,448]{1,0:T(2,128)S(1)}, f32[2,448]{1,0:T(2,128)S(1)}, u32[]{:S(2)}, u32[]{:S(2)}) collective-permute-start(f32[2,448]{1,0:T(2,128)S(1)} %reshape.265), channel_id=1, source_target_pairs={{0,256},{32,288},{64,320},{96,352},{128,384},{160,416},{192,448},{... | collective-permute-start | bytes 10760 | tf_op jit(solution)/shard_map/ppermute | solution.py:44
  234.0 19.5 %all-to-all-start.6 = ((bf16[32,6,896]{2,1,0:T(8,128)(2,1)}), bf16[32,6,896]{2,1,0:T(8,128)(2,1)S(1)}, u32[]{:S(2)}, u32[]{:S(2)}) async-start(bf16[32,6,896]{2,1,0:T(8,128)(2,1)} %fusion.18), calls=%async_computation.7 | async-start | bytes 917504 | tf_op jit(solution)/shard_map/all_to_all | solution.py:28
  238.0 50.4 %reduce-scatter.2.cloned.1.call-start = ((), (), s32[]{:S(2)}) async-start(), calls=%async_computation.9 | async-start | bytes 2654208 | tf_op jit(solution)/shard_map/reduce_scatter | solution.py:399
  240.6 13.1 %collective-permute-start.14 = (bf16[72,768]{1,0:T(8,128)(2,1)S(1)}, bf16[72,768]{1,0:T(8,128)(2,1)S(1)}, u32[]{:S(2)}, u32[]{:S(2)}) collective-permute-start(bf16[72,768]{1,0:T(8,128)(2,1)S(1)} %slice.504), channel_id=1, source_target_pairs={{0,256},{32,288},{64,320},{96,352},{128,384},{160,416},{192,448},{... | collective-permute-start | bytes 331784 | tf_op jit(solution)/shard_map/ppermute | solution.py:44
  253.8 7.1 %collective-permute-start.16 = (bf16[72,1536]{1,0:T(8,128)(2,1)S(1)}, bf16[72,1536]{1,0:T(8,128)(2,1)S(1)}, u32[]{:S(2)}, u32[]{:S(2)}) collective-permute-start(bf16[72,1536]{1,0:T(8,128)(2,1)S(1)} %maximum_select_fusion), channel_id=1, source_target_pairs={{0,16},{1,17},{2,18},{3,19},{4,20},{5,21},{6,22},{7,23},{8,24},{9,... | collective-permute-start | bytes 663560 | tf_op jit(solution)/shard_map/ppermute | solution.py:49
  256.1 4.9 %collective-permute-start.15 = (bf16[6,896]{1,0:T(8,128)(2,1)S(1)}, bf16[6,896]{1,0:T(8,128)(2,1)S(1)}, u32[]{:S(2)}, u32[]{:S(2)}) collective-permute-start(bf16[6,896]{1,0:T(8,128)(2,1)S(1)} %reduce_sum.174), channel_id=1, source_target_pairs={{16,256},{17,257},{18,258},{19,259},{20,260},{21,261},{22,262},{23... | collective-permute-start | bytes 32264 | tf_op jit(solution)/shard_map/ppermute | solution.py:442
  261.0 10.3 %collective-permute-start.17 = (bf16[144,1536]{1,0:T(8,128)(2,1)S(1)}, bf16[144,1536]{1,0:T(8,128)(2,1)S(1)}, u32[]{:S(2)}, u32[]{:S(2)}) collective-permute-start(bf16[144,1536]{1,0:T(8,128)(2,1)S(1)} %pad_maximum_fusion.2), channel_id=1, source_target_pairs={{0,1},{1,0},{2,3},{3,2},{4,5},{5,4},{6,7},{7,6},{8,9},{9,8},{10,11... | collective-permute-start | bytes 1327112 | tf_op jit(solution)/shard_map/ppermute | solution.py:49
  266.9 19.7 %all-to-all-start.7 = ((bf16[32,6,896]{2,1,0:T(8,128)(2,1)}), bf16[32,6,896]{2,1,0:T(8,128)(2,1)S(1)}, u32[]{:S(2)}, u32[]{:S(2)}) async-start(bf16[32,6,896]{2,1,0:T(8,128)(2,1)} %broadcast_in_dim.23), calls=%async_computation.8 | async-start | bytes 917504 | tf_op jit(solution)/shard_map/all_to_all | solution.py:28
  271.4 9.0 %collective-permute-start.18 = (bf16[96,448]{1,0:T(8,128)(2,1)S(1)}, bf16[96,448]{1,0:T(8,128)(2,1)S(1)}, u32[]{:S(2)}, u32[]{:S(2)}) collective-permute-start(bf16[96,448]{1,0:T(8,128)(2,1)S(1)} %slice.757), channel_id=1, source_target_pairs={{0,256},{32,288},{64,320},{96,352},{128,384},{160,416},{192,448},{... | collective-permute-start | bytes 258056 | tf_op jit(solution)/shard_map/ppermute | solution.py:44
  (63 other events, 538.6 us)
Sparse Core Ops, SparseCore 0:
  90.4 34.4 all-gather.4
  203.6 30.0 all-gather.6
  241.7 42.1 reduce-scatter.1

commit v6 on v5

--- a/solution.py
+++ b/solution.py
@@ -367,12 +367,16 @@
     frame_sums = jnp.pad(
         frame_sums.astype(bf16).reshape(sum_rows, spare), ((0, rows - sum_rows), (0, 0))
     )
-    normed_rows = line_exchange(line_product(glu_turned, pair_both, frame_sums, line))
+    normed_chunks = line_product(glu_turned, pair_both, frame_sums, line)
+    normed_chunks, pair_after, swished_after = lax.optimization_barrier(
+        (normed_chunks, pair_both, swished)
+    )
+    normed_rows = line_exchange(normed_chunks)
 
     standard = (half_float - frame_mean) * frame_rstd
     normed_half = (standard * side_half(gain_col) + side_half(bias_col)).astype(bf16)
-    proj_part = contract_last(jnp.pad(swished, ((0, 0), (half, half))), grad_full)
-    glu_part = contract_last(pair_both, normed_half)
+    proj_part = contract_last(jnp.pad(swished_after, ((0, 0), (half, half))), grad_full)
+    glu_part = contract_last(pair_after, normed_half)
     glu_part = jnp.concatenate([glu_part[: 2 * rows], glu_part[2 * rows :]], axis=1)
     early = jnp.concatenate([proj_part, glu_part])
     kernel_part = taps_grad(grad_wide, widened, taps, frames)

time: 299 us -> 301 us (level)
  local copies, waits for them, and re-layouts: 26.9 us -> 30.4 us
  waiting for transfers between devices: 99.3 us -> 95.8 us
  other arithmetic: 21.8 us -> 25 us
    ppermute x10, waiting for transfers between devices: 21.2 us -> 16.1 us  [across(): lax.ppermute(operand, 'head', [(i, (i + count // 2) % count) for i in ran...]
    unnamed x135 -> x153, local copies, waits for them, and re-layouts: 4.88 us -> 6.65 us
  transfers between devices with their start and end apart: 30 -> 30, of which waited for: 18 -> 17; matrix products, arithmetic and copies ran while one was open for 13% -> 15% of each run, Pallas kernels for 2% -> 2%
where the time goes in v6:
time: 301 us; the launch traced here: 299 us
  starting transfers between devices  115 us (38%)
  waiting for transfers between devices  95.8 us (32%)
  local copies, waits for them, and re-layouts  30.4 us (10%)
  other arithmetic  25 us (8%)
  between operations  15.6 us (5%)
  Pallas kernels  11.2 us (4%)
  matrix products  6.26 us (2%)
    ppermute x10, starting transfers between devices, across(): lax.ppermute(operand, 'head', [(i, (i + count // 2) % count) for i in ran...  42.5 us
    all_to_all x4, waiting for transfers between devices, exchange(): return lax.all_to_all(blocks, axis, 0, 0, tiled=True)  25.8 us
    all_to_all x4, starting transfers between devices, exchange(): return lax.all_to_all(blocks, axis, 0, 0, tiled=True)  21.5 us
    all_to_all x2, waiting for transfers between devices, line_gather(): lax.all_to_all(jnp.broadcast_to(block[None], (line, *block.shape)), 'head...  21.2 us
    ppermute x10, waiting for transfers between devices, across(): lax.ppermute(operand, 'head', [(i, (i + count // 2) % count) for i in ran...  16.1 us
    all_to_all x2, starting transfers between devices, line_exchange(): lax.all_to_all(blocks, 'head', 0, 0, tiled=True, axis_index_groups=line_g...  15.9 us
    all_to_all x2, waiting for transfers between devices, line_exchange(): lax.all_to_all(blocks, 'head', 0, 0, tiled=True, axis_index_groups=line_g...  13.9 us
    ppermute x4, starting transfers between devices, swap_bit(): return lax.ppermute(operand, 'seq', [(i, i ^ bit) for i in range(count)])  13.2 us
  transfers between devices with their start and end apart: 30, of which 17 were waited for; matrix products, arithmetic and copies ran while one was open for 15% of the time, Pallas kernels for 2%

profile of v6, /device:TPU:1, one launch (start us, length us, event | category | flops | bytes accessed | tf_op | source)
XLA Modules:
  0.0 299.0 jit_solution(4778811962753267367)
XLA Ops:
  9.3 5.5 %collective-permute-start = (bf16[96,1216]{1,0:T(8,128)(2,1)S(1)}, bf16[96,1216]{1,0:T(8,128)(2,1)S(1)}, u32[]{:S(2)}, u32[]{:S(2)}) collective-permute-start(bf16[96,1216]{1,0:T(8,128)(2,1)S(1)} %pad_maximum_fusion.8), channel_id=1, source_target_pairs={{0,256},{32,288},{64,320},{96,352},{128,384},{160,416},{192,448},{... | collective-permute-start | bytes 700424 | tf_op jit(solution)/shard_map/ppermute | solution.py:44
  20.7 12.0 %all-to-all-start = ((bf16[8,96,448]{2,1,0:T(8,128)(2,1)}), bf16[8,96,448]{2,1,0:T(8,128)(2,1)S(1)}, u32[]{:S(2)}, u32[]{:S(2)}) async-start(bf16[8,96,448]{2,1,0:T(8,128)(2,1)} %bitcast), calls=%async_computation | async-start | bytes 1572864 | tf_op jit(solution)/shard_map/all_to_all | solution.py:212
  32.9 4.9 %collective-permute-start.1 = (bf16[96,15]{1,0:T(8,128)(2,1)S(1)}, bf16[96,15]{1,0:T(8,128)(2,1)S(1)}, u32[]{:S(2)}, u32[]{:S(2)}) collective-permute-start(bf16[96,15]{1,0:T(8,128)(2,1)S(1)} %get-tuple-element.126), channel_id=1, source_target_pairs={{0,1},{1,2},{2,3},{3,4},{4,5},{5,6},{6,7},{7,8},{8,9},{9,10},{10,1... | collective-permute-start | bytes 8648 | tf_op jit(solution)/shard_map/ppermute | solution.py:174
  43.3 4.7 %collective-permute-start.3 = (bf16[96,478]{1,0:T(8,128)(2,1)S(1)}, bf16[96,478]{1,0:T(8,128)(2,1)S(1)}, u32[]{:S(2)}, u32[]{:S(2)}) collective-permute-start(bf16[96,478]{1,0:T(8,128)(2,1)S(1)} %pad_maximum_fusion.15), channel_id=1, source_target_pairs={{0,256},{32,288},{64,320},{96,352},{128,384},{160,416},{192,448},{... | collective-permute-start | bytes 275336 | tf_op jit(solution)/shard_map/ppermute | solution.py:44
  51.0 4.1 %all-to-all-done = bf16[8,96,448]{2,1,0:T(8,128)(2,1)S(1)} async-done(((bf16[8,96,448]{2,1,0:T(8,128)(2,1)}), bf16[8,96,448]{2,1,0:T(8,128)(2,1)S(1)}, u32[]{:S(2)}, u32[]{:S(2)}) %all-to-all-start) | async-done | bytes 688160 | tf_op jit(solution)/shard_map/all_to_all | solution.py:212
  60.9 4.7 %collective-permute-start.4 = (bf16[192,768]{0,1:T(8,128)(2,1)S(1)}, bf16[192,768]{0,1:T(8,128)(2,1)S(1)}, u32[]{:S(2)}, u32[]{:S(2)}) collective-permute-start(bf16[192,768]{0,1:T(8,128)(2,1)S(1)} %copy.98), channel_id=1, source_target_pairs={{0,256},{32,288},{64,320},{96,352},{128,384},{160,416},{192,448},{... | collective-permute-start | bytes 884744 | tf_op jit(solution)/shard_map/ppermute | solution.py:44
  68.9 14.0 %all-to-all-done.1 = bf16[8,96,448]{2,1,0:T(8,128)(2,1)S(1)} async-done(((bf16[8,96,448]{2,1,0:T(8,128)(2,1)}), bf16[8,96,448]{2,1,0:T(8,128)(2,1)S(1)}, u32[]{:S(2)}, u32[]{:S(2)}) %all-to-all-start.1) | async-done | bytes 688160 | tf_op jit(solution)/shard_map/all_to_all | solution.py:223
  84.5 5.9 %collective-permute-start.6 = (f32[2,448]{1,0:T(2,128)S(1)}, f32[2,448]{1,0:T(2,128)S(1)}, u32[]{:S(2)}, u32[]{:S(2)}) collective-permute-start(f32[2,448]{1,0:T(2,128)S(1)} %pad_maximum_fusion.16), channel_id=1, source_target_pairs={{0,256},{32,288},{64,320},{96,352},{128,384},{160,416},{192,448},{... | collective-permute-start | bytes 10760 | tf_op jit(solution)/shard_map/ppermute | solution.py:44
  95.5 6.6 %collective-permute-done.7 = bf16[192,448]{0,1:T(8,128)(2,1)S(1)} collective-permute-done((bf16[192,448]{0,1:T(8,128)(2,1)S(1)}, bf16[192,448]{0,1:T(8,128)(2,1)S(1)}, u32[]{:S(2)}, u32[]{:S(2)}) %collective-permute-start.7) | collective-permute-done | bytes 172064 | tf_op jit(solution)/shard_map/ppermute | solution.py:44
  103.7 4.6 %collective-permute-start.8 = (bf16[96,30]{1,0:T(8,128)(2,1)S(1)}, bf16[96,30]{1,0:T(8,128)(2,1)S(1)}, u32[]{:S(2)}, u32[]{:S(2)}) collective-permute-start(bf16[96,30]{1,0:T(8,128)(2,1)S(1)} %get-tuple-element.124), channel_id=1, source_target_pairs={{0,1},{1,2},{2,3},{3,4},{4,5},{5,6},{6,7},{7,8},{8,9},{9,10},{10,1... | collective-permute-start | bytes 17288 | tf_op jit(solution)/shard_map/ppermute | solution.py:174
  117.6 7.2 %all-to-all-start.2 = ((f32[32,2,96]{2,1,0:T(2,128)}), f32[32,2,96]{2,1,0:T(2,128)S(1)}, u32[]{:S(2)}, u32[]{:S(2)}) async-start(f32[32,2,96]{2,1,0:T(2,128)} %broadcast_in_dim.19), calls=%async_computation.2 | async-start | bytes 65536 | tf_op jit(solution)/shard_map/all_to_all | solution.py:28
  126.4 6.4 %all-to-all-done.2 = f32[32,2,96]{2,1,0:T(2,128)S(1)} async-done(((f32[32,2,96]{2,1,0:T(2,128)}), f32[32,2,96]{2,1,0:T(2,128)S(1)}, u32[]{:S(2)}, u32[]{:S(2)}) %all-to-all-start.2) | async-done | bytes 24608 | tf_op jit(solution)/shard_map/all_to_all | solution.py:28
  135.8 6.0 %all-to-all-start.3 = ((f32[32,2,96]{2,1,0:T(2,128)}), f32[32,2,96]{2,1,0:T(2,128)S(1)}, u32[]{:S(2)}, u32[]{:S(2)}) async-start(f32[32,2,96]{2,1,0:T(2,128)} %broadcast_in_dim.20), calls=%async_computation.3 | async-start | bytes 65536 | tf_op jit(solution)/shard_map/all_to_all | solution.py:28
  144.5 5.3 %all-to-all-done.3 = f32[32,2,96]{2,1,0:T(2,128)S(1)} async-done(((f32[32,2,96]{2,1,0:T(2,128)}), f32[32,2,96]{2,1,0:T(2,128)S(1)}, u32[]{:S(2)}, u32[]{:S(2)}) %all-to-all-start.3) | async-done | bytes 24608 | tf_op jit(solution)/shard_map/all_to_all | solution.py:28
  151.1 4.6 %conv_back.1 = (bf16[2,96,448]{2,1,0:T(8,128)(2,1)}, f32[96,512]{1,0:T(8,128)}) custom-call(f32[96,6]{1,0:T(8,128)} %copy.87.consts_ref, f32[96,31]{1,0:T(8,128)} %copy.88.taps_ref, f32[1,512]{1,0:T(1,128)} %and_convert_fusion.inside_ref, f32[96,512]{1,0:T(8,128)} %pad.34.swish_ref, f32[96,512]{1,0:T(8,128)} %pad.35.conv_ref, f32[2,96,448]{2,1,0:T(8,128)} %copy-done.3), custom_call_target="tpu_custom_call" | custom-call | tf_op jit(solution)/shard_map/conv_back/pallas_call | solution.py:149
  157.5 4.3 %collective-permute-start.10 = (bf16[288,448]{1,0:T(8,128)(2,1)}, bf16[288,448]{1,0:T(8,128)(2,1)S(1)}, u32[]{:S(2)}, u32[]{:S(2)}) collective-permute-start(bf16[288,448]{1,0:T(8,128)(2,1)} %pad_maximum_fusion.5), channel_id=1, source_target_pairs={{0,256},{32,288},{64,320},{96,352},{128,384},{160,416},{192,448},{... | collective-permute-start | bytes 774152 | tf_op jit(solution)/shard_map/ppermute | solution.py:44
  164.4 4.3 %collective-permute-done.10 = bf16[288,448]{1,0:T(8,128)(2,1)S(1)} collective-permute-done((bf16[288,448]{1,0:T(8,128)(2,1)}, bf16[288,448]{1,0:T(8,128)(2,1)S(1)}, u32[]{:S(2)}, u32[]{:S(2)}) %collective-permute-start.10) | collective-permute-done | bytes 258080 | tf_op jit(solution)/shard_map/ppermute | solution.py:44
  174.2 3.7 %collective-permute-start.11 = (bf16[144,1536]{1,0:T(8,128)(2,1)}, bf16[144,1536]{1,0:T(8,128)(2,1)}, u32[]{:S(2)}, u32[]{:S(2)}) collective-permute-start(bf16[144,1536]{1,0:T(8,128)(2,1)} %dynamic-slice_convert_fusion), channel_id=1, source_target_pairs={{0,1},{1,0},{2,3},{3,2},{4,5},{5,4},{6,7},{7,6},{8,9},{9,8},{10,11... | collective-permute-start | bytes 1327112 | tf_op jit(solution)/shard_map/ppermute | solution.py:49
  178.0 3.9 %all-to-all-start.4 = ((bf16[8,96,512]{2,1,0:T(8,128)(2,1)}), bf16[8,96,512]{2,1,0:T(8,128)(2,1)S(1)}, u32[]{:S(2)}, u32[]{:S(2)}) async-start(bf16[8,96,512]{2,1,0:T(8,128)(2,1)} %line_product.1), calls=%async_computation.4 | async-start | bytes 1572864 | tf_op jit(solution)/shard_map/all_to_all | solution.py:212
  187.7 6.3 %collective-permute-done.12 = bf16[72,1536]{1,0:T(8,128)(2,1)S(1)} collective-permute-done((bf16[72,1536]{1,0:T(8,128)(2,1)}, bf16[72,1536]{1,0:T(8,128)(2,1)S(1)}, u32[]{:S(2)}, u32[]{:S(2)}) %collective-permute-start.12) | collective-permute-done | bytes 221216 | tf_op jit(solution)/shard_map/ppermute | solution.py:49
  195.7 9.8 %all-to-all-done.4 = bf16[8,96,512]{2,1,0:T(8,128)(2,1)S(1)} async-done(((bf16[8,96,512]{2,1,0:T(8,128)(2,1)}), bf16[8,96,512]{2,1,0:T(8,128)(2,1)S(1)}, u32[]{:S(2)}, u32[]{:S(2)}) %all-to-all-start.4) | async-done | bytes 786464 | tf_op jit(solution)/shard_map/all_to_all | solution.py:212
  211.2 5.1 %taps_grad.1 = f32[8,2976]{1,0:T(8,128)} custom-call(f32[96,512]{1,0:T(8,128)} %get-tuple-element.45.grad_ref, f32[96,512]{1,0:T(8,128)} %copy-done), custom_call_target="tpu_custom_call" | custom-call | tf_op jit(solution)/shard_map/taps_grad/pallas_call | solution.py:161
  220.0 4.3 %collective-permute-start.13 = (f32[2,448]{1,0:T(2,128)S(1)}, f32[2,448]{1,0:T(2,128)S(1)}, u32[]{:S(2)}, u32[]{:S(2)}) collective-permute-start(f32[2,448]{1,0:T(2,128)S(1)} %reshape.265), channel_id=1, source_target_pairs={{0,256},{32,288},{64,320},{96,352},{128,384},{160,416},{192,448},{... | collective-permute-start | bytes 10760 | tf_op jit(solution)/shard_map/ppermute | solution.py:44
  226.6 7.1 %all-to-all-done.5 = bf16[8,96,448]{2,1,0:T(8,128)(2,1)S(1)} async-done(((bf16[8,96,448]{2,1,0:T(8,128)(2,1)}), bf16[8,96,448]{2,1,0:T(8,128)(2,1)S(1)}, u32[]{:S(2)}, u32[]{:S(2)}) %all-to-all-start.5) | async-done | bytes 688160 | tf_op jit(solution)/shard_map/all_to_all | solution.py:223
  236.5 4.0 %all-to-all-start.6 = ((bf16[32,6,896]{2,1,0:T(8,128)(2,1)}), bf16[32,6,896]{2,1,0:T(8,128)(2,1)S(1)}, u32[]{:S(2)}, u32[]{:S(2)}) async-start(bf16[32,6,896]{2,1,0:T(8,128)(2,1)} %fusion.18), calls=%async_computation.7 | async-start | bytes 917504 | tf_op jit(solution)/shard_map/all_to_all | solution.py:28
  243.1 4.3 %collective-permute-start.14 = (bf16[72,768]{1,0:T(8,128)(2,1)S(1)}, bf16[72,768]{1,0:T(8,128)(2,1)S(1)}, u32[]{:S(2)}, u32[]{:S(2)}) collective-permute-start(bf16[72,768]{1,0:T(8,128)(2,1)S(1)} %slice.504), channel_id=1, source_target_pairs={{0,256},{32,288},{64,320},{96,352},{128,384},{160,416},{192,448},{... | collective-permute-start | bytes 331784 | tf_op jit(solution)/shard_map/ppermute | solution.py:44
  247.4 8.6 %all-to-all-done.6 = bf16[32,6,896]{2,1,0:T(8,128)(2,1)S(1)} async-done(((bf16[32,6,896]{2,1,0:T(8,128)(2,1)}), bf16[32,6,896]{2,1,0:T(8,128)(2,1)S(1)}, u32[]{:S(2)}, u32[]{:S(2)}) %all-to-all-start.6) | async-done | bytes 344096 | tf_op jit(solution)/shard_map/all_to_all | solution.py:28
  259.3 4.1 %collective-permute-done.16 = bf16[72,1536]{1,0:T(8,128)(2,1)S(1)} collective-permute-done((bf16[72,1536]{1,0:T(8,128)(2,1)S(1)}, bf16[72,1536]{1,0:T(8,128)(2,1)S(1)}, u32[]{:S(2)}, u32[]{:S(2)}) %collective-permute-start.16) | collective-permute-done | bytes 221216 | tf_op jit(solution)/shard_map/ppermute | solution.py:49
  263.5 4.7 %collective-permute-start.17 = (bf16[144,1536]{1,0:T(8,128)(2,1)S(1)}, bf16[144,1536]{1,0:T(8,128)(2,1)S(1)}, u32[]{:S(2)}, u32[]{:S(2)}) collective-permute-start(bf16[144,1536]{1,0:T(8,128)(2,1)S(1)} %pad_maximum_fusion.2), channel_id=1, source_target_pairs={{0,1},{1,0},{2,3},{3,2},{4,5},{5,4},{6,7},{7,6},{8,9},{9,8},{10,11... | collective-permute-start | bytes 1327112 | tf_op jit(solution)/shard_map/ppermute | solution.py:49
  269.4 4.3 %all-to-all-start.7 = ((bf16[32,6,896]{2,1,0:T(8,128)(2,1)}), bf16[32,6,896]{2,1,0:T(8,128)(2,1)S(1)}, u32[]{:S(2)}, u32[]{:S(2)}) async-start(bf16[32,6,896]{2,1,0:T(8,128)(2,1)} %broadcast_in_dim.23), calls=%async_computation.8 | async-start | bytes 917504 | tf_op jit(solution)/shard_map/all_to_all | solution.py:28
  273.9 4.8 %collective-permute-start.18 = (bf16[96,448]{1,0:T(8,128)(2,1)S(1)}, bf16[96,448]{1,0:T(8,128)(2,1)S(1)}, u32[]{:S(2)}, u32[]{:S(2)}) collective-permute-start(bf16[96,448]{1,0:T(8,128)(2,1)S(1)} %slice.757), channel_id=1, source_target_pairs={{0,256},{32,288},{64,320},{96,352},{128,384},{160,416},{192,448},{... | collective-permute-start | bytes 258056 | tf_op jit(solution)/shard_map/ppermute | solution.py:44
  283.5 5.5 %all-to-all-done.7 = bf16[32,6,896]{2,1,0:T(8,128)(2,1)S(1)} async-done(((bf16[32,6,896]{2,1,0:T(8,128)(2,1)}), bf16[32,6,896]{2,1,0:T(8,128)(2,1)S(1)}, u32[]{:S(2)}, u32[]{:S(2)}) %all-to-all-start.7) | async-done | bytes 344096 | tf_op jit(solution)/shard_map/all_to_all | solution.py:28
  (320 shorter events, 97.6 us)
Async XLA Ops:
  9.3 9.1 %collective-permute-start = (bf16[96,1216]{1,0:T(8,128)(2,1)S(1)}, bf16[96,1216]{1,0:T(8,128)(2,1)S(1)}, u32[]{:S(2)}, u32[]{:S(2)}) collective-permute-start(bf16[96,1216]{1,0:T(8,128)(2,1)S(1)} %pad_maximum_fusion.8), channel_id=1, source_target_pairs={{0,256},{32,288},{64,320},{96,352},{128,384},{160,416},{192,448},{... | collective-permute-start | bytes 700424 | tf_op jit(solution)/shard_map/ppermute | solution.py:44
  19.6 28.4 %copy-start.9 = (bf16[96,1536]{1,0:T(8,128)(2,1)S(1)}, bf16[96,1536]{1,0:T(8,128)(2,1)}, u32[]{:S(2)}) copy-start(bf16[96,1536]{1,0:T(8,128)(2,1)} %param.20) | copy-start | bytes 884740
  20.7 34.4 %all-to-all-start = ((bf16[8,96,448]{2,1,0:T(8,128)(2,1)}), bf16[8,96,448]{2,1,0:T(8,128)(2,1)S(1)}, u32[]{:S(2)}, u32[]{:S(2)}) async-start(bf16[8,96,448]{2,1,0:T(8,128)(2,1)} %bitcast), calls=%async_computation | async-start | bytes 1572864 | tf_op jit(solution)/shard_map/all_to_all | solution.py:212
  32.8 22.5 %copy-start.26 = (bf16[96,448]{1,0:T(8,128)(2,1)S(1)}, bf16[96,448]{1,0:T(8,128)(2,1)}, u32[]{:S(2)}) copy-start(bf16[96,448]{1,0:T(8,128)(2,1)} %param.12) | copy-start | bytes 258052
  32.9 6.8 %collective-permute-start.1 = (bf16[96,15]{1,0:T(8,128)(2,1)S(1)}, bf16[96,15]{1,0:T(8,128)(2,1)S(1)}, u32[]{:S(2)}, u32[]{:S(2)}) collective-permute-start(bf16[96,15]{1,0:T(8,128)(2,1)S(1)} %get-tuple-element.126), channel_id=1, source_target_pairs={{0,1},{1,2},{2,3},{3,4},{4,5},{5,6},{6,7},{7,8},{8,9},{9,10},{10,1... | collective-permute-start | bytes 8648 | tf_op jit(solution)/shard_map/ppermute | solution.py:174
  37.8 5.4 %collective-permute-start.2 = (bf16[96,15]{1,0:T(8,128)(2,1)S(1)}, bf16[96,15]{1,0:T(8,128)(2,1)S(1)}, u32[]{:S(2)}, u32[]{:S(2)}) collective-permute-start(bf16[96,15]{1,0:T(8,128)(2,1)S(1)} %get-tuple-element.127), channel_id=1, source_target_pairs={{1,0},{2,1},{3,2},{4,3},{5,4},{6,5},{7,6},{8,7},{9,8},{10,9},{11,1... | collective-permute-start | bytes 8648 | tf_op jit(solution)/shard_map/ppermute | solution.py:175
  43.3 6.9 %collective-permute-start.3 = (bf16[96,478]{1,0:T(8,128)(2,1)S(1)}, bf16[96,478]{1,0:T(8,128)(2,1)S(1)}, u32[]{:S(2)}, u32[]{:S(2)}) collective-permute-start(bf16[96,478]{1,0:T(8,128)(2,1)S(1)} %pad_maximum_fusion.15), channel_id=1, source_target_pairs={{0,256},{32,288},{64,320},{96,352},{128,384},{160,416},{192,448},{... | collective-permute-start | bytes 275336 | tf_op jit(solution)/shard_map/ppermute | solution.py:44
  48.0 62.2 %collective-permute-start.5 = (bf16[96,768]{1,0:T(8,128)(2,1)S(1)}, bf16[96,768]{1,0:T(8,128)(2,1)S(1)}, u32[]{:S(2)}, u32[]{:S(2)}) collective-permute-start(bf16[96,768]{1,0:T(8,128)(2,1)S(1)} %get-tuple-element.117), channel_id=1, source_target_pairs={{0,256},{32,288},{64,320},{96,352},{128,384},{160,416},{192,448},{... | collective-permute-start | bytes 442376 | tf_op jit(solution)/shard_map/ppermute | solution.py:44
  56.9 26.1 %all-to-all-start.1 = ((bf16[8,96,448]{2,1,0:T(8,128)(2,1)}), bf16[8,96,448]{2,1,0:T(8,128)(2,1)S(1)}, u32[]{:S(2)}, u32[]{:S(2)}) async-start(bf16[8,96,448]{2,1,0:T(8,128)(2,1)} %broadcast_in_dim.17), calls=%async_computation.1 | async-start | bytes 1572864 | tf_op jit(solution)/shard_map/all_to_all | solution.py:223
  60.6 65.8 %all-gather.5.cloned.1.call-start = ((), (), s32[]{:S(2)}) async-start(), calls=%async_computation.10 | async-start | bytes 1769472 | tf_op jit(solution)/shard_map/all_gather | solution.py:254
  60.9 22.5 %collective-permute-start.4 = (bf16[192,768]{0,1:T(8,128)(2,1)S(1)}, bf16[192,768]{0,1:T(8,128)(2,1)S(1)}, u32[]{:S(2)}, u32[]{:S(2)}) collective-permute-start(bf16[192,768]{0,1:T(8,128)(2,1)S(1)} %copy.98), channel_id=1, source_target_pairs={{0,256},{32,288},{64,320},{96,352},{128,384},{160,416},{192,448},{... | collective-permute-start | bytes 884744 | tf_op jit(solution)/shard_map/ppermute | solution.py:44
  84.5 9.8 %collective-permute-start.6 = (f32[2,448]{1,0:T(2,128)S(1)}, f32[2,448]{1,0:T(2,128)S(1)}, u32[]{:S(2)}, u32[]{:S(2)}) collective-permute-start(f32[2,448]{1,0:T(2,128)S(1)} %pad_maximum_fusion.16), channel_id=1, source_target_pairs={{0,256},{32,288},{64,320},{96,352},{128,384},{160,416},{192,448},{... | collective-permute-start | bytes 10760 | tf_op jit(solution)/shard_map/ppermute | solution.py:44
  92.4 9.8 %collective-permute-start.7 = (bf16[192,448]{0,1:T(8,128)(2,1)S(1)}, bf16[192,448]{0,1:T(8,128)(2,1)S(1)}, u32[]{:S(2)}, u32[]{:S(2)}) collective-permute-start(bf16[192,448]{0,1:T(8,128)(2,1)S(1)} %slice.756), channel_id=1, source_target_pairs={{0,256},{32,288},{64,320},{96,352},{128,384},{160,416},{192,448},{... | collective-permute-start | bytes 516104 | tf_op jit(solution)/shard_map/ppermute | solution.py:44
  103.7 7.3 %collective-permute-start.8 = (bf16[96,30]{1,0:T(8,128)(2,1)S(1)}, bf16[96,30]{1,0:T(8,128)(2,1)S(1)}, u32[]{:S(2)}, u32[]{:S(2)}) collective-permute-start(bf16[96,30]{1,0:T(8,128)(2,1)S(1)} %get-tuple-element.124), channel_id=1, source_target_pairs={{0,1},{1,2},{2,3},{3,4},{4,5},{5,6},{6,7},{7,8},{8,9},{9,10},{10,1... | collective-permute-start | bytes 17288 | tf_op jit(solution)/shard_map/ppermute | solution.py:174
  108.3 5.5 %collective-permute-start.9 = (bf16[96,30]{1,0:T(8,128)(2,1)S(1)}, bf16[96,30]{1,0:T(8,128)(2,1)S(1)}, u32[]{:S(2)}, u32[]{:S(2)}) collective-permute-start(bf16[96,30]{1,0:T(8,128)(2,1)S(1)} %get-tuple-element.125), channel_id=1, source_target_pairs={{1,0},{2,1},{3,2},{4,3},{5,4},{6,5},{7,6},{8,7},{9,8},{10,9},{11,1... | collective-permute-start | bytes 17288 | tf_op jit(solution)/shard_map/ppermute | solution.py:175
  117.6 15.1 %all-to-all-start.2 = ((f32[32,2,96]{2,1,0:T(2,128)}), f32[32,2,96]{2,1,0:T(2,128)S(1)}, u32[]{:S(2)}, u32[]{:S(2)}) async-start(f32[32,2,96]{2,1,0:T(2,128)} %broadcast_in_dim.19), calls=%async_computation.2 | async-start | bytes 65536 | tf_op jit(solution)/shard_map/all_to_all | solution.py:28
  135.8 13.9 %all-to-all-start.3 = ((f32[32,2,96]{2,1,0:T(2,128)}), f32[32,2,96]{2,1,0:T(2,128)S(1)}, u32[]{:S(2)}, u32[]{:S(2)}) async-start(f32[32,2,96]{2,1,0:T(2,128)} %broadcast_in_dim.20), calls=%async_computation.3 | async-start | bytes 65536 | tf_op jit(solution)/shard_map/all_to_all | solution.py:28
  157.5 11.2 %collective-permute-start.10 = (bf16[288,448]{1,0:T(8,128)(2,1)}, bf16[288,448]{1,0:T(8,128)(2,1)S(1)}, u32[]{:S(2)}, u32[]{:S(2)}) collective-permute-start(bf16[288,448]{1,0:T(8,128)(2,1)} %pad_maximum_fusion.5), channel_id=1, source_target_pairs={{0,256},{32,288},{64,320},{96,352},{128,384},{160,416},{192,448},{... | collective-permute-start | bytes 774152 | tf_op jit(solution)/shard_map/ppermute | solution.py:44
  174.2 7.9 %collective-permute-start.11 = (bf16[144,1536]{1,0:T(8,128)(2,1)}, bf16[144,1536]{1,0:T(8,128)(2,1)}, u32[]{:S(2)}, u32[]{:S(2)}) collective-permute-start(bf16[144,1536]{1,0:T(8,128)(2,1)} %dynamic-slice_convert_fusion), channel_id=1, source_target_pairs={{0,1},{1,0},{2,3},{3,2},{4,5},{5,4},{6,7},{7,6},{8,9},{9,8},{10,11... | collective-permute-start | bytes 1327112 | tf_op jit(solution)/shard_map/ppermute | solution.py:49
  178.0 27.6 %all-to-all-start.4 = ((bf16[8,96,512]{2,1,0:T(8,128)(2,1)}), bf16[8,96,512]{2,1,0:T(8,128)(2,1)S(1)}, u32[]{:S(2)}, u32[]{:S(2)}) async-start(bf16[8,96,512]{2,1,0:T(8,128)(2,1)} %line_product.1), calls=%async_computation.4 | async-start | bytes 1572864 | tf_op jit(solution)/shard_map/all_to_all | solution.py:212
  181.9 59.4 %all-gather.7.cloned.1.call-start = ((), (), s32[]{:S(2)}) async-start(), calls=%async_computation.11 | async-start | bytes 1990656 | tf_op jit(solution)/shard_map/all_gather | solution.py:392
  185.2 8.8 %collective-permute-start.12 = (bf16[72,1536]{1,0:T(8,128)(2,1)}, bf16[72,1536]{1,0:T(8,128)(2,1)S(1)}, u32[]{:S(2)}, u32[]{:S(2)}) collective-permute-start(bf16[72,1536]{1,0:T(8,128)(2,1)} %dynamic-slice_convert_fusion.1), channel_id=1, source_target_pairs={{0,16},{1,17},{2,18},{3,19},{4,20},{5,21},{6,22},{7,23},{8,24},{9,... | collective-permute-start | bytes 663560 | tf_op jit(solution)/shard_map/ppermute | solution.py:49
  206.7 27.1 %all-to-all-start.5 = ((bf16[8,96,448]{2,1,0:T(8,128)(2,1)}), bf16[8,96,448]{2,1,0:T(8,128)(2,1)S(1)}, u32[]{:S(2)}, u32[]{:S(2)}) async-start(bf16[8,96,448]{2,1,0:T(8,128)(2,1)} %broadcast_in_dim.21), calls=%async_computation.5 | async-start | bytes 1572864 | tf_op jit(solution)/shard_map/all_to_all | solution.py:223
  220.0 6.6 %collective-permute-start.13 = (f32[2,448]{1,0:T(2,128)S(1)}, f32[2,448]{1,0:T(2,128)S(1)}, u32[]{:S(2)}, u32[]{:S(2)}) collective-permute-start(f32[2,448]{1,0:T(2,128)S(1)} %reshape.265), channel_id=1, source_target_pairs={{0,256},{32,288},{64,320},{96,352},{128,384},{160,416},{192,448},{... | collective-permute-start | bytes 10760 | tf_op jit(solution)/shard_map/ppermute | solution.py:44
  236.5 19.5 %all-to-all-start.6 = ((bf16[32,6,896]{2,1,0:T(8,128)(2,1)}), bf16[32,6,896]{2,1,0:T(8,128)(2,1)S(1)}, u32[]{:S(2)}, u32[]{:S(2)}) async-start(bf16[32,6,896]{2,1,0:T(8,128)(2,1)} %fusion.18), calls=%async_computation.7 | async-start | bytes 917504 | tf_op jit(solution)/shard_map/all_to_all | solution.py:28
  240.6 50.4 %reduce-scatter.2.cloned.1.call-start = ((), (), s32[]{:S(2)}) async-start(), calls=%async_computation.9 | async-start | bytes 2654208 | tf_op jit(solution)/shard_map/reduce_scatter | solution.py:403
  243.1 13.1 %collective-permute-start.14 = (bf16[72,768]{1,0:T(8,128)(2,1)S(1)}, bf16[72,768]{1,0:T(8,128)(2,1)S(1)}, u32[]{:S(2)}, u32[]{:S(2)}) collective-permute-start(bf16[72,768]{1,0:T(8,128)(2,1)S(1)} %slice.504), channel_id=1, source_target_pairs={{0,256},{32,288},{64,320},{96,352},{128,384},{160,416},{192,448},{... | collective-permute-start | bytes 331784 | tf_op jit(solution)/shard_map/ppermute | solution.py:44
  256.3 7.1 %collective-permute-start.16 = (bf16[72,1536]{1,0:T(8,128)(2,1)S(1)}, bf16[72,1536]{1,0:T(8,128)(2,1)S(1)}, u32[]{:S(2)}, u32[]{:S(2)}) collective-permute-start(bf16[72,1536]{1,0:T(8,128)(2,1)S(1)} %maximum_select_fusion), channel_id=1, source_target_pairs={{0,16},{1,17},{2,18},{3,19},{4,20},{5,21},{6,22},{7,23},{8,24},{9,... | collective-permute-start | bytes 663560 | tf_op jit(solution)/shard_map/ppermute | solution.py:49
  258.6 4.9 %collective-permute-start.15 = (bf16[6,896]{1,0:T(8,128)(2,1)S(1)}, bf16[6,896]{1,0:T(8,128)(2,1)S(1)}, u32[]{:S(2)}, u32[]{:S(2)}) collective-permute-start(bf16[6,896]{1,0:T(8,128)(2,1)S(1)} %reduce_sum.174), channel_id=1, source_target_pairs={{16,256},{17,257},{18,258},{19,259},{20,260},{21,261},{22,262},{23... | collective-permute-start | bytes 32264 | tf_op jit(solution)/shard_map/ppermute | solution.py:446
  263.5 10.2 %collective-permute-start.17 = (bf16[144,1536]{1,0:T(8,128)(2,1)S(1)}, bf16[144,1536]{1,0:T(8,128)(2,1)S(1)}, u32[]{:S(2)}, u32[]{:S(2)}) collective-permute-start(bf16[144,1536]{1,0:T(8,128)(2,1)S(1)} %pad_maximum_fusion.2), channel_id=1, source_target_pairs={{0,1},{1,0},{2,3},{3,2},{4,5},{5,4},{6,7},{7,6},{8,9},{9,8},{10,11... | collective-permute-start | bytes 1327112 | tf_op jit(solution)/shard_map/ppermute | solution.py:49
  269.4 19.7 %all-to-all-start.7 = ((bf16[32,6,896]{2,1,0:T(8,128)(2,1)}), bf16[32,6,896]{2,1,0:T(8,128)(2,1)S(1)}, u32[]{:S(2)}, u32[]{:S(2)}) async-start(bf16[32,6,896]{2,1,0:T(8,128)(2,1)} %broadcast_in_dim.23), calls=%async_computation.8 | async-start | bytes 917504 | tf_op jit(solution)/shard_map/all_to_all | solution.py:28
  273.9 9.0 %collective-permute-start.18 = (bf16[96,448]{1,0:T(8,128)(2,1)S(1)}, bf16[96,448]{1,0:T(8,128)(2,1)S(1)}, u32[]{:S(2)}, u32[]{:S(2)}) collective-permute-start(bf16[96,448]{1,0:T(8,128)(2,1)S(1)} %slice.757), channel_id=1, source_target_pairs={{0,256},{32,288},{64,320},{96,352},{128,384},{160,416},{192,448},{... | collective-permute-start | bytes 258056 | tf_op jit(solution)/shard_map/ppermute | solution.py:44
  (72 other events, 702.4 us)
Sparse Core Ops, SparseCore 0:
  92.5 33.8 all-gather.4
  205.8 30.0 all-gather.6
  244.3 42.0 reduce-scatter.1
